TPU v7x, 32 devices: a whole 2x2x4 slice. The times are simulated.
32 devices in a mesh: batch: 2 (over x), blk: 16 (over z, y, core).
Axes of the slice: x: 2, y: 2, z: 4, core: 2. Of those that a mesh axis runs over, the one named last changes fastest.
Arguments:
- layer_input: bfloat16 [2, 4, 1024, 768], P('batch', None, 'blk'), may hold values from -6 to 6
- cotangent: bfloat16 [2, 4, 1024, 768], P('batch', None, 'blk'), may hold values from -6 to 6
- doc_lengths: int32 [2, 4, 8], P('batch'), may hold values from 0 to 1024, as said below
- joined_weight: bfloat16 [768, 2304], replicated, may hold values from -0.21875 to 0.21875
- merge_weight: bfloat16 [768, 768], replicated, may hold values from -0.21875 to 0.21875
- expand_weight: bfloat16 [768, 3072], replicated, may hold values from -0.21875 to 0.21875
- shrink_weight: bfloat16 [3072, 768], replicated, may hold values from -0.109375 to 0.109375
- first_gain: float32 [768], replicated, may hold values from 0.1 to 1.9
- mixed_gain: float32 [768], replicated, may hold values from 0.1 to 1.9
- second_gain: float32 [768], replicated, may hold values from 0.1 to 1.9
- hidden_gain: float32 [3072], replicated, may hold values from 0.1 to 1.9
Outputs:
- layer_result: bfloat16 [2, 4, 1024, 768], P('batch', None, 'blk')
- input_grad: bfloat16 [2, 4, 1024, 768], P('batch', None, 'blk')
- joined_grad: float32 [768, 2304], P('blk')
- merge_grad: float32 [768, 768], P('blk')
- expand_grad: float32 [768, 3072], P('blk')
- shrink_grad: float32 [3072, 768], P('blk')
- first_grad: float32 [768], replicated
- mixed_grad: float32 [768], replicated
- second_grad: float32 [768], replicated
- hidden_grad: float32 [3072], replicated
Inputs may be any that keep to these rules, and one draw needn't show every extreme that they name: `doc_lengths`: each stream's lengths sum to at most 1024; tokens after that sum are padding. In every group one stream holds a single document of 1024 tokens.
All inputs are finite; a program needn't handle non-finite values.
Results may differ from a plain program's by a relative error of at most 0.02.
Values may be sent and summed in bfloat16 or wider, within the bound.
No kernel may reach another device: no remote copies, remote signals or barrier semaphores. Data moves between devices by JAX's collectives and lax.ppermute only.
A program may use at most 192 MiB of HBM per device.

v0:
```python
import jax
import jax.numpy as jnp
from jax import lax
from jax.sharding import PartitionSpec as P

HEAD = 64


big_negative = -1e30
norm_epsilon = 1e-05


def from_behind(shard, axis, by):
    size = lax.axis_size(axis)
    pairs = [(i, i + by) for i in range(size) if 0 <= i + by < size]
    return lax.ppermute(shard, axis, pairs)


def passed_along(shard, axis, by):
    size = lax.axis_size(axis)
    return lax.ppermute(shard, axis, [(i, (i + by) % size) for i in range(size)])


def layer_norm(values, gain):
    centred = values - jnp.mean(values, axis=-1, keepdims=True)
    spread = jnp.mean(centred * centred, axis=-1, keepdims=True)
    return centred * lax.rsqrt(spread + norm_epsilon) * gain


def hidden_norm(widened_hidden, gain):
    return layer_norm(jax.nn.gelu(widened_hidden, approximate=False), gain)


def document_ids(doc_ends, positions):
    return jnp.sum((doc_ends[:, None, :] <= positions[None, :, None]).astype(jnp.int32), axis=-1)


def over_rows(left, right):
    return lax.dot_general(
        left, right, (((0,), (0,)), ((), ())), preferred_element_type=jnp.float32
    )


def over_columns(left, right):
    return lax.dot_general(
        left, right, (((1,), (1,)), ((), ())), preferred_element_type=jnp.float32
    )


def per_device(
    layer_input,
    cotangent,
    doc_lengths,
    joined_weight,
    merge_weight,
    expand_weight,
    shrink_weight,
    first_gain,
    mixed_gain,
    second_gain,
    hidden_gain,
):
    streams = layer_input.shape[1]
    seg_rows = layer_input.shape[2]
    model_width = layer_input.shape[3]
    head_count = model_width // HEAD
    token_rows = streams * seg_rows
    cycle_size = lax.axis_size("blk")
    device_rank = lax.axis_index("blk")
    doc_ends = jnp.cumsum(doc_lengths[0], axis=-1)
    query_pos = device_rank * seg_rows + jnp.arange(seg_rows, dtype=jnp.int32)
    query_doc = document_ids(doc_ends, query_pos)
    valid_rows = (query_doc < doc_lengths.shape[2]).astype(jnp.float32).reshape(token_rows, 1)
    inputs = layer_input.reshape(token_rows, model_width).astype(jnp.float32)
    leading_norm, first_back = jax.vjp(layer_norm, inputs, first_gain)
    first_low = leading_norm.astype(jnp.bfloat16)
    combined_output = jnp.dot(first_low, joined_weight, preferred_element_type=jnp.float32).astype(
        jnp.bfloat16
    )
    queries = (combined_output[:, :model_width] * 0.125).reshape(
        streams, seg_rows, head_count, HEAD
    )
    keys_local = combined_output[:, model_width : 2 * model_width].reshape(
        streams, seg_rows, model_width
    )
    values_local = combined_output[:, 2 * model_width :].reshape(streams, seg_rows, model_width)

    def block_scores(key_block, key_start):
        key_count = key_block.shape[1]
        key_pos = key_start + jnp.arange(key_count, dtype=jnp.int32)
        key_doc = document_ids(doc_ends, key_pos)
        allowed = (query_doc[:, :, None] == key_doc[:, None, :]) & (
            key_pos[None, None, :] <= query_pos[None, :, None]
        )
        key_heads = key_block.reshape(streams, key_count, head_count, HEAD)
        scores = jnp.einsum(
            "sqhd,skhd->shqk", queries, key_heads, preferred_element_type=jnp.float32
        )
        allowed = allowed[:, None]
        return (jnp.where(allowed, scores, big_negative), allowed)

    def absorb(running, key_block, value_block, key_start):
        running_peak, running_total, mixed_sum = running
        scores, allowed = block_scores(key_block, key_start)
        new_peak = jnp.maximum(running_peak, jnp.max(scores, axis=-1))
        shares = jnp.where(allowed, jnp.exp(scores - new_peak[..., None]), 0.0)
        factor = jnp.exp(running_peak - new_peak)
        value_heads = value_block.reshape(streams, value_block.shape[1], head_count, HEAD)
        update = jnp.einsum(
            "shqk,skhd->shqd",
            shares.astype(jnp.bfloat16),
            value_heads,
            preferred_element_type=jnp.float32,
        )
        return (
            new_peak,
            running_total * factor + jnp.sum(shares, axis=-1),
            mixed_sum * factor[..., None] + update,
        )

    start_state = (
        jnp.full((streams, head_count, seg_rows), big_negative, jnp.float32),
        jnp.zeros((streams, head_count, seg_rows), jnp.float32),
        jnp.zeros((streams, head_count, seg_rows, HEAD), jnp.float32),
    )
    key_piece = lax.all_gather(keys_local, "blk", axis=1, tiled=True)
    value_piece = lax.all_gather(values_local, "blk", axis=1, tiled=True)
    block_rows = min(key_piece.shape[1], seg_rows)
    blocks = key_piece.shape[1] // block_rows

    def one_block(block_index, inner_state):
        offset = block_index * block_rows
        key_block = lax.dynamic_slice_in_dim(key_piece, offset, block_rows, 1)
        value_block = lax.dynamic_slice_in_dim(value_piece, offset, block_rows, 1)
        return absorb(inner_state, key_block, value_block, offset)

    running_peak, running_total, mixed_sum = lax.fori_loop(0, blocks, one_block, start_state)
    log_total = running_peak + jnp.log(running_total)
    attention_heads = mixed_sum / running_total[..., None]
    attention = attention_heads.transpose(0, 2, 1, 3).reshape(token_rows, model_width)
    attention_mixed_norm, mixed_back = jax.vjp(layer_norm, attention, mixed_gain)
    mixed_low = attention_mixed_norm.astype(jnp.bfloat16)
    intermediate = inputs + jnp.dot(mixed_low, merge_weight, preferred_element_type=jnp.float32)
    trailing_branch, second_back = jax.vjp(layer_norm, intermediate, second_gain)
    second_low = trailing_branch.astype(jnp.bfloat16)
    widened_hidden = jnp.dot(second_low, expand_weight, preferred_element_type=jnp.float32)
    hidden_state, hidden_back = jax.vjp(hidden_norm, widened_hidden, hidden_gain)
    hidden_low = hidden_state.astype(jnp.bfloat16)
    result = intermediate + jnp.dot(hidden_low, shrink_weight, preferred_element_type=jnp.float32)
    layer_result = result.astype(jnp.bfloat16).reshape(layer_input.shape)
    grad_out = cotangent.reshape(token_rows, model_width).astype(jnp.float32) * valid_rows
    grad_branch = grad_out.astype(jnp.bfloat16)
    shrink_part = over_rows(hidden_low, grad_branch)
    grad_hidden = over_columns(grad_branch, shrink_weight)
    grad_expanded, hidden_part = hidden_back(grad_hidden)
    expanded_low = grad_expanded.astype(jnp.bfloat16)
    expand_part = over_rows(second_low, expanded_low)
    grad_second = over_columns(expanded_low, expand_weight)
    middle_extra, second_part = second_back(grad_second)
    grad_middle = grad_out + middle_extra
    grad_mix = grad_middle.astype(jnp.bfloat16)
    merge_part = over_rows(mixed_low, grad_mix)
    grad_mixed = over_columns(grad_mix, merge_weight)
    grad_attention, mixed_part = mixed_back(grad_mixed)
    grad_heads = grad_attention.astype(jnp.bfloat16).reshape(streams, seg_rows, head_count, HEAD)
    row_inner = jnp.einsum("sqhd,shqd->shq", grad_heads.astype(jnp.float32), attention_heads)

    def release(key_block, value_block, key_start):
        scores, allowed = block_scores(key_block, key_start)
        shares = jnp.where(allowed, jnp.exp(scores - log_total[..., None]), 0.0)
        key_heads = key_block.reshape(streams, seg_rows, head_count, HEAD)
        value_heads = value_block.reshape(streams, seg_rows, head_count, HEAD)
        value_add = jnp.einsum(
            "shqk,sqhd->skhd",
            shares.astype(jnp.bfloat16),
            grad_heads,
            preferred_element_type=jnp.float32,
        )
        grad_shares = jnp.einsum(
            "sqhd,skhd->shqk", grad_heads, value_heads, preferred_element_type=jnp.float32
        )
        grad_scores = (shares * (grad_shares - row_inner[..., None])).astype(jnp.bfloat16)
        query_add = (
            jnp.einsum(
                "shqk,skhd->sqhd", grad_scores, key_heads, preferred_element_type=jnp.float32
            )
            * 0.125
        )
        key_add = jnp.einsum(
            "shqk,sqhd->skhd", grad_scores, queries, preferred_element_type=jnp.float32
        )
        return (
            query_add,
            key_add.reshape(streams, seg_rows, model_width),
            value_add.reshape(streams, seg_rows, model_width),
        )

    zero_adds = (
        jnp.zeros((streams, seg_rows, head_count, HEAD), jnp.float32),
        jnp.zeros((streams, seg_rows, model_width), jnp.float32),
        jnp.zeros((streams, seg_rows, model_width), jnp.float32),
    )

    def cycle_step(turn_index, carried):
        moving_blocks, moving_grads, query_grad = carried
        key_now, value_now = moving_blocks
        owner_rank = (device_rank - turn_index) % cycle_size
        key_start = owner_rank * seg_rows
        query_add, key_add, value_add = release(key_now, value_now, key_start)
        key_grad = moving_grads[0] + key_add
        value_grad = moving_grads[1] + value_add
        moved_blocks = from_behind((key_now, value_now), "blk", 1)
        moved_grads = (
            passed_along(key_grad.astype(jnp.bfloat16), "blk", 1).astype(key_grad.dtype),
            passed_along(value_grad.astype(jnp.bfloat16), "blk", 1).astype(value_grad.dtype),
        )
        return (moved_blocks, moved_grads, query_grad + query_add)

    cycle_start = ((keys_local, values_local), (zero_adds[1], zero_adds[2]), zero_adds[0])
    cycle_end = lax.fori_loop(0, cycle_size, cycle_step, cycle_start)
    key_grad, value_grad = cycle_end[1]
    query_grad = cycle_end[2]
    grad_joined = jnp.concatenate(
        [
            query_grad.reshape(token_rows, model_width),
            key_grad.reshape(token_rows, model_width),
            value_grad.reshape(token_rows, model_width),
        ],
        axis=1,
    ).astype(jnp.bfloat16)
    joined_part = over_rows(first_low, grad_joined)
    grad_first = over_columns(grad_joined, joined_weight)
    input_extra, first_part = first_back(grad_first)
    input_grad = (grad_middle + input_extra).astype(jnp.bfloat16).reshape(layer_input.shape)
    row_parts = (
        lax.psum_scatter(
            joined_part.astype(jnp.bfloat16), "blk", scatter_dimension=0, tiled=True
        ).astype(jnp.float32),
        lax.psum_scatter(
            merge_part.astype(jnp.bfloat16), "blk", scatter_dimension=0, tiled=True
        ).astype(jnp.float32),
        lax.psum_scatter(
            expand_part.astype(jnp.bfloat16), "blk", scatter_dimension=0, tiled=True
        ).astype(jnp.float32),
        lax.psum_scatter(
            shrink_part.astype(jnp.bfloat16), "blk", scatter_dimension=0, tiled=True
        ).astype(jnp.float32),
    )
    summed = (
        lax.psum(row_parts[0].astype(jnp.bfloat16), "batch").astype(jnp.float32),
        lax.psum(row_parts[1].astype(jnp.bfloat16), "batch").astype(jnp.float32),
        lax.psum(row_parts[2].astype(jnp.bfloat16), "batch").astype(jnp.float32),
        lax.psum(row_parts[3].astype(jnp.bfloat16), "batch").astype(jnp.float32),
    )
    gain_totals = lax.psum((first_part, mixed_part, second_part, hidden_part), ("batch", "blk"))
    return (
        layer_result,
        input_grad,
        summed[0],
        summed[1],
        summed[2],
        summed[3],
        gain_totals[0],
        gain_totals[1],
        gain_totals[2],
        gain_totals[3],
    )


def solution(mesh):
    placed = (
        P("batch", None, "blk", None),
        P("batch", None, "blk", None),
        P("batch", None, None),
        P(),
        P(),
        P(),
        P(),
        P(),
        P(),
        P(),
        P(),
    )
    return jax.shard_map(
        per_device,
        mesh=mesh,
        in_specs=placed,
        out_specs=(
            P("batch", None, "blk", None),
            P("batch", None, "blk", None),
            P("blk", None),
            P("blk", None),
            P("blk", None),
            P("blk", None),
            P(),
            P(),
            P(),
            P(),
        ),
        check_vma=False,
    )
```

profile of v0, /device:TPU:0, one launch (start us, length us, event | category | flops | bytes accessed | tf_op | source)
XLA Modules:
  0.0 1582.5 jit_solution(1460200102613399631)
XLA Ops:
  21.9 56.9 %all-gather.3.cloned.1.call-done = bf16[4,1024,768]{2,1,0:T(8,128)(2,1)} async-done(((bf16[4,64,768]{2,1,0:T(8,128)(2,1)}), bf16[4,1024,768]{2,1,0:T(8,128)(2,1)}) %all-gather.3.cloned.1.call-update) | async-done | bytes 6291472 | tf_op jit(solution)/shard_map/all_gather | solution.py:126
  78.8 62.8 %all-gather.5.cloned.1.call-done = bf16[4,1024,768]{2,1,0:T(8,128)(2,1)} async-done(((bf16[4,64,768]{2,1,0:T(8,128)(2,1)}), bf16[4,1024,768]{2,1,0:T(8,128)(2,1)}) %all-gather.5.cloned.1.call-update) | async-done | bytes 6291472 | tf_op jit(solution)/shard_map/all_gather | solution.py:127
  141.6 327.0 %while.42 = (s32[]{:T(128)}, f32[4,12,64]{2,1,0:T(8,128)}, f32[4,12,64]{2,1,0:T(8,128)}, f32[4,12,64,64]{3,2,1,0:T(8,128)}, s32[4,64]{1,0:T(4,128)S(1)}, /*index...) while((s32[]{:T(128)}, f32[4,12,64]{2,1,0:T(8,128)}, ...), condition=%wide.region_8.9_spmd.clone, body=%wide.region_4.8_spmd.clone.sunk | while | flops 52552580 | bytes 8630915 | solution.py:137
  483.0 10.1 fusion.42
  524.5 760.5 %while.43 = (s32[]{:T(128)}, bf16[4,64,768]{2,1,0:T(8,128)(2,1)}, bf16[4,64,768]{2,1,0:T(8,128)(2,1)}, f32[4,64,768]{2,1,0:T(8,128)}, f32[4,64,768]{2,1,0:T(8,12...) while((s32[]{:T(128)}, bf16[4,64,768]{2,1,0:T(8,128)(2,1)}, ...), condition=%wide.region_23.24_spmd.clone, body=%wide.region_21.23_spmd.clone.sunk | while | flops 129410960 | bytes 41014280 | solution.py:220
  602.4 6.0 collective-permute-start
  608.4 5.3 collective-permute-start.1
  703.4 5.2 collective-permute-start.1
  750.8 5.2 collective-permute-start.1
  845.6 5.2 collective-permute-start.1
  893.0 5.2 collective-permute-start.1
  987.8 5.2 collective-permute-start.1
  1035.2 5.2 collective-permute-start.1
  1130.1 5.2 collective-permute-start.1
  1177.5 5.2 collective-permute-start.1
  1224.9 5.2 collective-permute-start.1
  1304.8 5.7 convolution_convert_fusion
  1311.3 5.5 convolution_convert_fusion.1
  1321.3 42.3 %all-reduce = (f32[768]{0:T(1024)}, f32[768]{0:T(1024)}, f32[768]{0:T(1024)}, f32[3072]{0:T(1024)}) all-reduce(f32[768]{0:T(1024)} %get-tuple-element.708, f32[768]{0:T(1024)} %get-tuple-element.706, f32[768]{0:T(1024)} %get-tuple-element.704, f32[3072]{0:T(1024)} %get-tuple-element.700), channel_id=1, replica_groups=mesh['batch'=2,'blk'=16] {'batch','blk'}, use_global_device_ids=true, to_apply=%region_35.36 | all-reduce | flops 5376 | bytes 43008 | tf_op jit(solution)/shard_map/psum | solution.py:255
  1364.9 7.8 reduce-scatter.5.cloned.1.call-done
  1372.6 78.2 %reduce-scatter.11.cloned.1.call-done = bf16[192,768]{1,0:T(8,128)(2,1)} async-done(((bf16[3072,768]{1,0:T(8,128)(2,1)}), bf16[192,768]{1,0:T(8,128)(2,1)}) %reduce-scatter.11.cloned.1.call-update) | async-done | bytes 294928 | tf_op jit(solution)/shard_map/reduce_scatter | solution.py:245
  1450.9 78.8 %reduce-scatter.9.cloned.1.call-done = bf16[48,3072]{1,0:T(8,128)(2,1)} async-done(((bf16[768,3072]{1,0:T(8,128)(2,1)}), bf16[48,3072]{1,0:T(8,128)(2,1)}) %reduce-scatter.9.cloned.1.call-update) | async-done | bytes 294928 | tf_op jit(solution)/shard_map/reduce_scatter | solution.py:242
  1532.5 5.6 fusion.28
  1538.1 30.2 %all-reduce.4.cloned.1.call-done = (bf16[48,2304]{1,0:T(8,128)(2,1)}, bf16[48,768]{1,0:T(8,128)(2,1)}, bf16[48,3072]{1,0:T(8,128)(2,1)}, bf16[192,768]{1,0:T(8,128)(2,1)}) async-done(((bf16[48,2304]{1,0:T(8,128)(2,1)}, bf16[48,768]{1,0:T(8,128)(2,1)}, bf16[48,3072]{1,0:T(8,128)(2,1)}, bf16[192,768]{1,0:T(8,128)(2,1)}), (bf16[48,2304]{1,0:T(8,128)(2,1)}, bf16[48,768]{1,0:T(8,128)(2,1)}, ...) | async-done | bytes 884752 | tf_op jit(solution)/shard_map/psum | solution.py:250
  (1126 shorter events, 1123.2 us)
Async XLA Ops:
  7.2 71.6 %all-gather.3.cloned.1.call-start = ((), (), s32[]{:S(2)}) async-start(), calls=%async_computation.4 | async-start | bytes 6684672 | tf_op jit(solution)/shard_map/all_gather | solution.py:126
  14.0 127.7 %all-gather.5.cloned.1.call-start = ((), (), s32[]{:S(2)}) async-start(), calls=%async_computation.5 | async-start | bytes 6684672 | tf_op jit(solution)/shard_map/all_gather | solution.py:127
  14.7 1350.1 %reduce-scatter.7.cloned.1.call-start = ((), (), s32[]{:S(2)}) async-start(), calls=%async_computation.7 | async-start | bytes 1253376 | tf_op jit(solution)/shard_map/reduce_scatter | solution.py:239
  524.5 848.2 %reduce-scatter.5.cloned.1.call-start = ((), (), s32[]{:S(2)}) async-start(), calls=%async_computation.6 | async-start | bytes 3760128 | tf_op jit(solution)/shard_map/reduce_scatter | solution.py:236
  545.9 19.8 %collective-permute-start.2 = (bf16[4,64,768]{2,1,0:T(8,128)(2,1)}, bf16[4,64,768]{2,1,0:T(8,128)(2,1)}, u32[]{:S(2)}, u32[]{:S(2)}) collective-permute-start(bf16[4,64,768]{2,1,0:T(8,128)(2,1)} %fusion.108), channel_id=1, source_target_pairs={{0,1},{1,2},{2,3},{3,4},{4,5},{5,6},{6,7},{7,8},{8,9},{9,10},{10,1... | collective-permute-start | bytes 1179656 | tf_op jit(solution)/shard_map/while/body/eval_jaxpr/ppermute | solution.py:21
  591.0 26.2 %collective-permute-start.2 = (bf16[4,64,768]{2,1,0:T(8,128)(2,1)}, bf16[4,64,768]{2,1,0:T(8,128)(2,1)}, u32[]{:S(2)}, u32[]{:S(2)}) collective-permute-start(bf16[4,64,768]{2,1,0:T(8,128)(2,1)} %fusion.108), channel_id=1, source_target_pairs={{0,1},{1,2},{2,3},{3,4},{4,5},{5,6},{6,7},{7,8},{8,9},{9,10},{10,1... | collective-permute-start | bytes 1179656 | tf_op jit(solution)/shard_map/while/body/eval_jaxpr/ppermute | solution.py:21
  600.3 19.0 %collective-permute-start.3 = (bf16[4,64,768]{2,1,0:T(8,128)(2,1)}, bf16[4,64,768]{2,1,0:T(8,128)(2,1)}, u32[]{:S(2)}, u32[]{:S(2)}) collective-permute-start(bf16[4,64,768]{2,1,0:T(8,128)(2,1)} %fusion.109), channel_id=1, source_target_pairs={{0,1},{1,2},{2,3},{3,4},{4,5},{5,6},{6,7},{7,8},{8,9},{9,10},{10,1... | collective-permute-start | bytes 1179656 | tf_op jit(solution)/shard_map/while/body/eval_jaxpr/ppermute | solution.py:21
  642.6 22.1 %collective-permute-start.2 = (bf16[4,64,768]{2,1,0:T(8,128)(2,1)}, bf16[4,64,768]{2,1,0:T(8,128)(2,1)}, u32[]{:S(2)}, u32[]{:S(2)}) collective-permute-start(bf16[4,64,768]{2,1,0:T(8,128)(2,1)} %fusion.108), channel_id=1, source_target_pairs={{0,1},{1,2},{2,3},{3,4},{4,5},{5,6},{6,7},{7,8},{8,9},{9,10},{10,1... | collective-permute-start | bytes 1179656 | tf_op jit(solution)/shard_map/while/body/eval_jaxpr/ppermute | solution.py:21
  690.0 22.1 %collective-permute-start.2 = (bf16[4,64,768]{2,1,0:T(8,128)(2,1)}, bf16[4,64,768]{2,1,0:T(8,128)(2,1)}, u32[]{:S(2)}, u32[]{:S(2)}) collective-permute-start(bf16[4,64,768]{2,1,0:T(8,128)(2,1)} %fusion.108), channel_id=1, source_target_pairs={{0,1},{1,2},{2,3},{3,4},{4,5},{5,6},{6,7},{7,8},{8,9},{9,10},{10,1... | collective-permute-start | bytes 1179656 | tf_op jit(solution)/shard_map/while/body/eval_jaxpr/ppermute | solution.py:21
  737.4 22.1 %collective-permute-start.2 = (bf16[4,64,768]{2,1,0:T(8,128)(2,1)}, bf16[4,64,768]{2,1,0:T(8,128)(2,1)}, u32[]{:S(2)}, u32[]{:S(2)}) collective-permute-start(bf16[4,64,768]{2,1,0:T(8,128)(2,1)} %fusion.108), channel_id=1, source_target_pairs={{0,1},{1,2},{2,3},{3,4},{4,5},{5,6},{6,7},{7,8},{8,9},{9,10},{10,1... | collective-permute-start | bytes 1179656 | tf_op jit(solution)/shard_map/while/body/eval_jaxpr/ppermute | solution.py:21
  784.8 22.1 %collective-permute-start.2 = (bf16[4,64,768]{2,1,0:T(8,128)(2,1)}, bf16[4,64,768]{2,1,0:T(8,128)(2,1)}, u32[]{:S(2)}, u32[]{:S(2)}) collective-permute-start(bf16[4,64,768]{2,1,0:T(8,128)(2,1)} %fusion.108), channel_id=1, source_target_pairs={{0,1},{1,2},{2,3},{3,4},{4,5},{5,6},{6,7},{7,8},{8,9},{9,10},{10,1... | collective-permute-start | bytes 1179656 | tf_op jit(solution)/shard_map/while/body/eval_jaxpr/ppermute | solution.py:21
  832.2 22.1 %collective-permute-start.2 = (bf16[4,64,768]{2,1,0:T(8,128)(2,1)}, bf16[4,64,768]{2,1,0:T(8,128)(2,1)}, u32[]{:S(2)}, u32[]{:S(2)}) collective-permute-start(bf16[4,64,768]{2,1,0:T(8,128)(2,1)} %fusion.108), channel_id=1, source_target_pairs={{0,1},{1,2},{2,3},{3,4},{4,5},{5,6},{6,7},{7,8},{8,9},{9,10},{10,1... | collective-permute-start | bytes 1179656 | tf_op jit(solution)/shard_map/while/body/eval_jaxpr/ppermute | solution.py:21
  879.7 22.1 %collective-permute-start.2 = (bf16[4,64,768]{2,1,0:T(8,128)(2,1)}, bf16[4,64,768]{2,1,0:T(8,128)(2,1)}, u32[]{:S(2)}, u32[]{:S(2)}) collective-permute-start(bf16[4,64,768]{2,1,0:T(8,128)(2,1)} %fusion.108), channel_id=1, source_target_pairs={{0,1},{1,2},{2,3},{3,4},{4,5},{5,6},{6,7},{7,8},{8,9},{9,10},{10,1... | collective-permute-start | bytes 1179656 | tf_op jit(solution)/shard_map/while/body/eval_jaxpr/ppermute | solution.py:21
  927.1 22.1 %collective-permute-start.2 = (bf16[4,64,768]{2,1,0:T(8,128)(2,1)}, bf16[4,64,768]{2,1,0:T(8,128)(2,1)}, u32[]{:S(2)}, u32[]{:S(2)}) collective-permute-start(bf16[4,64,768]{2,1,0:T(8,128)(2,1)} %fusion.108), channel_id=1, source_target_pairs={{0,1},{1,2},{2,3},{3,4},{4,5},{5,6},{6,7},{7,8},{8,9},{9,10},{10,1... | collective-permute-start | bytes 1179656 | tf_op jit(solution)/shard_map/while/body/eval_jaxpr/ppermute | solution.py:21
  974.5 22.1 %collective-permute-start.2 = (bf16[4,64,768]{2,1,0:T(8,128)(2,1)}, bf16[4,64,768]{2,1,0:T(8,128)(2,1)}, u32[]{:S(2)}, u32[]{:S(2)}) collective-permute-start(bf16[4,64,768]{2,1,0:T(8,128)(2,1)} %fusion.108), channel_id=1, source_target_pairs={{0,1},{1,2},{2,3},{3,4},{4,5},{5,6},{6,7},{7,8},{8,9},{9,10},{10,1... | collective-permute-start | bytes 1179656 | tf_op jit(solution)/shard_map/while/body/eval_jaxpr/ppermute | solution.py:21
  1021.9 22.1 %collective-permute-start.2 = (bf16[4,64,768]{2,1,0:T(8,128)(2,1)}, bf16[4,64,768]{2,1,0:T(8,128)(2,1)}, u32[]{:S(2)}, u32[]{:S(2)}) collective-permute-start(bf16[4,64,768]{2,1,0:T(8,128)(2,1)} %fusion.108), channel_id=1, source_target_pairs={{0,1},{1,2},{2,3},{3,4},{4,5},{5,6},{6,7},{7,8},{8,9},{9,10},{10,1... | collective-permute-start | bytes 1179656 | tf_op jit(solution)/shard_map/while/body/eval_jaxpr/ppermute | solution.py:21
  1069.3 22.1 %collective-permute-start.2 = (bf16[4,64,768]{2,1,0:T(8,128)(2,1)}, bf16[4,64,768]{2,1,0:T(8,128)(2,1)}, u32[]{:S(2)}, u32[]{:S(2)}) collective-permute-start(bf16[4,64,768]{2,1,0:T(8,128)(2,1)} %fusion.108), channel_id=1, source_target_pairs={{0,1},{1,2},{2,3},{3,4},{4,5},{5,6},{6,7},{7,8},{8,9},{9,10},{10,1... | collective-permute-start | bytes 1179656 | tf_op jit(solution)/shard_map/while/body/eval_jaxpr/ppermute | solution.py:21
  1116.7 22.1 %collective-permute-start.2 = (bf16[4,64,768]{2,1,0:T(8,128)(2,1)}, bf16[4,64,768]{2,1,0:T(8,128)(2,1)}, u32[]{:S(2)}, u32[]{:S(2)}) collective-permute-start(bf16[4,64,768]{2,1,0:T(8,128)(2,1)} %fusion.108), channel_id=1, source_target_pairs={{0,1},{1,2},{2,3},{3,4},{4,5},{5,6},{6,7},{7,8},{8,9},{9,10},{10,1... | collective-permute-start | bytes 1179656 | tf_op jit(solution)/shard_map/while/body/eval_jaxpr/ppermute | solution.py:21
  1164.1 22.1 %collective-permute-start.2 = (bf16[4,64,768]{2,1,0:T(8,128)(2,1)}, bf16[4,64,768]{2,1,0:T(8,128)(2,1)}, u32[]{:S(2)}, u32[]{:S(2)}) collective-permute-start(bf16[4,64,768]{2,1,0:T(8,128)(2,1)} %fusion.108), channel_id=1, source_target_pairs={{0,1},{1,2},{2,3},{3,4},{4,5},{5,6},{6,7},{7,8},{8,9},{9,10},{10,1... | collective-permute-start | bytes 1179656 | tf_op jit(solution)/shard_map/while/body/eval_jaxpr/ppermute | solution.py:21
  1211.5 22.1 %collective-permute-start.2 = (bf16[4,64,768]{2,1,0:T(8,128)(2,1)}, bf16[4,64,768]{2,1,0:T(8,128)(2,1)}, u32[]{:S(2)}, u32[]{:S(2)}) collective-permute-start(bf16[4,64,768]{2,1,0:T(8,128)(2,1)} %fusion.108), channel_id=1, source_target_pairs={{0,1},{1,2},{2,3},{3,4},{4,5},{5,6},{6,7},{7,8},{8,9},{9,10},{10,1... | collective-permute-start | bytes 1179656 | tf_op jit(solution)/shard_map/while/body/eval_jaxpr/ppermute | solution.py:21
  1258.9 22.1 %collective-permute-start.2 = (bf16[4,64,768]{2,1,0:T(8,128)(2,1)}, bf16[4,64,768]{2,1,0:T(8,128)(2,1)}, u32[]{:S(2)}, u32[]{:S(2)}) collective-permute-start(bf16[4,64,768]{2,1,0:T(8,128)(2,1)} %fusion.108), channel_id=1, source_target_pairs={{0,1},{1,2},{2,3},{3,4},{4,5},{5,6},{6,7},{7,8},{8,9},{9,10},{10,1... | collective-permute-start | bytes 1179656 | tf_op jit(solution)/shard_map/while/body/eval_jaxpr/ppermute | solution.py:21
  1304.2 146.7 %reduce-scatter.11.cloned.1.call-start = ((), (), s32[]{:S(2)}) async-start(), calls=%async_computation.9 | async-start | bytes 5013504 | tf_op jit(solution)/shard_map/reduce_scatter | solution.py:245
  1310.6 219.1 %reduce-scatter.9.cloned.1.call-start = ((), (), s32[]{:S(2)}) async-start(), calls=%async_computation.8 | async-start | bytes 5013504 | tf_op jit(solution)/shard_map/reduce_scatter | solution.py:242
  1316.8 251.5 %all-reduce.4.cloned.1.call-start = ((), (), s32[]{:S(2)}) async-start(), calls=%async_computation.10 | async-start | bytes 1769472 | tf_op jit(solution)/shard_map/psum | solution.py:250
  (224 other events, 1560.9 us)
Sparse Core Ops, SparseCore 0:
  14.1 64.6 all-gather.2
  81.1 60.5 all-gather.4
  524.6 58.5 reduce-scatter.6
  1304.3 68.3 reduce-scatter.4
  1376.3 74.4 reduce-scatter.10
  1455.1 74.5 reduce-scatter.8
  1532.2 36.0 all-reduce.3
where the time goes:
time: 1600 us; the launch traced here: 1580 us
  local copies, waits for them, and re-layouts  463 us (29%)
  waiting for transfers between devices  316 us (20%)
  matrix products  312 us (20%)
  other arithmetic  280 us (18%)
  starting transfers between devices  152 us (10%)
  blocking collectives  42.3 us (3%)
    ppermute x32, starting transfers between devices, from_behind(): return lax.ppermute(shard, axis, pairs)  128 us
    dot_general x32, matrix products, block_scores(): jnp.einsum('sqhd,skhd->shqk', queries, key_heads, preferred_element_type=...  94.1 us
    while x304, local copies, waits for them, and re-layouts  80.8 us
    reduce_scatter x1, waiting for transfers between devices, per_device(): lax.psum_scatter(expand_part.astype(jnp.bfloat16), 'blk', scatter_dimensi...  78.8 us
    reshape x32, local copies, waits for them, and re-layouts, block_scores(): key_heads = key_block.reshape(streams, key_count, head_count, HEAD)  78.3 us
    reduce_scatter x1, waiting for transfers between devices, per_device(): lax.psum_scatter(shrink_part.astype(jnp.bfloat16), 'blk', scatter_dimensi...  78.2 us
    dot_general x16, matrix products, absorb(): jnp.einsum('shqk,skhd->shqd', shares.astype(jnp.bfloat16), value_heads, p...  67.4 us
    all_gather x1, waiting for transfers between devices, per_device(): value_piece = lax.all_gather(values_local, 'blk', axis=1, tiled=True)  62.8 us
  transfers between devices with their start and end apart: 71, of which 6 were waited for; matrix products, arithmetic and copies ran while one was open for 41% of the time, Pallas kernels for 0%

commit v1 on v0

v1 whole, which is shorter than its diff:
```python
import functools

import jax
import jax.numpy as jnp
from jax import lax
from jax.experimental import pallas as pl
from jax.experimental.pallas import tpu as pltpu
from jax.sharding import PartitionSpec as P

HEAD = 64
TILE = 256
WIDE = 512
big_negative = -1e30
norm_epsilon = 1e-05
VMEM_BYTES = 52 * 1024 * 1024

f32 = jnp.float32
bf16 = jnp.bfloat16


def dot(left, right):
    return jnp.dot(left, right, preferred_element_type=f32)


def dot_nt(left, right):
    return lax.dot_general(left, right, (((1,), (1,)), ((), ())), preferred_element_type=f32)


def dot_tn(left, right):
    return lax.dot_general(left, right, (((0,), (0,)), ((), ())), preferred_element_type=f32)


def normalized(values):
    centred = values - jnp.mean(values, axis=-1, keepdims=True)
    rate = lax.rsqrt(jnp.mean(centred * centred, axis=-1, keepdims=True) + norm_epsilon)
    return centred * rate, rate


def norm_back(normal, rate, weighted):
    return rate * (
        weighted
        - jnp.mean(weighted, axis=-1, keepdims=True)
        - normal * jnp.mean(weighted * normal, axis=-1, keepdims=True)
    )


def forward_kernel(
    place_ref, start_ref, gain_ref, weight_ref, pieces_ref,
    first_ref, joined_ref, shares_ref, attention_ref, sent_ref, rows_ref,
    *, planes, slots, seg, heads,
):
    plane, slot = place_ref[0], place_ref[1]
    for u in range(slots):
        for k in range(planes):
            offset = ((plane ^ k) * slots + (slot ^ u)) * seg
            rows_ref[pl.ds(pl.multiple_of(offset, seg), seg), :] = pieces_ref[u, k]
    length = planes * slots * seg
    width = heads * HEAD

    def project(tile, carry):
        rows = pl.ds(pl.multiple_of(tile * TILE, TILE), TILE)
        normal, _ = normalized(rows_ref[rows, :].astype(f32))
        first = (normal * gain_ref[...]).astype(bf16)
        first_ref[rows, :] = first
        joined = dot(first, weight_ref[...]).astype(bf16)
        for part in range(3):
            for h in range(heads):
                column = part * width + h * HEAD
                value = joined[:, column : column + HEAD]
                if part == 0:
                    value = value * jnp.asarray(0.125, bf16)
                joined_ref[part * heads + h, rows, :] = value
        return carry

    lax.fori_loop(0, length // TILE, project, 0)

    for q in range(length // TILE):
        rows = slice(q * TILE, (q + 1) * TILE)
        reach = (q + 1) * TILE
        query_pos = q * TILE + lax.broadcasted_iota(jnp.int32, (TILE, reach), 0)
        key_pos = lax.broadcasted_iota(jnp.int32, (TILE, reach), 1)
        allowed = (key_pos <= query_pos) & (key_pos >= start_ref[rows, :])
        for h in range(heads):
            scores = dot_nt(joined_ref[h, rows, :], joined_ref[heads + h, :reach, :])
            scores = jnp.where(allowed, scores, big_negative)
            peak = jnp.max(scores, axis=-1, keepdims=True)
            raised = jnp.exp(scores - peak)
            total = jnp.sum(raised, axis=-1, keepdims=True)
            shares = (raised * (1.0 / total)).astype(bf16)
            shares_ref[h, rows, :reach] = shares
            mixed = dot(shares, joined_ref[2 * heads + h, :reach, :])
            attention_ref[h, rows, :] = mixed
    block = slots * seg
    for s in range(slots):
        for z in range(planes):
            for h in range(heads):
                part = attention_ref[h, pl.ds(z * block + s * seg, seg), :]
                sent_ref[s, z * seg : (z + 1) * seg, h * HEAD : (h + 1) * HEAD] = part.astype(bf16)


def forward_call(place, start, gain, weight, pieces):
    slots, planes, seg, width = pieces.shape
    length = planes * slots * seg
    heads = weight.shape[1] // (3 * HEAD)
    kernel = functools.partial(forward_kernel, planes=planes, slots=slots, seg=seg, heads=heads)
    vmem = pl.BlockSpec(memory_space=pltpu.VMEM)
    return pl.pallas_call(
        kernel,
        out_shape=(
            jax.ShapeDtypeStruct((length, width), bf16),
            jax.ShapeDtypeStruct((3 * heads, length, HEAD), bf16),
            jax.ShapeDtypeStruct((heads, length, length), bf16),
            jax.ShapeDtypeStruct((heads, length, HEAD), f32),
            jax.ShapeDtypeStruct((slots, planes * seg, heads * HEAD), bf16),
        ),
        in_specs=[pl.BlockSpec(memory_space=pltpu.SMEM)] + [vmem] * 4,
        out_specs=(vmem,) * 5,
        scratch_shapes=[pltpu.VMEM((length, width), bf16)],
        compiler_params=pltpu.CompilerParams(vmem_limit_bytes=VMEM_BYTES),
        name="attention_forward",
    )(place, start, gain, weight, pieces)


def backward_kernel(
    place_ref, joined_ref, shares_ref, attention_ref, weight_ref, pieces_ref,
    grad_ref, branch_ref, arrived_ref, key_ref, value_ref, total_ref,
    *, planes, slots, seg, heads,
):
    slot = place_ref[1]
    block = slots * seg
    length = planes * block
    width = heads * HEAD
    for u in range(slots):
        for z in range(planes):
            offset = z * block + (slot ^ u) * seg
            arrived_ref[pl.ds(pl.multiple_of(offset, seg), seg), :] = pieces_ref[
                u, z * seg : (z + 1) * seg, :
            ]
    tiles = length // TILE
    for h in range(heads):
        for q in reversed(range(tiles)):
            rows = slice(q * TILE, (q + 1) * TILE)
            reach = (q + 1) * TILE
            grad = arrived_ref[rows, h * HEAD : (h + 1) * HEAD]
            inner = jnp.sum(grad.astype(f32) * attention_ref[h, rows, :], axis=-1, keepdims=True)
            shares = shares_ref[h, rows, :reach]
            grad_shares = dot_nt(grad, joined_ref[2 * heads + h, :reach, :])
            grad_scores = (shares.astype(f32) * (grad_shares - inner)).astype(bf16)
            query_grad = dot(grad_scores, joined_ref[heads + h, :reach, :]) * 0.125
            grad_ref[rows, h * HEAD : (h + 1) * HEAD] = query_grad.astype(bf16)
            key_add = dot_tn(joined_ref[h, rows, :], grad_scores)
            value_add = dot_tn(grad, shares)
            if q == tiles - 1:
                key_ref[...] = key_add
                value_ref[...] = value_add
            else:
                key_ref[:, :reach] += key_add
                value_ref[:, :reach] += value_add
        for part, source in ((1, key_ref), (2, value_ref)):
            column = part * width + h * HEAD
            for q in range(tiles):
                rows = slice(q * TILE, (q + 1) * TILE)
                grad_ref[rows, column : column + HEAD] = source[:, rows].T.astype(bf16)

    def back(tile, carry):
        rows = pl.ds(pl.multiple_of(tile * TILE, TILE), TILE)
        total_ref[rows, :] = dot_nt(grad_ref[rows, :], weight_ref[...]).astype(bf16)
        return carry

    lax.fori_loop(0, tiles, back, 0)
    for s in range(slots):
        for z in range(planes):
            branch_ref[s, z * seg : (z + 1) * seg, :] = total_ref[
                z * block + s * seg : z * block + (s + 1) * seg, :
            ]


def backward_call(place, joined, shares, attention, weight, pieces, planes):
    slots, tokens, _ = pieces.shape
    heads, length, _ = shares.shape
    width = weight.shape[0]
    kernel = functools.partial(
        backward_kernel, planes=planes, slots=slots, seg=tokens // planes, heads=heads
    )
    vmem = pl.BlockSpec(memory_space=pltpu.VMEM)
    return pl.pallas_call(
        kernel,
        out_shape=(
            jax.ShapeDtypeStruct((length, 3 * heads * HEAD), bf16),
            jax.ShapeDtypeStruct((slots, tokens, width), bf16),
        ),
        in_specs=[pl.BlockSpec(memory_space=pltpu.SMEM)] + [vmem] * 5,
        out_specs=(vmem,) * 2,
        scratch_shapes=[
            pltpu.VMEM((length, heads * HEAD), bf16),
            pltpu.VMEM((HEAD, length), f32),
            pltpu.VMEM((HEAD, length), f32),
            pltpu.VMEM((length, width), bf16),
        ],
        compiler_params=pltpu.CompilerParams(vmem_limit_bytes=VMEM_BYTES),
        name="attention_backward",
    )(place, joined, shares, attention, weight, pieces)


def middle_kernel(
    place_ref, pieces_ref, input_ref, cotangent_ref, valid_ref,
    merge_ref, expand_ref, shrink_ref, mixed_gain_ref, second_gain_ref, hidden_gain_ref,
    result_ref, mixed_ref, second_ref, hidden_ref, expanded_ref, mix_ref, branch_ref,
    grad_ref, away_ref, mixed_part_ref, second_part_ref, hidden_part_ref,
    held_ref, normal_ref, slope_ref, weighted_ref,
    *, slots, groups, width, spread,
):
    slot = place_ref[1]
    piece = width // groups
    for u in range(slots):
        held_ref[slot ^ u] = pieces_ref[u].astype(f32)
    mean = sum(jnp.sum(held_ref[g], axis=-1, keepdims=True) for g in range(groups)) * (1.0 / width)
    square = 0.0
    for g in range(groups):
        centred = held_ref[g] - mean
        held_ref[g] = centred
        square = square + jnp.sum(centred * centred, axis=-1, keepdims=True)
    mixed_rate = lax.rsqrt(square * (1.0 / width) + norm_epsilon)
    middle = input_ref[...].astype(f32)
    for g in range(groups):
        normal = held_ref[g] * mixed_rate
        held_ref[g] = normal
        mixed = (normal * mixed_gain_ref[g]).astype(bf16)
        mixed_ref[g] = mixed
        middle = middle + dot(mixed, merge_ref[g * piece : (g + 1) * piece, :])
    second_normal, second_rate = normalized(middle)
    second = (second_normal * second_gain_ref[...]).astype(bf16)
    second_ref[...] = second
    grad_out = cotangent_ref[...].astype(f32) * valid_ref[...]
    branch = grad_out.astype(bf16)
    branch_ref[...] = branch
    tokens = middle.shape[0]
    steps = spread // WIDE
    column = jnp.zeros((tokens, 1), f32)

    def columns(step):
        return pl.ds(pl.multiple_of(step * WIDE, WIDE), WIDE)

    def widen(step, total):
        at = columns(step)
        value = dot(second, expand_ref[:, at])
        share = 0.5 * (1.0 + lax.erf(value * 0.7071067811865476))
        gelu = value * share
        normal_ref[:, at] = gelu
        slope_ref[:, at] = share + value * (0.3989422804014327 * jnp.exp(-0.5 * value * value))
        return total + jnp.sum(gelu, axis=-1, keepdims=True)

    hidden_mean = lax.fori_loop(0, steps, widen, column) * (1.0 / spread)

    def deviate(step, total):
        centred = normal_ref[:, columns(step)] - hidden_mean
        return total + jnp.sum(centred * centred, axis=-1, keepdims=True)

    variance = lax.fori_loop(0, steps, deviate, column) * (1.0 / spread)
    hidden_rate = lax.rsqrt(variance + norm_epsilon)

    def narrow(step, carry):
        result, weighted_sum, inner_sum = carry
        at = columns(step)
        normal = (normal_ref[:, at] - hidden_mean) * hidden_rate
        normal_ref[:, at] = normal
        gain = hidden_gain_ref[:, at]
        hidden = (normal * gain).astype(bf16)
        hidden_ref[:, at] = hidden
        result = result + dot(hidden, shrink_ref[at, :])
        grad_hidden = dot_nt(branch, shrink_ref[at, :])
        hidden_part_ref[:, at] = jnp.sum(grad_hidden * normal, axis=0, keepdims=True)
        weighted = grad_hidden * gain
        weighted_ref[:, at] = weighted
        return (
            result,
            weighted_sum + jnp.sum(weighted, axis=-1, keepdims=True),
            inner_sum + jnp.sum(weighted * normal, axis=-1, keepdims=True),
        )

    result, weighted_sum, inner_sum = lax.fori_loop(0, steps, narrow, (middle, column, column))
    result_ref[...] = result.astype(bf16)
    weighted_mean = weighted_sum * (1.0 / spread)
    inner_mean = inner_sum * (1.0 / spread)

    def turn(step, total):
        at = columns(step)
        grad = hidden_rate * (
            weighted_ref[:, at] - weighted_mean - normal_ref[:, at] * inner_mean
        )
        expanded = (grad * slope_ref[:, at]).astype(bf16)
        expanded_ref[:, at] = expanded
        return total + dot_nt(expanded, expand_ref[:, at])

    grad_second = lax.fori_loop(0, steps, turn, jnp.zeros((tokens, width), f32))
    second_part_ref[...] = jnp.sum(grad_second * second_normal, axis=0, keepdims=True)
    grad_middle = grad_out + norm_back(
        second_normal, second_rate, grad_second * second_gain_ref[...]
    )
    grad_ref[...] = grad_middle
    mix = grad_middle.astype(bf16)
    mix_ref[...] = mix
    grads = []
    weighted_sum = 0.0
    inner_sum = 0.0
    for g in range(groups):
        grad_mixed = dot_nt(mix, merge_ref[g * piece : (g + 1) * piece, :])
        mixed_part_ref[g] = jnp.sum(grad_mixed * held_ref[g], axis=0, keepdims=True)
        weighted = grad_mixed * mixed_gain_ref[g]
        grads.append(weighted)
        weighted_sum = weighted_sum + jnp.sum(weighted, axis=-1, keepdims=True)
        inner_sum = inner_sum + jnp.sum(weighted * held_ref[g], axis=-1, keepdims=True)
    weighted_mean = weighted_sum * (1.0 / width)
    inner_mean = inner_sum * (1.0 / width)
    for g in range(slots):
        if g < groups:
            grad = mixed_rate * (grads[g] - weighted_mean - held_ref[g] * inner_mean)
            away_ref[g] = grad.astype(bf16)
        else:
            away_ref[g] = jnp.zeros(away_ref.shape[1:], bf16)


def middle_call(
    place, pieces, inputs, cotangent, valid, merge, expand, shrink,
    mixed_gain, second_gain, hidden_gain,
):
    slots, tokens, piece = pieces.shape
    width, spread = expand.shape
    groups = width // piece
    kernel = functools.partial(
        middle_kernel, slots=slots, groups=groups, width=width, spread=spread
    )
    vmem = pl.BlockSpec(memory_space=pltpu.VMEM)

    def low(*shape):
        return jax.ShapeDtypeStruct(shape, bf16)

    def full(*shape):
        return jax.ShapeDtypeStruct(shape, f32)

    return pl.pallas_call(
        kernel,
        out_shape=(
            low(tokens, width),
            low(groups, tokens, piece),
            low(tokens, width),
            low(tokens, spread),
            low(tokens, spread),
            low(tokens, width),
            low(tokens, width),
            full(tokens, width),
            low(slots, tokens, piece),
            full(groups, 1, piece),
            full(1, width),
            full(1, spread),
        ),
        in_specs=[pl.BlockSpec(memory_space=pltpu.SMEM)] + [vmem] * 10,
        out_specs=(vmem,) * 12,
        scratch_shapes=[
            pltpu.VMEM((slots, tokens, piece), f32),
            pltpu.VMEM((tokens, spread), f32),
            pltpu.VMEM((tokens, spread), f32),
            pltpu.VMEM((tokens, spread), f32),
        ],
        compiler_params=pltpu.CompilerParams(vmem_limit_bytes=VMEM_BYTES),
        name="middle",
    )(
        place, pieces, inputs, cotangent, valid, merge, expand, shrink,
        mixed_gain.reshape(groups, 1, piece), second_gain.reshape(1, width),
        hidden_gain.reshape(1, spread),
    )


def swap(value, axis, bits):
    size = lax.axis_size(axis)
    return lax.ppermute(value, axis, [(i, i ^ bits) for i in range(size)])


def pick(value, index, axis=0):
    return lax.dynamic_index_in_dim(value, index, axis, keepdims=False)


def added(left, right):
    return (left.astype(f32) + right.astype(f32)).astype(bf16)


def bits_of(size):
    return size.bit_length() - 1


def per_device(
    layer_input, cotangent, doc_lengths, joined_weight, merge_weight, expand_weight,
    shrink_weight, first_gain, mixed_gain, second_gain, hidden_gain,
):
    _, planes, seg, width = layer_input.shape
    spread = expand_weight.shape[1]
    size = lax.axis_size("blk")
    slots = size // planes
    batches = lax.axis_size("batch")
    rank = lax.axis_index("blk")
    group_rank = lax.axis_index("batch")
    plane = rank // slots
    slot = rank % slots
    head_count = width // HEAD
    heads = -(-head_count // slots)
    groups = head_count // heads
    piece = heads * HEAD
    tokens = planes * seg
    length = slots * tokens
    place = jnp.stack([plane, slot]).astype(jnp.int32)

    def to_planes(blocks):
        return [pick(blocks, plane)] + [
            swap(pick(blocks, plane ^ k), "blk", k * slots) for k in range(1, planes)
        ]

    def in_order(blocks):
        stacked = jnp.stack(blocks)
        return jnp.stack([pick(stacked, plane ^ k) for k in range(planes)])

    def all_slots(value):
        held = [value]
        for bit in reversed(range(bits_of(slots))):
            held = held + [swap(v, "blk", 1 << bit) for v in held]
        ordered = [None] * slots
        for at, v in enumerate(held):
            code = 0
            for order, bit in enumerate(reversed(range(bits_of(slots)))):
                if at >> order & 1:
                    code |= 1 << bit
            ordered[code] = v
        return ordered

    def over_slots(blocks):
        return jnp.stack(
            [pick(blocks, slot)]
            + [swap(pick(blocks, slot ^ u), "blk", u) for u in range(1, slots)]
        )

    arrived = to_planes(layer_input[0])
    quarter = jnp.stack(arrived)
    pieces = jnp.stack(all_slots(quarter))
    ends = jnp.cumsum(pick(doc_lengths[0], plane), axis=-1)
    positions = jnp.arange(length, dtype=jnp.int32)
    reached = ends[None, :] <= positions[:, None]
    start = jnp.max(jnp.where(reached, ends[None, :], 0), axis=-1, keepdims=True)
    own_start = jnp.clip(jnp.minimum(slot, groups - 1) * piece, 0, width - piece)
    columns = [
        lax.dynamic_slice_in_dim(joined_weight, part * width + own_start, piece, 1)
        for part in range(3)
    ]
    own_weight = jnp.concatenate(columns, axis=1)
    first, joined, shares, attention, sent = forward_call(
        place, start, first_gain.reshape(1, width), own_weight, pieces
    )
    cotangent_rows = in_order(to_planes(cotangent[0])).reshape(tokens, width)
    input_rows = in_order(arrived).reshape(tokens, width)
    own_pos = (
        jnp.arange(planes, dtype=jnp.int32)[:, None] * (slots * seg)
        + slot * seg
        + jnp.arange(seg, dtype=jnp.int32)[None, :]
    ).reshape(tokens, 1)
    valid = (own_pos < ends[-1]).astype(f32)
    (
        result, mixed, second, hidden, expanded, mix, branch, grad_middle, away,
        mixed_part, second_part, hidden_part,
    ) = middle_call(
        place, over_slots(sent), input_rows, cotangent_rows, valid,
        merge_weight, expand_weight, shrink_weight, mixed_gain, second_gain, hidden_gain,
    )

    def to_owners(rows):
        blocks = rows.reshape(planes, seg, width)
        return in_order(to_planes(blocks)).reshape(layer_input.shape)

    layer_result = to_owners(result)
    grad_joined, first_branch = backward_call(
        place, joined, shares, attention, own_weight, over_slots(away), planes
    )

    rows_view = (planes, slots)

    def halve(value, axis, stride, bit_axis):
        rank_bit = (lax.axis_index(axis) // stride) % 2
        keep = pick(value, rank_bit, bit_axis)
        give = pick(value, 1 - rank_bit, bit_axis)
        return added(keep, swap(give, axis, stride))

    def split_bits(value):
        return value.reshape((2,) * bits_of(size) + (value.shape[0] // size,) + value.shape[1:])

    def halve_blk(value, bit, left):
        at = left.index(bit)
        return halve(value, "blk", 1 << bit, at), [b for b in left if b != bit]

    def halve_batch(value):
        half = value.shape[-1] // 2
        bit = group_rank % 2
        keep = lax.dynamic_slice_in_dim(value, bit * half, half, value.ndim - 1)
        give = lax.dynamic_slice_in_dim(value, (1 - bit) * half, half, value.ndim - 1)
        return added(keep, swap(give, "batch", 1))

    def finish(value):
        for bit in range(1, bits_of(batches)):
            value = added(value, swap(value, "batch", 1 << bit))
        other = swap(value, "batch", 1)
        low_first = group_rank % 2 == 0
        return jnp.concatenate(
            [jnp.where(low_first, value, other), jnp.where(low_first, other, value)], axis=-1
        ).astype(f32)

    all_bits = list(reversed(range(bits_of(size))))
    slot_bits = bits_of(slots)
    row_bits = list(range(1, slot_bits))
    plane_bits = list(range(slot_bits, bits_of(size)))

    def reduce_rows(value, order):
        value = split_bits(value.astype(bf16))
        left = all_bits
        for step in order:
            if step == "batch":
                value = halve_batch(value)
            else:
                value, left = halve_blk(value, step, left)
        return finish(value)

    shrink_grad = reduce_rows(dot_tn(hidden, branch), [0, "batch"] + row_bits + plane_bits)
    expand_grad = reduce_rows(dot_tn(second, expanded), [0] + row_bits + ["batch"] + plane_bits)
    merge_part = jnp.concatenate([dot_tn(mixed[g], mix) for g in range(groups)], axis=0)
    merge_grad = reduce_rows(merge_part, [0] + row_bits + ["batch"] + plane_bits)

    joined_part = dot_tn(first, grad_joined).astype(bf16)
    value = joined_part.reshape((2,) * len(plane_bits) + (width // planes, 3 * piece))
    left = list(reversed(plane_bits))
    for bit in plane_bits:
        value, left = halve_blk(value, bit, left)
    for bit in range(bits_of(batches)):
        value = added(value, swap(value, "batch", 1 << bit))
    value = over_slots(value.reshape(slots, width // size, 3 * piece))
    value = jnp.stack([pick(value, slot ^ u) for u in range(groups)])
    value = value.reshape(groups, width // size, 3, piece).transpose(1, 2, 0, 3)
    joined_grad = value.reshape(width // size, 3 * width).astype(f32)

    branch_sum = first_branch.reshape((2,) * slot_bits + (tokens, width))
    left = list(reversed(range(slot_bits)))
    for bit in range(slot_bits):
        branch_sum, left = halve_blk(branch_sum, bit, left)
    grad_first = branch_sum.astype(f32)
    first_normal, first_rate = normalized(input_rows.astype(f32))
    first_part = jnp.sum(grad_first * first_normal, axis=0)
    input_grad = to_owners(
        (grad_middle + norm_back(first_normal, first_rate, grad_first * first_gain)).astype(bf16)
    )

    def everywhere(value):
        for bit in range(bits_of(size)):
            value = value + swap(value, "blk", 1 << bit)
        for bit in range(bits_of(batches)):
            value = value + swap(value, "batch", 1 << bit)
        return value

    early = everywhere(
        jnp.concatenate([mixed_part.reshape(1, width), second_part, hidden_part], axis=1)
    )[0]
    first_total = everywhere(first_part.reshape(1, width))[0]
    return (
        layer_result, input_grad, joined_grad, merge_grad, expand_grad, shrink_grad,
        first_total, early[:width], early[width : 2 * width], early[2 * width :],
    )


def solution(mesh):
    rows = P("batch", None, "blk", None)
    return jax.shard_map(
        per_device,
        mesh=mesh,
        in_specs=(rows, rows, P("batch", None, None)) + (P(),) * 8,
        out_specs=(rows, rows) + (P("blk", None),) * 4 + (P(),) * 4,
        check_vma=False,
    )
```

time: 1600 us -> 286 us (0.18); the launches traced: 1580 us -> 285 us
  local copies, waits for them, and re-layouts: 463 us -> 24.4 us
  matrix products: 312 us -> 13.3 us
  other arithmetic: 280 us -> 24.7 us
  waiting for transfers between devices: 316 us -> 114 us
  starting transfers between devices: 152 us -> 59.1 us
  Pallas kernels: 0 us -> 48.2 us
  blocking collectives: 42.3 us -> 0 us
    dot_general x124 -> x7, matrix products: 312 us -> 13.3 us  [dot_tn(): lax.dot_general(left, right, (((0,), (0,)), ((), ())), preferred_element_...]
    reshape x103 -> x6, local copies, waits for them, and re-layouts: 260 us -> 0.18 us  [the longest x1 0.09 us: per_device(): mixed_part.reshape(1, width)]
    reduce_scatter x4 -> x0, waiting for transfers between devices: 165 us -> none  [the longest x1 78.8 us: per_device(): lax.psum_scatter(expand_part.astype(jnp.bfloat16), 'blk', scatter_dimensi...]
    convert_element_type x75 -> x25, other arithmetic: 150 us -> 12.3 us  [the longest x19 8.77 us: added(): return (left.astype(f32) + right.astype(f32)).astype(bf16)]
    all_gather x2 -> x0, waiting for transfers between devices: 120 us -> none  [the longest x1 62.8 us: per_device(): value_piece = lax.all_gather(values_local, 'blk', axis=1, tiled=True)]
    ppermute x64 -> x57, waiting for transfers between devices: 0.17 us -> 114 us  [swap(): return lax.ppermute(value, axis, [(i, i ^ bits) for i in range(size)])]
    ppermute x64 -> x57, starting transfers between devices: 151 us -> 59.1 us  [swap(): return lax.ppermute(value, axis, [(i, i ^ bits) for i in range(size)])]
    while x304 -> x0, local copies, waits for them, and re-layouts: 80.8 us -> none
  transfers between devices with their start and end apart: 71 -> 57, of which waited for: 6 -> 30; matrix products, arithmetic and copies ran while one was open for 41% -> 18% of each run, Pallas kernels for 0% -> 4%
where the time goes in v1:
time: 286 us; the launch traced here: 285 us
  waiting for transfers between devices  114 us (40%)
  starting transfers between devices  59.1 us (21%)
  Pallas kernels  48.2 us (17%)
  other arithmetic  24.7 us (9%)
  local copies, waits for them, and re-layouts  24.4 us (9%)
  matrix products  13.3 us (5%)
    ppermute x57, waiting for transfers between devices, swap(): return lax.ppermute(value, axis, [(i, i ^ bits) for i in range(size)])  114 us
    ppermute x57, starting transfers between devices, swap(): return lax.ppermute(value, axis, [(i, i ^ bits) for i in range(size)])  59.1 us
    pallas_call x1, Pallas kernels, middle_call(): pl.pallas_call(kernel, out_shape=(low(tokens, width), low(groups, tokens,...  22.2 us
    pallas_call x1, Pallas kernels, forward_call(): pl.pallas_call(kernel, out_shape=(jax.ShapeDtypeStruct((length, width), b...  13.9 us
    dot_general x7, matrix products, dot_tn(): lax.dot_general(left, right, (((0,), (0,)), ((), ())), preferred_element_...  13.3 us
    dynamic_slice x18, local copies, waits for them, and re-layouts, pick(): return lax.dynamic_index_in_dim(value, index, axis, keepdims=False)  12.2 us
    pallas_call x1, Pallas kernels, backward_call(): pl.pallas_call(kernel, out_shape=(jax.ShapeDtypeStruct((length, 3 * heads...  12.2 us
    convert_element_type x19, other arithmetic, added(): return (left.astype(f32) + right.astype(f32)).astype(bf16)  8.77 us
  transfers between devices with their start and end apart: 57, of which 30 were waited for; matrix products, arithmetic and copies ran while one was open for 18% of the time, Pallas kernels for 4%

profile of v1, /device:TPU:0, one launch (start us, length us, event | category | flops | bytes accessed | tf_op | source)
XLA Modules:
  0.0 285.0 jit_solution(9903174341538752099)
XLA Ops:
  1.8 5.1 %collective-permute-start.2 = (bf16[64,768]{1,0:T(8,128)(2,1)S(1)}, bf16[64,768]{1,0:T(8,128)(2,1)S(1)}, u32[]{:S(2)}, u32[]{:S(2)}) collective-permute-start(bf16[64,768]{1,0:T(8,128)(2,1)S(1)} %get-tuple-element.105), channel_id=1, source_target_pairs={{0,12},{1,13},{2,14},{3,15},{4,8},{5,9},{6,10},{7,11},{8,4},{9,5},... | collective-permute-start | bytes 294920 | tf_op jit(solution)/shard_map/ppermute | solution.py:376
  9.3 3.7 %collective-permute-start.11 = (bf16[64,768]{1,0:T(8,128)(2,1)}, bf16[64,768]{1,0:T(8,128)(2,1)S(1)}, u32[]{:S(2)}, u32[]{:S(2)}) collective-permute-start(bf16[64,768]{1,0:T(8,128)(2,1)} %get-tuple-element.95), channel_id=1, source_target_pairs={{0,12},{1,13},{2,14},{3,15},{4,8},{5,9},{6,10},{7,11},{8,4},{9,5},... | collective-permute-start | bytes 294920 | tf_op jit(solution)/shard_map/ppermute | solution.py:376
  22.5 7.3 %collective-permute-done.4 = bf16[4,64,768]{2,1,0:T(8,128)(2,1)S(1)} collective-permute-done((bf16[4,64,768]{2,1,0:T(8,128)(2,1)S(1)}, bf16[4,64,768]{2,1,0:T(8,128)(2,1)S(1)}, u32[]{:S(2)}, u32[]{:S(2)}) %collective-permute-start.4) | collective-permute-done | bytes 393248 | tf_op jit(solution)/shard_map/ppermute | solution.py:376
  32.9 13.9 %attention_forward.1 = (bf16[1024,768]{1,0:T(8,128)(2,1)}, bf16[9,1024,64]{2,1,0:T(8,128)(2,1)}, bf16[3,1024,1024]{2,1,0:T(8,128)(2,1)}, f32[3,1024,64]{2,1,0:T(8,128)}, bf16[4,256,192]{2,1,0:T(8,128)(2,1)S(1)}) custom-call(s32[2]{0:T(128)S(1)} %pad_add_fusion.place_ref, s32[1024,1]{1,0:T(8,128)S(1)} %copy.49.start_ref, f32[1,768]{1,0:T(1,128)S(1)} %reshape.223.gain_ref, ...), custom_call_target="tpu_custom_call" | custom-call | tf_op jit(solution)/shard_map/attention_forward/pallas_call | solution.py:107
  49.6 2.8 collective-permute-done.8
  52.4 3.1 %collective-permute-done.7 = bf16[256,192]{1,0:T(8,128)(2,1)S(1)} collective-permute-done((bf16[256,192]{1,0:T(8,128)(2,1)S(1)}, bf16[256,192]{1,0:T(8,128)(2,1)S(1)}, u32[]{:S(2)}, u32[]{:S(2)}) %collective-permute-start.7) | collective-permute-done | bytes 98336 | tf_op jit(solution)/shard_map/ppermute | solution.py:376
  56.4 22.2 %middle.1 = (bf16[256,768]{1,0:T(8,128)(2,1)S(1)}, bf16[4,256,192]{2,1,0:T(8,128)(2,1)}, bf16[256,768]{1,0:T(8,128)(2,1)S(1)}, bf16[256,3072]{1,0:T(8,128)(2,1)}...) custom-call(s32[2]{0:T(128)S(1)} %pad_add_fusion.place_ref, ...), custom_call_target="tpu_custom_call" | custom-call | tf_op jit(solution)/shard_map/middle/pallas_call | solution.py:341
  94.6 2.6 collective-permute-start.14
  102.5 4.2 %collective-permute-done.55 = f32[1,4608]{1,0:T(1,128)S(1)} collective-permute-done((f32[1,4608]{1,0:T(1,128)S(1)}, f32[1,4608]{1,0:T(1,128)S(1)}, u32[]{:S(2)}, u32[]{:S(2)}) %collective-permute-start.55) | collective-permute-done | bytes 18464 | tf_op jit(solution)/shard_map/ppermute | solution.py:376
  116.9 12.2 %attention_backward.1 = (bf16[1024,576]{1,0:T(8,128)(2,1)}, bf16[4,256,768]{2,1,0:T(8,128)(2,1)}) custom-call(s32[2]{0:T(128)S(1)} %pad_add_fusion.place_ref, bf16[9,1024,64]{2,1,0:T(8,128)(2,1)} %get-tuple-element.32.joined_ref, bf16[3,1024,1024]{2,1,0:T(8,128)(2,1)} %get-tuple-element.33.shares_ref, f32[3,1024,64]{2,1,0:T(8,128)} %get-tuple-element.34.attention_ref, ...), custom_call_target="tpu_custom_call" | custom-call | tf_op jit(solution)/shard_map/attention_backward/pallas_call | solution.py:186
  129.1 3.4 %convolution_convert_fusion.2 = bf16[768,576]{0,1:T(8,128)(2,1)} fusion(bf16[1024,768]{1,0:T(8,128)(2,1)S(1)} %copy-done.21, bf16[1024,576]{1,0:T(8,128)(2,1)} %get-tuple-element.38), kind=kOutput, calls=%fused_computation.16 | convolution fusion | flops 906412032 | bytes 3637248 | tf_op jit(solution)/shard_map/dot_general | solution.py:30
  137.1 10.8 %collective-permute-done.23 = bf16[2,192,576]{2,1,0:T(8,128)(2,1)S(1)} collective-permute-done((bf16[2,192,576]{2,1,0:T(8,128)(2,1)S(1)}, bf16[2,192,576]{2,1,0:T(8,128)(2,1)S(1)}, u32[]{:S(2)}, u32[]{:S(2)}) %collective-permute-start.23) | collective-permute-done | bytes 442400 | tf_op jit(solution)/shard_map/ppermute | solution.py:376
  152.2 9.5 %collective-permute-done.24 = bf16[192,576]{1,0:T(8,128)(2,1)S(1)} collective-permute-done((bf16[192,576]{1,0:T(8,128)(2,1)S(1)}, bf16[192,576]{1,0:T(8,128)(2,1)S(1)}, u32[]{:S(2)}, u32[]{:S(2)}) %collective-permute-start.24) | collective-permute-done | bytes 221216 | tf_op jit(solution)/shard_map/ppermute | solution.py:376
  165.1 5.6 %collective-permute-done.25 = bf16[192,576]{1,0:T(8,128)(2,1)S(1)} collective-permute-done((bf16[192,576]{1,0:T(8,128)(2,1)S(1)}, bf16[192,576]{1,0:T(8,128)(2,1)S(1)}, u32[]{:S(2)}, u32[]{:S(2)}) %collective-permute-start.25) | collective-permute-done | bytes 221216 | tf_op jit(solution)/shard_map/ppermute | solution.py:376
  176.5 4.2 %collective-permute-done.32 = bf16[2,48,384]{2,1,0:T(8,128)(2,1)S(1)} collective-permute-done((bf16[2,48,384]{2,1,0:T(8,128)(2,1)S(1)}, bf16[2,48,384]{2,1,0:T(8,128)(2,1)S(1)}, u32[]{:S(2)}, u32[]{:S(2)}) %collective-permute-start.32) | collective-permute-done | bytes 73760 | tf_op jit(solution)/shard_map/ppermute | solution.py:376
  201.3 2.9 %collective-permute-done.50 = f32[1,768]{1,0:T(1,128)S(1)} collective-permute-done((f32[1,768]{1,0:T(1,128)S(1)}, f32[1,768]{1,0:T(1,128)S(1)}, u32[]{:S(2)}, u32[]{:S(2)}) %collective-permute-start.50) | collective-permute-done | bytes 3104 | tf_op jit(solution)/shard_map/ppermute | solution.py:376
  217.4 7.1 %collective-permute-done.36 = bf16[2,2,48,3072]{3,2,0,1:T(8,128)(2,1)S(1)} collective-permute-done((bf16[2,2,48,3072]{3,2,0,1:T(8,128)(2,1)S(1)}, bf16[2,2,48,3072]{3,2,0,1:T(8,128)(2,1)S(1)}, u32[]{:S(2)}, u32[]{:S(2)}) %collective-permute-start.36) | collective-permute-done | bytes 1179680 | tf_op jit(solution)/shard_map/ppermute | solution.py:376
  227.6 17.7 %collective-permute-done.42 = bf16[2,2,2,192,384]{4,3,0,1,2:T(8,128)(2,1)S(1)} collective-permute-done((bf16[2,2,2,192,384]{4,3,0,1,2:T(8,128)(2,1)S(1)}, bf16[2,2,2,192,384]{4,3,0,1,2:T(8,128)(2,1)S(1)}, u32[]{:S(2)}, u32[]{:S(2)}) %collective-permute-start.42) | collective-permute-done | bytes 1179680 | tf_op jit(solution)/shard_map/ppermute | solution.py:376
  247.0 5.9 %collective-permute-done.37 = bf16[2,2,48,1536]{3,2,0,1:T(8,128)(2,1)S(1)} collective-permute-done((bf16[2,2,48,1536]{3,2,0,1:T(8,128)(2,1)S(1)}, bf16[2,2,48,1536]{3,2,0,1:T(8,128)(2,1)S(1)}, u32[]{:S(2)}, u32[]{:S(2)}) %collective-permute-start.37) | collective-permute-done | bytes 589856 | tf_op jit(solution)/shard_map/ppermute | solution.py:376
  256.1 4.2 %collective-permute-done.38 = bf16[2,48,1536]{2,1,0:T(8,128)(2,1)S(1)} collective-permute-done((bf16[2,48,1536]{2,1,0:T(8,128)(2,1)S(1)}, bf16[2,48,1536]{2,1,0:T(8,128)(2,1)S(1)}, u32[]{:S(2)}, u32[]{:S(2)}) %collective-permute-start.38) | collective-permute-done | bytes 294944 | tf_op jit(solution)/shard_map/ppermute | solution.py:376
  260.5 7.2 %collective-permute-start.39 = (bf16[48,1536]{1,0:T(8,128)(2,1)S(1)}, bf16[48,1536]{1,0:T(8,128)(2,1)S(1)}, u32[]{:S(2)}, u32[]{:S(2)}) collective-permute-start(bf16[48,1536]{1,0:T(8,128)(2,1)S(1)} %dynamic-slice_bitcast_fusion.10), channel_id=1, source_target_pairs={{0,8},{1,9},{2,10},{3,11},{4,12},{5,13},{6,14},{7,15},{8,0},{9,1},... | collective-permute-start | bytes 442376 | tf_op jit(solution)/shard_map/ppermute | solution.py:376
  267.8 4.1 %collective-permute-start.45 = (bf16[192,384]{1,0:T(8,128)(2,1)S(1)}, bf16[192,384]{1,0:T(8,128)(2,1)S(1)}, u32[]{:S(2)}, u32[]{:S(2)}) collective-permute-start(bf16[192,384]{1,0:T(8,128)(2,1)S(1)} %dynamic-slice_bitcast_fusion.9), channel_id=1, source_target_pairs={{0,8},{1,9},{2,10},{3,11},{4,12},{5,13},{6,14},{7,15},{8,0},{9,1},... | collective-permute-start | bytes 442376 | tf_op jit(solution)/shard_map/ppermute | solution.py:376
  271.9 5.0 %collective-permute-done.39 = bf16[48,1536]{1,0:T(8,128)(2,1)S(1)} collective-permute-done((bf16[48,1536]{1,0:T(8,128)(2,1)S(1)}, bf16[48,1536]{1,0:T(8,128)(2,1)S(1)}, u32[]{:S(2)}, u32[]{:S(2)}) %collective-permute-start.39) | collective-permute-done | bytes 147488 | tf_op jit(solution)/shard_map/ppermute | solution.py:376
  279.2 3.4 %collective-permute-done.40 = bf16[48,1536]{1,0:T(8,128)(2,1)S(1)} collective-permute-done((bf16[48,1536]{1,0:T(8,128)(2,1)S(1)}, bf16[48,1536]{1,0:T(8,128)(2,1)S(1)}, u32[]{:S(2)}, u32[]{:S(2)}) %collective-permute-start.40) | collective-permute-done | bytes 147488 | tf_op jit(solution)/shard_map/ppermute | solution.py:376
  (261 shorter events, 115.3 us)
Async XLA Ops:
  1.8 16.8 %collective-permute-start.2 = (bf16[64,768]{1,0:T(8,128)(2,1)S(1)}, bf16[64,768]{1,0:T(8,128)(2,1)S(1)}, u32[]{:S(2)}, u32[]{:S(2)}) collective-permute-start(bf16[64,768]{1,0:T(8,128)(2,1)S(1)} %get-tuple-element.105), channel_id=1, source_target_pairs={{0,12},{1,13},{2,14},{3,15},{4,8},{5,9},{6,10},{7,11},{8,4},{9,5},... | collective-permute-start | bytes 294920 | tf_op jit(solution)/shard_map/ppermute | solution.py:376
  6.9 13.4 %collective-permute-start.1 = (bf16[64,768]{1,0:T(8,128)(2,1)S(1)}, bf16[64,768]{1,0:T(8,128)(2,1)S(1)}, u32[]{:S(2)}, u32[]{:S(2)}) collective-permute-start(bf16[64,768]{1,0:T(8,128)(2,1)S(1)} %get-tuple-element.106), channel_id=1, source_target_pairs={{0,8},{1,9},{2,10},{3,11},{4,12},{5,13},{6,14},{7,15},{8,0},{9,1},... | collective-permute-start | bytes 294920 | tf_op jit(solution)/shard_map/ppermute | solution.py:376
  6.9 13.4 %collective-permute-start = (bf16[64,768]{1,0:T(8,128)(2,1)S(1)}, bf16[64,768]{1,0:T(8,128)(2,1)S(1)}, u32[]{:S(2)}, u32[]{:S(2)}) collective-permute-start(bf16[64,768]{1,0:T(8,128)(2,1)S(1)} %get-tuple-element.104), channel_id=1, source_target_pairs={{0,4},{1,5},{2,6},{3,7},{4,0},{5,1},{6,2},{7,3},{8,12},{9,13},{10,... | collective-permute-start | bytes 294920 | tf_op jit(solution)/shard_map/ppermute | solution.py:376
  9.3 20.6 %collective-permute-start.11 = (bf16[64,768]{1,0:T(8,128)(2,1)}, bf16[64,768]{1,0:T(8,128)(2,1)S(1)}, u32[]{:S(2)}, u32[]{:S(2)}) collective-permute-start(bf16[64,768]{1,0:T(8,128)(2,1)} %get-tuple-element.95), channel_id=1, source_target_pairs={{0,12},{1,13},{2,14},{3,15},{4,8},{5,9},{6,10},{7,11},{8,4},{9,5},... | collective-permute-start | bytes 294920 | tf_op jit(solution)/shard_map/ppermute | solution.py:376
  13.0 16.8 %collective-permute-start.10 = (bf16[64,768]{1,0:T(8,128)(2,1)}, bf16[64,768]{1,0:T(8,128)(2,1)S(1)}, u32[]{:S(2)}, u32[]{:S(2)}) collective-permute-start(bf16[64,768]{1,0:T(8,128)(2,1)} %get-tuple-element.96), channel_id=1, source_target_pairs={{0,8},{1,9},{2,10},{3,11},{4,12},{5,13},{6,14},{7,15},{8,0},{9,1},... | collective-permute-start | bytes 294920 | tf_op jit(solution)/shard_map/ppermute | solution.py:376
  85.2 30.6 %collective-permute-start.16 = (bf16[256,192]{1,0:T(8,128)(2,1)}, bf16[256,192]{1,0:T(8,128)(2,1)}, u32[]{:S(2)}, u32[]{:S(2)}) collective-permute-start(bf16[256,192]{1,0:T(8,128)(2,1)} %get-tuple-element.67), channel_id=1, source_target_pairs={{0,2},{1,3},{2,0},{3,1},{4,6},{5,7},{6,4},{7,5},{8,10},{9,11},{10,... | collective-permute-start | bytes 294920 | tf_op jit(solution)/shard_map/ppermute | solution.py:376
  86.7 29.1 %collective-permute-start.15 = (bf16[256,192]{1,0:T(8,128)(2,1)}, bf16[256,192]{1,0:T(8,128)(2,1)}, u32[]{:S(2)}, u32[]{:S(2)}) collective-permute-start(bf16[256,192]{1,0:T(8,128)(2,1)} %get-tuple-element.68), channel_id=1, source_target_pairs={{0,1},{1,0},{2,3},{3,2},{4,5},{5,4},{6,7},{7,6},{8,9},{9,8},{10,11... | collective-permute-start | bytes 294920 | tf_op jit(solution)/shard_map/ppermute | solution.py:376
  94.6 40.5 %collective-permute-start.14 = (bf16[64,768]{1,0:T(8,128)(2,1)}, bf16[64,768]{1,0:T(8,128)(2,1)S(1)}, u32[]{:S(2)}, u32[]{:S(2)}) collective-permute-start(bf16[64,768]{1,0:T(8,128)(2,1)} %get-tuple-element.86), channel_id=1, source_target_pairs={{0,12},{1,13},{2,14},{3,15},{4,8},{5,9},{6,10},{7,11},{8,4},{9,5},... | collective-permute-start | bytes 294920 | tf_op jit(solution)/shard_map/ppermute | solution.py:376
  97.2 16.3 %collective-permute-start.17 = (bf16[256,192]{1,0:T(8,128)(2,1)S(1)}, bf16[256,192]{1,0:T(8,128)(2,1)S(1)}, u32[]{:S(2)}, u32[]{:S(2)}) collective-permute-start(bf16[256,192]{1,0:T(8,128)(2,1)S(1)} %copy-done.17), channel_id=1, source_target_pairs={{0,3},{1,2},{2,1},{3,0},{4,7},{5,6},{6,5},{7,4},{8,11},{9,10},{10,... | collective-permute-start | bytes 294920 | tf_op jit(solution)/shard_map/ppermute | solution.py:376
  112.2 23.4 %collective-permute-start.13 = (bf16[64,768]{1,0:T(8,128)(2,1)}, bf16[64,768]{1,0:T(8,128)(2,1)}, u32[]{:S(2)}, u32[]{:S(2)}) collective-permute-start(bf16[64,768]{1,0:T(8,128)(2,1)} %get-tuple-element.87), channel_id=1, source_target_pairs={{0,8},{1,9},{2,10},{3,11},{4,12},{5,13},{6,14},{7,15},{8,0},{9,1},... | collective-permute-start | bytes 294920 | tf_op jit(solution)/shard_map/ppermute | solution.py:376
  113.5 22.1 %collective-permute-start.12 = (bf16[64,768]{1,0:T(8,128)(2,1)}, bf16[64,768]{1,0:T(8,128)(2,1)}, u32[]{:S(2)}, u32[]{:S(2)}) collective-permute-start(bf16[64,768]{1,0:T(8,128)(2,1)} %get-tuple-element.88), channel_id=1, source_target_pairs={{0,4},{1,5},{2,6},{3,7},{4,0},{5,1},{6,2},{7,3},{8,12},{9,13},{10,... | collective-permute-start | bytes 294920 | tf_op jit(solution)/shard_map/ppermute | solution.py:376
  115.8 33.1 %collective-permute-start.29 = (bf16[2,2,2,48,768]{4,3,0,1,2:T(8,128)(2,1)}, bf16[2,2,2,48,768]{4,3,0,1,2:T(8,128)(2,1)}, u32[]{:S(2)}, u32[]{:S(2)}) collective-permute-start(bf16[2,2,2,48,768]{4,3,0,1,2:T(8,128)(2,1)} %bitcast.212), channel_id=1, source_target_pairs={{0,1},{1,0},{2,3},{3,2},{4,5},{5,4},{6,7},{7,6},{8,9},{9,8},{10,11... | collective-permute-start | bytes 1769480 | tf_op jit(solution)/shard_map/ppermute | solution.py:376
  134.2 13.7 %collective-permute-start.23 = (bf16[2,192,576]{2,1,0:T(8,128)(2,1)S(1)}, bf16[2,192,576]{2,1,0:T(8,128)(2,1)S(1)}, u32[]{:S(2)}, u32[]{:S(2)}) collective-permute-start(bf16[2,192,576]{2,1,0:T(8,128)(2,1)S(1)} %dynamic-slice_bitcast_fusion.3), channel_id=1, source_target_pairs={{0,4},{1,5},{2,6},{3,7},{4,0},{5,1},{6,2},{7,3},{8,12},{9,13},{10,... | collective-permute-start | bytes 1327112 | tf_op jit(solution)/shard_map/ppermute | solution.py:376
  135.0 61.1 %collective-permute-start.35 = (bf16[2,2,2,48,3072]{4,3,0,1,2:T(8,128)(2,1)}, bf16[2,2,2,48,3072]{4,3,0,1,2:T(8,128)(2,1)}, u32[]{:S(2)}, u32[]{:S(2)}) collective-permute-start(bf16[2,2,2,48,3072]{4,3,0,1,2:T(8,128)(2,1)} %bitcast.211), channel_id=1, source_target_pairs={{0,1},{1,0},{2,3},{3,2},{4,5},{5,4},{6,7},{7,6},{8,9},{9,8},{10,11... | collective-permute-start | bytes 7077896 | tf_op jit(solution)/shard_map/ppermute | solution.py:376
  135.6 78.3 %collective-permute-start.41 = (bf16[2,2,2,192,768]{4,3,0,1,2:T(8,128)(2,1)}, bf16[2,2,2,192,768]{4,3,0,1,2:T(8,128)(2,1)}, u32[]{:S(2)}, u32[]{:S(2)}) collective-permute-start(bf16[2,2,2,192,768]{4,3,0,1,2:T(8,128)(2,1)} %bitcast.210), channel_id=1, source_target_pairs={{0,1},{1,0},{2,3},{3,2},{4,5},{5,4},{6,7},{7,6},{8,9},{9,8},{10,11... | collective-permute-start | bytes 7077896 | tf_op jit(solution)/shard_map/ppermute | solution.py:376
  135.6 28.5 %collective-permute-start.18 = (bf16[2,256,768]{2,1,0:T(8,128)(2,1)S(1)}, bf16[2,256,768]{2,1,0:T(8,128)(2,1)S(1)}, u32[]{:S(2)}, u32[]{:S(2)}) collective-permute-start(bf16[2,256,768]{2,1,0:T(8,128)(2,1)S(1)} %dynamic-slice_bitcast_fusion.1), channel_id=1, source_target_pairs={{0,1},{1,0},{2,3},{3,2},{4,5},{5,4},{6,7},{7,6},{8,9},{9,8},{10,11... | collective-permute-start | bytes 2359304 | tf_op jit(solution)/shard_map/ppermute | solution.py:376
  148.1 13.7 %collective-permute-start.24 = (bf16[192,576]{1,0:T(8,128)(2,1)S(1)}, bf16[192,576]{1,0:T(8,128)(2,1)S(1)}, u32[]{:S(2)}, u32[]{:S(2)}) collective-permute-start(bf16[192,576]{1,0:T(8,128)(2,1)S(1)} %dynamic-slice_bitcast_fusion.8), channel_id=1, source_target_pairs={{0,8},{1,9},{2,10},{3,11},{4,12},{5,13},{6,14},{7,15},{8,0},{9,1},... | collective-permute-start | bytes 663560 | tf_op jit(solution)/shard_map/ppermute | solution.py:376
  150.1 12.3 %collective-permute-start.30 = (bf16[2,2,48,768]{3,2,0,1:T(8,128)(2,1)S(1)}, bf16[2,2,48,768]{3,2,0,1:T(8,128)(2,1)S(1)}, u32[]{:S(2)}, u32[]{:S(2)}) collective-permute-start(bf16[2,2,48,768]{3,2,0,1:T(8,128)(2,1)S(1)} %dynamic-slice_bitcast_fusion.7), channel_id=1, source_target_pairs={{0,2},{1,3},{2,0},{3,1},{4,6},{5,7},{6,4},{7,5},{8,10},{9,11},{10,... | collective-permute-start | bytes 884744 | tf_op jit(solution)/shard_map/ppermute | solution.py:376
  175.2 12.8 %collective-permute-start.19 = (bf16[256,768]{1,0:T(8,128)(2,1)}, bf16[256,768]{1,0:T(8,128)(2,1)}, u32[]{:S(2)}, u32[]{:S(2)}) collective-permute-start(bf16[256,768]{1,0:T(8,128)(2,1)} %dynamic-slice_bitcast_fusion.4), channel_id=1, source_target_pairs={{0,2},{1,3},{2,0},{3,1},{4,6},{5,7},{6,4},{7,5},{8,10},{9,11},{10,... | collective-permute-start | bytes 1179656 | tf_op jit(solution)/shard_map/ppermute | solution.py:376
  198.8 25.7 %collective-permute-start.36 = (bf16[2,2,48,3072]{3,2,0,1:T(8,128)(2,1)S(1)}, bf16[2,2,48,3072]{3,2,0,1:T(8,128)(2,1)S(1)}, u32[]{:S(2)}, u32[]{:S(2)}) collective-permute-start(bf16[2,2,48,3072]{3,2,0,1:T(8,128)(2,1)S(1)} %dynamic-slice_bitcast_fusion), channel_id=1, source_target_pairs={{0,2},{1,3},{2,0},{3,1},{4,6},{5,7},{6,4},{7,5},{8,10},{9,11},{10,... | collective-permute-start | bytes 3538952 | tf_op jit(solution)/shard_map/ppermute | solution.py:376
  216.3 29.0 %collective-permute-start.42 = (bf16[2,2,2,192,384]{4,3,0,1,2:T(8,128)(2,1)S(1)}, bf16[2,2,2,192,384]{4,3,0,1,2:T(8,128)(2,1)S(1)}, u32[]{:S(2)}, u32[]{:S(2)}) collective-permute-start(bf16[2,2,2,192,384]{4,3,0,1,2:T(8,128)(2,1)S(1)} %constant_dynamic-slice_fusion), channel_id=1, source_target_pairs={{0,16},{16,0},{1,17},{17,1},{2,18},{18,2},{3,19},{19,3},{4,20},{20... | collective-permute-start | bytes 3538952 | tf_op jit(solution)/shard_map/ppermute | solution.py:376
  225.0 27.9 %collective-permute-start.37 = (bf16[2,2,48,1536]{3,2,0,1:T(8,128)(2,1)S(1)}, bf16[2,2,48,1536]{3,2,0,1:T(8,128)(2,1)S(1)}, u32[]{:S(2)}, u32[]{:S(2)}) collective-permute-start(bf16[2,2,48,1536]{3,2,0,1:T(8,128)(2,1)S(1)} %constant_dynamic-slice_fusion.3), channel_id=1, source_target_pairs={{0,16},{16,0},{1,17},{17,1},{2,18},{18,2},{3,19},{19,3},{4,20},{20... | collective-permute-start | bytes 1769480 | tf_op jit(solution)/shard_map/ppermute | solution.py:376
  255.8 11.9 %collective-permute-start.44 = (bf16[2,192,384]{2,1,0:T(8,128)(2,1)S(1)}, bf16[2,192,384]{2,1,0:T(8,128)(2,1)S(1)}, u32[]{:S(2)}, u32[]{:S(2)}) collective-permute-start(bf16[2,192,384]{2,1,0:T(8,128)(2,1)S(1)} %dynamic-slice_bitcast_fusion.5), channel_id=1, source_target_pairs={{0,4},{1,5},{2,6},{3,7},{4,0},{5,1},{6,2},{7,3},{8,12},{9,13},{10,... | collective-permute-start | bytes 884744 | tf_op jit(solution)/shard_map/ppermute | solution.py:376
  260.5 16.4 %collective-permute-start.39 = (bf16[48,1536]{1,0:T(8,128)(2,1)S(1)}, bf16[48,1536]{1,0:T(8,128)(2,1)S(1)}, u32[]{:S(2)}, u32[]{:S(2)}) collective-permute-start(bf16[48,1536]{1,0:T(8,128)(2,1)S(1)} %dynamic-slice_bitcast_fusion.10), channel_id=1, source_target_pairs={{0,8},{1,9},{2,10},{3,11},{4,12},{5,13},{6,14},{7,15},{8,0},{9,1},... | collective-permute-start | bytes 442376 | tf_op jit(solution)/shard_map/ppermute | solution.py:376
  (55 other events, 367.5 us)

commit v2 on v1

v2 whole, which is shorter than its diff:
```python
import functools

import jax
import jax.numpy as jnp
from jax import lax
from jax.experimental import pallas as pl
from jax.experimental.pallas import tpu as pltpu
from jax.sharding import PartitionSpec as P

HEAD = 64
TILE = 256
WIDE = 512
FORWARD_MIB = 24
BACKWARD_MIB = 24
WIDEN_MIB = 16
TURN_MIB = 20
OUTER_MIB = 16
big_negative = -1e30
norm_epsilon = 1e-05

f32 = jnp.float32
bf16 = jnp.bfloat16


def dot(left, right):
    return jnp.dot(left, right, preferred_element_type=f32)


def dot_nt(left, right):
    return lax.dot_general(left, right, (((1,), (1,)), ((), ())), preferred_element_type=f32)


def dot_tn(left, right):
    return lax.dot_general(left, right, (((0,), (0,)), ((), ())), preferred_element_type=f32)


def normalized(values):
    centred = values - jnp.mean(values, axis=-1, keepdims=True)
    rate = lax.rsqrt(jnp.mean(centred * centred, axis=-1, keepdims=True) + norm_epsilon)
    return centred * rate, rate


def norm_back(normal, rate, weighted):
    return rate * (
        weighted
        - jnp.mean(weighted, axis=-1, keepdims=True)
        - normal * jnp.mean(weighted * normal, axis=-1, keepdims=True)
    )


def vmem_spec():
    return pl.BlockSpec(memory_space=pltpu.VMEM)


def hbm_spec():
    return pl.BlockSpec(memory_space=pltpu.HBM)


def params(mebibytes):
    return pltpu.CompilerParams(vmem_limit_bytes=mebibytes * 1024 * 1024)


def cost(flops, moved):
    return pl.CostEstimate(flops=flops, bytes_accessed=moved, transcendentals=0)


def codes(steps):
    listed = [((), 0)]
    for bit in steps:
        listed = [(at + (b,), code | (b << bit)) for at, code in listed for b in (0, 1)]
    return listed


def forward_kernel(*refs, planes, slots, seg, heads):
    place_ref, start_ref, gain_ref, weight_ref = refs[:4]
    pieces = refs[4 : 4 + slots]
    refs = refs[4 + slots :]
    length = planes * slots * seg
    tiles = length // TILE
    first_to, joined_to = refs[:2]
    sent = refs[2 : 2 + slots]
    shares_to = refs[2 + slots : 2 + slots + tiles]
    rows_ref, first_ref, joined_ref, attention_ref = refs[2 + slots + tiles : 6 + slots + tiles]
    shares = refs[6 + slots + tiles : 6 + slots + 2 * tiles]
    ready = refs[-1]
    copies = [
        pltpu.make_async_copy(source, target, ready.at[at])
        for at, (source, target) in enumerate(
            zip((first_ref, joined_ref) + shares, (first_to, joined_to) + shares_to)
        )
    ]
    plane, slot = place_ref[0], place_ref[1]
    for u in range(slots):
        for k in range(planes):
            offset = ((plane ^ k) * slots + (slot ^ u)) * seg
            rows_ref[pl.ds(pl.multiple_of(offset, seg), seg), :] = pieces[u][k]
    width = heads * HEAD

    def project(tile, carry):
        rows = pl.ds(pl.multiple_of(tile * TILE, TILE), TILE)
        normal, _ = normalized(rows_ref[rows, :].astype(f32))
        first = (normal * gain_ref[...]).astype(bf16)
        first_ref[rows, :] = first
        joined = dot(first, weight_ref[...]).astype(bf16)
        for part in range(3):
            for h in range(heads):
                column = part * width + h * HEAD
                value = joined[:, column : column + HEAD]
                if part == 0:
                    value = value * jnp.asarray(0.125, bf16)
                joined_ref[part * heads + h, rows, :] = value
        return carry

    lax.fori_loop(0, tiles, project, 0)
    copies[0].start()
    copies[1].start()
    for q in reversed(range(tiles)):
        rows = slice(q * TILE, (q + 1) * TILE)
        reach = (q + 1) * TILE
        query_pos = q * TILE + lax.broadcasted_iota(jnp.int32, (TILE, reach), 0)
        key_pos = lax.broadcasted_iota(jnp.int32, (TILE, reach), 1)
        allowed = (key_pos <= query_pos) & (key_pos >= start_ref[rows, :])
        for h in range(heads):
            scores = dot_nt(joined_ref[h, rows, :], joined_ref[heads + h, :reach, :])
            scores = jnp.where(allowed, scores, big_negative)
            peak = jnp.max(scores, axis=-1, keepdims=True)
            raised = jnp.exp(scores - peak)
            total = jnp.sum(raised, axis=-1, keepdims=True)
            share = (raised * (1.0 / total)).astype(bf16)
            shares[q][h] = share
            attention_ref[h, rows, :] = dot(share, joined_ref[2 * heads + h, :reach, :])
        copies[2 + q].start()
    half = planes // 2
    for u in range(slots):
        for k in range(planes):
            offset = ((plane ^ k) * slots + (slot ^ u)) * seg
            rows = slice(k % half * seg, (k % half + 1) * seg)
            for h in range(heads):
                part = attention_ref[h, pl.ds(pl.multiple_of(offset, seg), seg), :]
                column = k // half * width + h * HEAD
                sent[u][rows, column : column + HEAD] = part.astype(bf16)
    for copy in copies:
        copy.wait()


def forward_call(place, start, gain, weight, pieces):
    slots = len(pieces)
    planes, seg, width = pieces[0].shape
    length = planes * slots * seg
    heads = weight.shape[1] // (3 * HEAD)
    kernel = functools.partial(forward_kernel, planes=planes, slots=slots, seg=seg, heads=heads)
    packed = jax.ShapeDtypeStruct((planes * seg // 2, 2 * heads * HEAD), bf16)
    tiled = [(heads, TILE, reach) for reach in range(TILE, length + 1, TILE)]
    outs = pl.pallas_call(
        kernel,
        out_shape=(
            pltpu.HBM((length, width), bf16),
            pltpu.HBM((3 * heads, length, HEAD), bf16),
        )
        + (packed,) * slots
        + tuple(pltpu.HBM(shape, bf16) for shape in tiled),
        in_specs=[pl.BlockSpec(memory_space=pltpu.SMEM)] + [vmem_spec()] * (3 + slots),
        out_specs=(hbm_spec(),) * 2 + (vmem_spec(),) * slots + (hbm_spec(),) * len(tiled),
        scratch_shapes=[
            pltpu.VMEM((length, width), bf16),
            pltpu.VMEM((length, width), bf16),
            pltpu.VMEM((3 * heads, length, HEAD), bf16),
            pltpu.VMEM((heads, length, HEAD), f32),
        ]
        + [pltpu.VMEM(shape, bf16) for shape in tiled]
        + [pltpu.SemaphoreType.DMA((2 + len(tiled),))],
        compiler_params=params(FORWARD_MIB * length // 1024),
        cost_estimate=cost(8 << 30, 8 << 20),
        name="attention_forward",
    )(place, start, gain, weight, *pieces)
    return outs[:2], outs[2 : 2 + slots], outs[2 + slots :]


def backward_kernel(*refs, planes, slots, seg, heads, rows_each, sides):
    place_ref, first_from, joined_from, weight_ref, gain_ref, parts_ref = refs[:6]
    pieces = refs[6 : 6 + slots]
    length = planes * slots * seg
    tiles = length // TILE
    refs = refs[6 + slots :]
    shares_from = refs[:tiles]
    joined_keep, joined_give, branch_keep, branch_give = refs[tiles : tiles + 4]
    (
        grad_ref, arrived_ref, key_ref, value_ref, total_ref, outer_ref, row_ref,
        first_ref, joined_ref,
    ) = refs[tiles + 4 : tiles + 13]
    shares = refs[tiles + 13 : 2 * tiles + 13]
    ready = refs[-1]
    copies = [
        pltpu.make_async_copy(source, target, ready.at[at])
        for at, (source, target) in enumerate(
            zip((joined_from, first_from) + shares_from, (joined_ref, first_ref) + shares)
        )
    ]
    copies[0].start()
    for q in reversed(range(tiles)):
        copies[2 + q].start()
    copies[1].start()
    plane, slot, side = place_ref[0], place_ref[1], place_ref[3]
    width = heads * HEAD
    half = planes // 2
    for u in range(slots):
        for k in range(planes):
            offset = ((plane ^ k) * slots + (slot ^ u)) * seg
            column = k // half * width
            arrived_ref[pl.ds(pl.multiple_of(offset, seg), seg), :] = pieces[u][
                k % half * seg : (k % half + 1) * seg, column : column + width
            ]
    copies[0].wait()
    for h in range(heads):
        for q in reversed(range(tiles)):
            rows = slice(q * TILE, (q + 1) * TILE)
            reach = (q + 1) * TILE
            grad = arrived_ref[rows, h * HEAD : (h + 1) * HEAD]
            if h == 0:
                copies[2 + q].wait()
            share = shares[q][h]
            product = share.astype(f32) * dot_nt(grad, joined_ref[2 * heads + h, :reach, :])
            inner = jnp.sum(product, axis=-1, keepdims=True)
            grad_scores = (product - share.astype(f32) * inner).astype(bf16)
            query_grad = dot(grad_scores, joined_ref[heads + h, :reach, :]) * 0.125
            grad_ref[rows, h * HEAD : (h + 1) * HEAD] = query_grad.astype(bf16)
            key_add = dot_tn(joined_ref[h, rows, :], grad_scores)
            value_add = dot_tn(grad, share)
            if q == tiles - 1:
                key_ref[...] = key_add
                value_ref[...] = value_add
            else:
                key_ref[:, :reach] += key_add
                value_ref[:, :reach] += value_add
        for part, source in ((1, key_ref), (2, value_ref)):
            column = part * width + h * HEAD
            for q in range(tiles):
                rows = slice(q * TILE, (q + 1) * TILE)
                grad_ref[rows, column : column + HEAD] = source[:, rows].T.astype(bf16)

    def back(tile, carry):
        rows = pl.ds(pl.multiple_of(tile * TILE, TILE), TILE)
        total_ref[rows, :] = dot_nt(grad_ref[rows, :], weight_ref[...])
        return carry

    lax.fori_loop(0, tiles, back, 0)
    for at, code in codes(range(1, bits_of(slots))):
        for out, u in ((branch_keep, code), (branch_give, code | 1)):
            for k in range(planes):
                offset = ((plane ^ k) * slots + (slot ^ u)) * seg
                out[at + (slice(k * seg, (k + 1) * seg),)] = total_ref[
                    pl.ds(pl.multiple_of(offset, seg), seg), :
                ].astype(bf16)
    model = first_ref.shape[1]
    copies[1].wait()
    for d in range(0, model, TILE):
        outer = dot_tn(first_ref[:, d : d + TILE], grad_ref[...])
        outer_ref[d : d + TILE, :] = outer
        scaled = jnp.sum(outer * weight_ref[d : d + TILE, :].astype(f32), axis=-1, keepdims=True)
        scaled = jnp.broadcast_to(scaled / gain_ref[d : d + TILE, :], (TILE, 128)).T
        row_ref[:, d : d + TILE] = scaled[:1]
    wide = 3 * width
    row_ref[:, model : model + parts_ref.shape[1]] = parts_ref[...]
    gains = model + parts_ref.shape[1]
    rows = rows_each // sides
    outs = [joined_keep, joined_give][:sides] if sides > 1 else [joined_keep]
    for other, out in enumerate(outs):
        at = 0
        for _, code in codes(range(bits_of(planes))):
            for u in range(slots):
                offset = ((plane ^ code) * slots + (slot ^ u)) * rows_each + (side ^ other) * rows
                if sides == 1:
                    offset = ((plane ^ code) * slots + (slot ^ u)) * rows_each
                out[at] = outer_ref[pl.ds(pl.multiple_of(offset, rows), rows), :].astype(bf16)
                at += 1
        out[at] = jnp.zeros((rows, wide), bf16)
        for r in range(-(-gains // wide)):
            end = min((r + 1) * wide, gains)
            out[at, r : r + 1, : end - r * wide] = row_ref[:, r * wide : end].astype(bf16)


def backward_call(
    place, first, joined, weight, gain, parts, pieces, shares, planes, sides
):
    slots = len(pieces)
    tokens = pieces[0].shape[0] * 2
    heads, length = joined.shape[0] // 3, joined.shape[1]
    width = weight.shape[0]
    rows_each = width // (planes * slots)
    kernel = functools.partial(
        backward_kernel, planes=planes, slots=slots, seg=tokens // planes, heads=heads,
        rows_each=rows_each, sides=sides,
    )
    pairs = (2,) * (bits_of(slots) - 1)
    wide = 3 * heads * HEAD
    row = -(-(width + parts.shape[1]) // 128) * 128
    blocks = jax.ShapeDtypeStruct((planes * slots + 1, rows_each // sides, wide), bf16)
    return pl.pallas_call(
        kernel,
        out_shape=(
            blocks,
            blocks,
            jax.ShapeDtypeStruct(pairs + (tokens, width), bf16),
            jax.ShapeDtypeStruct(pairs + (tokens, width), bf16),
        ),
        in_specs=[pl.BlockSpec(memory_space=pltpu.SMEM)]
        + [hbm_spec()] * 2
        + [vmem_spec()] * (3 + slots)
        + [hbm_spec()] * len(shares),
        out_specs=(vmem_spec(),) * 4,
        scratch_shapes=[
            pltpu.VMEM((length, wide), bf16),
            pltpu.VMEM((length, heads * HEAD), bf16),
            pltpu.VMEM((HEAD, length), f32),
            pltpu.VMEM((HEAD, length), f32),
            pltpu.VMEM((length, width), f32),
            pltpu.VMEM((width, wide), f32),
            pltpu.VMEM((1, row), f32),
            pltpu.VMEM(first.shape, bf16),
            pltpu.VMEM(joined.shape, bf16),
        ]
        + [pltpu.VMEM(share.shape, bf16) for share in shares]
        + [pltpu.SemaphoreType.DMA((2 + len(shares),))],
        compiler_params=params(BACKWARD_MIB * length // 1024),
        cost_estimate=cost(10 << 30, 10 << 20),
        name="attention_backward",
    )(place, first, joined, weight, gain, parts, *pieces, *shares)


def widen_kernel(*refs, slots, planes, groups, width, spread):
    place_ref = refs[0]
    pieces = refs[1 : 1 + slots]
    blocks = refs[1 + slots : 1 + slots + planes]
    refs = refs[1 + slots + planes :]
    (
        valid_ref, input_ref, mixed_gain_ref, second_gain_ref, hidden_gain_ref, merge_ref, expand_from,
    ) = refs[:7]
    (
        mixed_ref, middle_ref, second_ref, hidden_ref, normal_ref, slope_ref, held_ref,
        mixed_rate_ref, hidden_rate_ref, branch_ref,
    ) = refs[7:17]
    expand_ref, gelu_ref, ready = refs[17:]
    steps = spread // WIDE

    def copy(step):
        at = pl.ds(step * WIDE, WIDE)
        return pltpu.make_async_copy(
            expand_from.at[:, at], expand_ref.at[:, at], ready.at[step]
        )

    for step in range(steps):
        copy(step).start()
    slot = place_ref[1]
    piece = width // groups
    tokens = input_ref.shape[0]
    half = tokens // 2
    for u in range(slots):
        for side in range(2):
            held_ref[slot ^ u, side * half : (side + 1) * half, :] = pieces[u][
                :, side * piece : (side + 1) * piece
            ].astype(f32)
    mean = sum(jnp.sum(held_ref[g], axis=-1, keepdims=True) for g in range(groups)) * (1.0 / width)
    square = 0.0
    for g in range(groups):
        centred = held_ref[g] - mean
        held_ref[g] = centred
        square = square + jnp.sum(centred * centred, axis=-1, keepdims=True)
    mixed_rate = lax.rsqrt(square * (1.0 / width) + norm_epsilon)
    mixed_rate_ref[...] = mixed_rate
    middle = input_ref[...].astype(f32)
    for g in range(groups):
        normal = held_ref[g] * mixed_rate
        held_ref[g] = normal
        mixed = (normal * mixed_gain_ref[g]).astype(bf16)
        mixed_ref[:, g * piece : (g + 1) * piece] = mixed
        middle = middle + dot(mixed, merge_ref[g * piece : (g + 1) * piece, :])
    middle_ref[...] = middle
    seg = tokens // planes
    for k in range(planes):
        at = slice(k * seg, (k + 1) * seg)
        branch_ref[at, :] = (blocks[k][...].astype(f32) * valid_ref[at, :]).astype(bf16)
    second_normal, _ = normalized(middle)
    second = (second_normal * second_gain_ref[...]).astype(bf16)
    second_ref[...] = second
    total = jnp.zeros((tokens, 1), f32)
    for step in range(steps):
        copy(step).wait()
        at = slice(step * WIDE, (step + 1) * WIDE)
        value = dot(second, expand_ref[:, at])
        share = 0.5 * (1.0 + lax.erf(value * 0.7071067811865476))
        gelu = value * share
        gelu_ref[:, at] = gelu
        slope = share + value * (0.3989422804014327 * jnp.exp(-0.5 * value * value))
        slope_ref[:, at] = slope.astype(bf16)
        total = total + jnp.sum(gelu, axis=-1, keepdims=True)
    mean = total * (1.0 / spread)
    total = jnp.zeros((tokens, 1), f32)
    for step in range(steps):
        centred = gelu_ref[:, step * WIDE : (step + 1) * WIDE] - mean
        total = total + jnp.sum(centred * centred, axis=-1, keepdims=True)
    rate = lax.rsqrt(total * (1.0 / spread) + norm_epsilon)
    hidden_rate_ref[...] = rate
    for step in range(steps):
        at = slice(step * WIDE, (step + 1) * WIDE)
        normal = (gelu_ref[:, at] - mean) * rate
        normal_ref[:, at] = normal.astype(bf16)
        hidden_ref[:, at] = (normal * hidden_gain_ref[:, at]).astype(bf16)


def widen_call(
    place, pieces, blocks, valid, inputs, mixed_gain, second_gain, hidden_gain, merge, expand
):
    slots = len(pieces)
    tokens = inputs.shape[0]
    piece = pieces[0].shape[1] // 2
    width, spread = expand.shape
    groups = width // piece

    def low(*shape):
        return jax.ShapeDtypeStruct(shape, bf16)

    def full(*shape):
        return jax.ShapeDtypeStruct(shape, f32)

    return pl.pallas_call(
        functools.partial(
            widen_kernel, slots=slots, planes=len(blocks), groups=groups, width=width,
            spread=spread,
        ),
        out_shape=(
            low(tokens, width),
            full(tokens, width),
            low(tokens, width),
            low(tokens, spread),
            low(tokens, spread),
            low(tokens, spread),
            full(slots, tokens, piece),
            full(tokens, 1),
            full(tokens, 1),
            low(tokens, width),
        ),
        in_specs=[pl.BlockSpec(memory_space=pltpu.SMEM)]
        + [vmem_spec()] * (6 + slots + len(blocks))
        + [hbm_spec()],
        out_specs=(vmem_spec(),) * 10,
        scratch_shapes=[
            pltpu.VMEM((width, spread), bf16),
            pltpu.VMEM((tokens, spread), f32),
            pltpu.SemaphoreType.DMA((spread // WIDE,)),
        ],
        compiler_params=params(WIDEN_MIB),
        cost_estimate=cost(6 << 30, 6 << 20),
        name="widen",
    )(
        place, *pieces, *blocks, valid, inputs, mixed_gain.reshape(groups, 1, piece),
        second_gain.reshape(1, width), hidden_gain.reshape(1, spread), merge, expand,
    )


def turn_kernel(*refs, slots, planes, groups, width, spread):
    (
        place_ref, branch_ref, hidden_ref, normal_ref, slope_ref, middle_ref, held_ref,
        mixed_rate_ref, hidden_rate_ref,
        mixed_gain_ref, second_gain_ref, hidden_gain_ref, merge_ref, shrink_from, expand_from,
    ) = refs[:15]
    expanded_ref, mix_ref, grad_ref, parts_ref = refs[15:19]
    away = refs[19 : 19 + slots]
    results = refs[19 + slots : 19 + slots + planes]
    shrink_ref, expand_ref, weighted_ref, sent_ref, ready = refs[19 + slots + planes :]
    steps = spread // WIDE

    def copy_shrink(step):
        at = pl.ds(step * WIDE, WIDE)
        return pltpu.make_async_copy(shrink_from.at[at], shrink_ref.at[at], ready.at[step])

    def copy_expand(step):
        at = pl.ds(step * WIDE, WIDE)
        return pltpu.make_async_copy(
            expand_from.at[:, at], expand_ref.at[:, at], ready.at[steps + step]
        )

    for step in range(steps):
        copy_shrink(step).start()
    for step in range(steps):
        copy_expand(step).start()
    slot = place_ref[1]
    piece = width // groups
    tokens = middle_ref.shape[0]
    half = tokens // 2
    branch = branch_ref[...]
    result = middle_ref[...]
    weighted_sum = jnp.zeros((tokens, 1), f32)
    inner_sum = jnp.zeros((tokens, 1), f32)
    for step in range(steps):
        copy_shrink(step).wait()
        at = slice(step * WIDE, (step + 1) * WIDE)
        result = result + dot(hidden_ref[:, at], shrink_ref[at, :])
        grad_hidden = dot_nt(branch, shrink_ref[at, :])
        normal = normal_ref[:, at].astype(f32)
        start = 2 * width + step * WIDE
        parts_ref[:, start : start + WIDE] = jnp.sum(grad_hidden * normal, axis=0, keepdims=True)
        weighted = grad_hidden * hidden_gain_ref[:, at]
        weighted_ref[:, at] = weighted
        weighted_sum = weighted_sum + jnp.sum(weighted, axis=-1, keepdims=True)
        inner_sum = inner_sum + jnp.sum(weighted * normal, axis=-1, keepdims=True)
    seg = tokens // planes
    for k in range(planes):
        results[k][...] = result[k * seg : (k + 1) * seg, :].astype(bf16)
    weighted_mean = weighted_sum * (1.0 / spread)
    inner_mean = inner_sum * (1.0 / spread)
    rate = hidden_rate_ref[...]
    grad_second = jnp.zeros((tokens, width), f32)
    for step in range(steps):
        copy_expand(step).wait()
        at = slice(step * WIDE, (step + 1) * WIDE)
        grad = rate * (
            weighted_ref[:, at] - weighted_mean - normal_ref[:, at].astype(f32) * inner_mean
        )
        expanded = (grad * slope_ref[:, at].astype(f32)).astype(bf16)
        expanded_ref[:, at] = expanded
        grad_second = grad_second + dot_nt(expanded, expand_ref[:, at])
    second_normal, second_rate = normalized(middle_ref[...])
    parts_ref[:, width : 2 * width] = jnp.sum(grad_second * second_normal, axis=0, keepdims=True)
    grad_middle = branch.astype(f32) + norm_back(
        second_normal, second_rate, grad_second * second_gain_ref[...]
    )
    grad_ref[...] = grad_middle
    mix = grad_middle.astype(bf16)
    mix_ref[...] = mix
    grads = []
    weighted_sum = 0.0
    inner_sum = 0.0
    for g in range(groups):
        grad_mixed = dot_nt(mix, merge_ref[g * piece : (g + 1) * piece, :])
        parts_ref[:, g * piece : (g + 1) * piece] = jnp.sum(
            grad_mixed * held_ref[g], axis=0, keepdims=True
        )
        weighted = grad_mixed * mixed_gain_ref[g]
        grads.append(weighted)
        weighted_sum = weighted_sum + jnp.sum(weighted, axis=-1, keepdims=True)
        inner_sum = inner_sum + jnp.sum(weighted * held_ref[g], axis=-1, keepdims=True)
    weighted_mean = weighted_sum * (1.0 / width)
    inner_mean = inner_sum * (1.0 / width)
    for g in range(slots):
        if g < groups:
            sent_ref[g] = mixed_rate_ref[...] * (
                grads[g] - weighted_mean - held_ref[g] * inner_mean
            )
        else:
            sent_ref[g] = jnp.zeros(sent_ref.shape[1:], f32)
    for u in range(slots):
        for side in range(2):
            away[u][:, side * piece : (side + 1) * piece] = sent_ref[
                slot ^ u, side * half : (side + 1) * half, :
            ].astype(bf16)


def turn_call(
    place, branch, hidden, normal, slope, middle, held, mixed_rate, hidden_rate,
    mixed_gain, second_gain, hidden_gain, merge, shrink, expand, planes,
):
    slots, tokens, piece = held.shape
    width, spread = expand.shape
    groups = width // piece

    def low(*shape):
        return jax.ShapeDtypeStruct(shape, bf16)

    def full(*shape):
        return jax.ShapeDtypeStruct(shape, f32)

    outs = pl.pallas_call(
        functools.partial(
            turn_kernel, slots=slots, planes=planes, groups=groups, width=width, spread=spread
        ),
        out_shape=(
            low(tokens, spread),
            low(tokens, width),
            full(tokens, width),
            full(1, 2 * width + spread),
        )
        + (low(tokens // 2, 2 * piece),) * slots
        + (low(tokens // planes, width),) * planes,
        in_specs=[pl.BlockSpec(memory_space=pltpu.SMEM)] + [vmem_spec()] * 12 + [hbm_spec()] * 2,
        out_specs=(vmem_spec(),) * (4 + slots + planes),
        scratch_shapes=[
            pltpu.VMEM((spread, width), bf16),
            pltpu.VMEM((width, spread), bf16),
            pltpu.VMEM((tokens, spread), f32),
            pltpu.VMEM((slots, tokens, piece), f32),
            pltpu.SemaphoreType.DMA((2 * spread // WIDE,)),
        ],
        compiler_params=params(TURN_MIB),
        cost_estimate=cost(9 << 30, 8 << 20),
        name="turn",
    )(
        place, branch, hidden, normal, slope, middle, held, mixed_rate, hidden_rate,
        mixed_gain.reshape(groups, 1, piece), second_gain.reshape(1, width),
        hidden_gain.reshape(1, spread), merge, shrink, expand,
    )
    return outs[:4], outs[4 : 4 + slots], outs[4 + slots :]


def cut_out(keep_ref, give_ref, total_ref, place_ref, bands, steps, rows_each):
    rank, side = place_ref[2], place_ref[3]
    for at, code in codes(steps):
        other, far = code & 1, code >> 1
        for out, core in ((keep_ref, 0), (give_ref, 1)):
            offset = pl.multiple_of((rank ^ (far << 1 | core)) * rows_each, rows_each)
            start = 0
            for first, wide in bands:
                column = pl.multiple_of(first + (side ^ other) * wide, 128)
                out[at + (slice(None), slice(start, start + wide))] = total_ref[
                    pl.ds(offset, rows_each), pl.ds(column, wide)
                ].astype(bf16)
                start += wide


def shrink_kernel(
    place_ref, hidden_ref, branch_ref, keep_ref, give_ref, total_ref, *, steps, rows_each
):
    spread, width = total_ref.shape
    for at in range(0, spread, WIDE):
        total_ref[at : at + WIDE, :] = dot_tn(hidden_ref[:, at : at + WIDE], branch_ref[...])
    cut_out(
        keep_ref, give_ref, total_ref, place_ref, ((0, width // 2),), steps, rows_each
    )


def expand_kernel(
    place_ref, second_ref, expanded_ref, mixed_ref, mix_ref, keep_ref, give_ref, total_ref,
    *, steps, rows_each,
):
    width, spread = second_ref.shape[1], expanded_ref.shape[1]
    turned = second_ref[...].T
    for at in range(0, spread, WIDE):
        total_ref[:, at : at + WIDE] = dot(turned, expanded_ref[:, at : at + WIDE])
    total_ref[:, spread:] = dot(mixed_ref[...].T, mix_ref[...])
    cut_out(
        keep_ref, give_ref, total_ref, place_ref,
        ((0, spread // 2), (spread, width // 2)), steps, rows_each,
    )


def outer_call(kernel, place, operands, rows, columns, steps, size, name):
    rows_each = rows // size
    out = jax.ShapeDtypeStruct((2,) * len(steps) + (rows_each, columns // 2), bf16)
    return pl.pallas_call(
        functools.partial(kernel, steps=steps, rows_each=rows_each),
        out_shape=(out, out),
        in_specs=[pl.BlockSpec(memory_space=pltpu.SMEM)] + [vmem_spec()] * len(operands),
        out_specs=(vmem_spec(),) * 2,
        scratch_shapes=[pltpu.VMEM((rows, columns), f32)],
        compiler_params=params(OUTER_MIB),
        cost_estimate=cost(2 << 30, 10 << 20),
        name=name,
    )(place, *operands)


def settle_kernel(place_ref, *refs):
    out = refs[-1]
    for k, ref in enumerate(refs[:-1]):
        out[place_ref[0] ^ k] = ref[...]


def settle_call(place, blocks):
    return pl.pallas_call(
        settle_kernel,
        out_shape=jax.ShapeDtypeStruct((len(blocks),) + blocks[0].shape, blocks[0].dtype),
        in_specs=[pl.BlockSpec(memory_space=pltpu.SMEM)] + [vmem_spec()] * len(blocks),
        out_specs=vmem_spec(),
        compiler_params=params(8),
        name="settle",
    )(place, *blocks)


def heads_kernel(place_ref, *refs, groups, gains):
    joined_out, gains_out, held_ref = refs[-3:]
    pieces = refs[:-3]
    sums = []
    for u, ref in enumerate(pieces):
        held_ref[place_ref[1] ^ u] = ref[0].astype(f32)
        sums.append(ref[1].astype(f32))
    piece = pieces[0].shape[2] // 3
    for part in range(3):
        for g in range(groups):
            start = (part * groups + g) * piece
            joined_out[:, start : start + piece] = held_ref[
                g, :, part * piece : (part + 1) * piece
            ].astype(joined_out.dtype)
    while len(sums) > 1:
        sums = [sums[i] + sums[i + 1] for i in range(0, len(sums), 2)]
    wide = 3 * piece
    for r in range(-(-gains // wide)):
        end = min((r + 1) * wide, gains)
        gains_out[:, r * wide : end] = sums[0][r : r + 1, : end - r * wide]


def heads_call(place, blocks, width, gains, dtype):
    _, rows, wide = blocks[0].shape
    return pl.pallas_call(
        functools.partial(heads_kernel, groups=3 * width // wide, gains=gains),
        out_shape=(
            jax.ShapeDtypeStruct((rows, 3 * width), dtype),
            jax.ShapeDtypeStruct((1, gains), f32),
        ),
        in_specs=[pl.BlockSpec(memory_space=pltpu.SMEM)] + [vmem_spec()] * len(blocks),
        out_specs=(vmem_spec(),) * 2,
        scratch_shapes=[pltpu.VMEM((len(blocks), rows, wide), f32)],
        compiler_params=params(8),
        name="heads_side_by_side",
    )(place, *blocks)


def input_kernel(*refs, planes, parts):
    input_ref, grad_ref, gain_ref = refs[:3]
    grad = sum(ref[at].astype(f32) for ref, at in zip(refs[3 : 3 + len(parts)], parts))
    outs = refs[3 + len(parts) :]
    normal, rate = normalized(input_ref[...].astype(f32))
    value = grad_ref[...] + norm_back(normal, rate, grad * gain_ref[...])
    seg = value.shape[0] // planes
    for k in range(planes):
        outs[k][...] = value[k * seg : (k + 1) * seg, :].astype(bf16)


def input_call(inputs, grad_middle, gain, held, parts, planes):
    tokens, width = inputs.shape
    return pl.pallas_call(
        functools.partial(input_kernel, planes=planes, parts=parts),
        out_shape=(jax.ShapeDtypeStruct((tokens // planes, width), bf16),) * planes,
        in_specs=[vmem_spec()] * (3 + len(held)),
        out_specs=(vmem_spec(),) * planes,
        compiler_params=params(16),
        name="input_back",
    )(inputs, grad_middle, gain.reshape(1, width), *held)


def swap(value, axis, bits):
    size = lax.axis_size(axis)
    return lax.ppermute(value, axis, [(i, i ^ bits) for i in range(size)])


def pick(value, index, axis=0):
    return lax.dynamic_index_in_dim(value, index, axis, keepdims=False)


def in_hbm(*values):
    return [pltpu.with_memory_space_constraint(value, pltpu.HBM) for value in values]


def bits_of(size):
    return size.bit_length() - 1


def total(values):
    return sum(v.astype(f32) for v in values)


class Halves:
    def __init__(self, bands):
        self.entries = []
        self.bands = bands
        self.chosen = {}

    def hold(self, array, names):
        self.entries.append((array, names))

    def summed(self, choice=()):
        chosen = dict(self.chosen)
        chosen.update(choice)
        values = []
        for array, names in self.entries:
            at = tuple(
                chosen[n] if n in chosen
                else self.bands.get(n, slice(None)) if len(names) == len(self.entries[0][1])
                else slice(None)
                for n in names
            )
            values.append(array[at].astype(f32))
        return sum(values)

    def send(self, name):
        return self.summed({name: 1}).astype(bf16)

    def receive(self, name, array):
        self.chosen[name] = 0
        self.hold(array, [n for n in self.entries[0][1] if n not in self.chosen])


def per_device(
    layer_input, cotangent, doc_lengths, joined_weight, merge_weight, expand_weight,
    shrink_weight, first_gain, mixed_gain, second_gain, hidden_gain,
):
    _, planes, seg, width = layer_input.shape
    size = lax.axis_size("blk")
    slots = size // planes
    batches = lax.axis_size("batch")
    rank = lax.axis_index("blk")
    group_rank = lax.axis_index("batch")
    plane = rank // slots
    slot = rank % slots
    head_count = width // HEAD
    heads = -(-head_count // slots)
    groups = head_count // heads
    piece = heads * HEAD
    tokens = planes * seg
    length = slots * tokens
    side = group_rank % 2
    place = jnp.stack([plane, slot, rank, side]).astype(jnp.int32)

    def to_planes(blocks):
        return [pick(blocks, plane)] + [
            swap(pick(blocks, plane ^ k), "blk", k * slots) for k in range(1, planes)
        ]

    def all_slots(value):
        held = {0: value}
        for bit in reversed(range(bits_of(slots))):
            held.update({u | 1 << bit: swap(v, "blk", 1 << bit) for u, v in held.items()})
        return [held[u] for u in range(slots)]

    def over_slots(blocks):
        return [blocks[0]] + [swap(blocks[u], "blk", u) for u in range(1, slots)]

    spread = expand_weight.shape[1]
    expand_weight, shrink_weight = in_hbm(expand_weight, shrink_weight)
    first_arrived = to_planes(layer_input[0])
    ends = jnp.cumsum(pick(doc_lengths[0], plane), axis=-1)
    positions = jnp.arange(length, dtype=jnp.int32)
    reached = ends[None, :] <= positions[:, None]
    start = jnp.max(jnp.where(reached, ends[None, :], 0), axis=-1, keepdims=True)
    own_start = jnp.minimum(slot, groups - 1) * piece
    own_weight = jnp.concatenate(
        [
            lax.dynamic_slice_in_dim(joined_weight, part * width + own_start, piece, 1)
            for part in range(3)
        ],
        axis=1,
    )
    own_pos = (
        (plane ^ jnp.arange(planes, dtype=jnp.int32))[:, None] * (slots * seg)
        + slot * seg
        + jnp.arange(seg, dtype=jnp.int32)[None, :]
    ).reshape(tokens, 1)
    valid = (own_pos < ends[-1]).astype(f32)
    first_arrived, start, own_weight, valid, cotangent = lax.optimization_barrier(
        (first_arrived, start, own_weight, valid, cotangent)
    )
    arrived = jnp.stack(first_arrived)
    cotangent_blocks = to_planes(cotangent[0])
    pieces = all_slots(arrived)
    (first, joined), sent, shares = forward_call(
        place, start, first_gain.reshape(1, width), own_weight, pieces
    )
    sent, cotangent_blocks = lax.optimization_barrier((sent, cotangent_blocks))
    input_rows = arrived.reshape(tokens, width)
    (
        mixed, middle, second, hidden, normal, slope, held, mixed_rate, hidden_rate, branch,
    ) = widen_call(
        place, over_slots(sent), cotangent_blocks, valid, input_rows, mixed_gain, second_gain,
        hidden_gain, merge_weight, expand_weight,
    )

    row_bits = list(range(1, bits_of(slots)))
    plane_bits = list(range(bits_of(slots), bits_of(size)))
    names = ["side"] + row_bits + plane_bits + ["rows", "columns"]
    steps = [0] + row_bits + plane_bits

    def cross(name, value):
        return swap(value, "batch", 1) if name == "side" else swap(value, "blk", 1 << name)

    def chains(axis, cut, keep, arrived):
        both = []
        for band in (slice(0, cut), slice(cut, None)):
            chain = Halves({axis: band})
            chain.hold(keep, names)
            chain.hold(arrived, names)
            both.append(chain)
        return both

    shrink_keep, shrink_give = outer_call(
        shrink_kernel, place, [hidden, branch], spread, width, steps, size, "shrink_outer"
    )
    shrink_got = swap(shrink_give, "blk", 1)
    (expanded, mix, grad_middle, parts), away, results = turn_call(
        place, branch, hidden, normal, slope, middle, held, mixed_rate, hidden_rate,
        mixed_gain, second_gain, hidden_gain, merge_weight, shrink_weight, expand_weight, planes,
    )
    orders = (["side"] + row_bits, row_bits + ["side"])
    stages = len(orders[0])

    def depart(pair, at):
        return [
            cross(order[at], chain.send(order[at])) for chain, order in zip(pair, orders)
        ]

    def arrive(pair, at, values):
        for chain, order, value in zip(pair, orders, values):
            chain.receive(order[at], value)

    def plane_depart(pair, bit, axis):
        return cross(bit, jnp.concatenate([chain.send(bit) for chain in pair], axis=axis))

    def plane_arrive(pair, bit, axis, both):
        if axis == -2:
            cut = pair[0].bands["rows"].stop
            values = both[..., :cut, :], both[..., cut:, :]
        else:
            cut = pair[0].bands["columns"].stop
            values = both[..., :cut], both[..., cut:]
        for chain, value in zip(pair, values):
            chain.receive(bit, value)

    def closed(pair, axis):
        value = jnp.concatenate([chain.summed() for chain in pair], axis=axis).astype(bf16)
        for bit in range(1, bits_of(batches)):
            value = total([value, swap(value, "batch", 1 << bit)]).astype(bf16)
        return value

    def both_sides(value):
        other = swap(value, "batch", 1)
        return jnp.where(side == 0, value, other), jnp.where(side == 0, other, value)

    returned = over_slots(away)
    expand_keep, expand_give = outer_call(
        expand_kernel, place, [second, expanded, mixed, mix], width, spread + width, steps, size,
        "expand_outer",
    )
    returned, expand_give, shrink_got, results = lax.optimization_barrier(
        (returned, expand_give, shrink_got, results)
    )
    shrink_chains = chains("rows", spread // size // 2, shrink_keep, shrink_got)
    expand_got = swap(expand_give, "blk", 1)
    shrink_sent = depart(shrink_chains, 0)
    result_blocks = [results[0]] + [
        swap(results[k], "blk", k * slots) for k in range(1, planes)
    ]
    rows_each = width // size
    joined_sides = 2 if batches > 1 and rows_each % 16 == 0 else 1
    joined_keep, joined_give, branch_keep, branch_give = backward_call(
        place, *in_hbm(first, joined), own_weight, first_gain.reshape(width, 1), parts,
        returned, in_hbm(*shares), planes, joined_sides,
    )
    (
        joined_give, branch_give, shrink_sent, expand_got, result_blocks,
    ) = lax.optimization_barrier(
        (joined_give, branch_give, shrink_sent, expand_got, result_blocks)
    )
    expand_chains = chains(
        "columns", ((spread + width) // 4 + 127) // 128 * 128, expand_keep, expand_got
    )
    arrive(shrink_chains, 0, shrink_sent)

    joined_held, batch_bits = [joined_keep], list(range(bits_of(batches)))
    branch_got = swap(branch_give, "blk", 1)
    for at in range(1, stages):
        shrink_sent = depart(shrink_chains, at)
        if at < stages - 1:
            arrive(shrink_chains, at, shrink_sent)
    expand_sent = depart(expand_chains, 0)
    if joined_sides > 1:
        joined_held.append(swap(joined_give, "batch", 1))
        batch_bits = batch_bits[1:]
    shrink_sent, joined_held, branch_got = lax.optimization_barrier(
        (shrink_sent, joined_held, branch_got)
    )
    arrive(shrink_chains, stages - 1, shrink_sent)

    blocks = planes * slots
    gains = sum(v[blocks].astype(f32) for v in joined_held)
    joined_sum = [v[:blocks] for v in joined_held]

    def joined_depart(bit):
        half = joined_sum[0].shape[0] // 2
        give = sum(v[half:].astype(f32) for v in joined_sum).astype(bf16)
        return swap(jnp.concatenate([give, gains.astype(bf16)[None]]), "blk", 1 << bit)

    def joined_arrive(got):
        half = got.shape[0] - 1
        return (
            [v[:half] for v in joined_sum] + [got[:half]],
            gains.astype(bf16).astype(f32) + got[half].astype(f32),
        )

    joined_got = joined_depart(plane_bits[0])
    shrink_both = plane_depart(shrink_chains, plane_bits[0], -2)
    branch_held, prefixes = [branch_keep, branch_got], [(), ()]
    for bit in row_bits:
        give = sum(v[p + (1,)].astype(f32) for v, p in zip(branch_held, prefixes)).astype(bf16)
        prefixes = [p + (0,) for p in prefixes] + [()]
        branch_held.append(swap(give, "blk", 1 << bit))
    joined_got, shrink_both, expand_sent, branch_held = lax.optimization_barrier(
        (joined_got, shrink_both, expand_sent, branch_held)
    )
    joined_sum, gains = joined_arrive(joined_got)
    plane_arrive(shrink_chains, plane_bits[0], -2, shrink_both)
    arrive(expand_chains, 0, expand_sent)

    for at in range(1, stages):
        expand_sent = depart(expand_chains, at)
        if at < stages - 1:
            arrive(expand_chains, at, expand_sent)
    input_blocks = input_call(
        input_rows, grad_middle, first_gain, branch_held, prefixes, planes
    )
    for bit in plane_bits[1:]:
        joined_sum, gains = joined_arrive(joined_depart(bit))
        plane_arrive(shrink_chains, bit, -2, plane_depart(shrink_chains, bit, -2))
    shrink_last, joined_last = closed(shrink_chains, -2), jnp.concatenate(
        [sum(v.astype(f32) for v in joined_sum), gains[None]]
    ).astype(bf16)
    expand_sent, shrink_last, joined_last = lax.optimization_barrier(
        (expand_sent, shrink_last, joined_last)
    )
    arrive(expand_chains, stages - 1, expand_sent)

    expand_both = plane_depart(expand_chains, plane_bits[0], -1)
    input_blocks = [input_blocks[0]] + [
        swap(input_blocks[k], "blk", k * slots) for k in range(1, planes)
    ]
    for bit in batch_bits:
        joined_last = total([joined_last, swap(joined_last, "batch", 1 << bit)]).astype(bf16)
    shrink_lower, shrink_upper = both_sides(shrink_last)
    shrink_grad = jnp.concatenate([shrink_lower, shrink_upper], axis=1).astype(f32)
    joined_half, gain_row = heads_call(
        place,
        [jnp.stack([joined_last[0], joined_last[slots]])]
        + [
            swap(jnp.stack([joined_last[u], joined_last[slots]]), "blk", u)
            for u in range(1, slots)
        ],
        width, 3 * width + spread, f32 if joined_sides == 1 else bf16,
    )
    expand_both, input_blocks, joined_half, shrink_grad = lax.optimization_barrier(
        (expand_both, input_blocks, joined_half, shrink_grad)
    )
    plane_arrive(expand_chains, plane_bits[0], -1, expand_both)
    for bit in plane_bits[1:]:
        plane_arrive(expand_chains, bit, -1, plane_depart(expand_chains, bit, -1))
    expand_lower, expand_upper = both_sides(closed(expand_chains, -1))
    cut = spread // 2
    expand_grad = jnp.concatenate([expand_lower[:, :cut], expand_upper[:, :cut]], axis=1)
    merge_grad = jnp.concatenate([expand_lower[:, cut:], expand_upper[:, cut:]], axis=1)
    if joined_sides == 1:
        joined_grad = joined_half
    else:
        joined_grad = jnp.concatenate(both_sides(joined_half), axis=0).astype(f32)
    layer_result = settle_call(place, result_blocks).reshape(layer_input.shape)
    input_grad = settle_call(place, input_blocks).reshape(layer_input.shape)
    gain_row = gain_row[0]
    return (
        layer_result, input_grad, joined_grad, merge_grad.astype(f32), expand_grad.astype(f32),
        shrink_grad, gain_row[:width], gain_row[width : 2 * width],
        gain_row[2 * width : 3 * width], gain_row[3 * width :],
    )


def solution(mesh):
    rows = P("batch", None, "blk", None)
    return jax.shard_map(
        per_device,
        mesh=mesh,
        in_specs=(rows, rows, P("batch", None, None)) + (P(),) * 8,
        out_specs=(rows, rows) + (P("blk", None),) * 4 + (P(),) * 4,
        check_vma=False,
    )
```

time: 286 us -> 216 us (0.76)
  waiting for transfers between devices: 114 us -> 73.4 us
  local copies, waits for them, and re-layouts: 24.4 us -> 10.6 us
  matrix products: 13.3 us -> 0 us
  starting transfers between devices: 59.1 us -> 46.1 us
  Pallas kernels: 48.2 us -> 55.9 us
    ppermute x57 -> x46, waiting for transfers between devices: 114 us -> 73.4 us  [swap(): return lax.ppermute(value, axis, [(i, i ^ bits) for i in range(size)])]
    dot_general x7 -> x0, matrix products: 13.3 us -> none  [dot_tn(): lax.dot_general(left, right, (((0,), (0,)), ((), ())), preferred_element_...]
    ppermute x57 -> x46, starting transfers between devices: 59.1 us -> 46.1 us  [swap(): return lax.ppermute(value, axis, [(i, i ^ bits) for i in range(size)])]
    dynamic_slice x21 -> x0, local copies, waits for them, and re-layouts: 12.4 us -> none  [the longest x18 12.2 us: pick(): return lax.dynamic_index_in_dim(value, index, axis, keepdims=False)]
    pallas_call x3 -> x10, Pallas kernels: 48.2 us -> 55.9 us  [the longest x1 13.9 us: forward_call(): pl.pallas_call(kernel, out_shape=(pltpu.HBM((length, width), bf16), pltpu...]
    convert_element_type x24 -> x22, other arithmetic: 11.5 us -> 17.1 us  [the longest x13 10.9 us: send(): return self.summed({name: 1}).astype(bf16)]
    convert_element_type x4 -> x0, local copies, waits for them, and re-layouts: 5.52 us -> none  [the longest x3 3.87 us: per_device(): joined_grad = value.reshape(width // size, 3 * width).astype(f32)]
    unnamed x46 -> x72, local copies, waits for them, and re-layouts: 0.12 us -> 4.98 us
  transfers between devices with their start and end apart: 57 -> 46, of which waited for: 30 -> 19; matrix products, arithmetic and copies ran while one was open for 18% -> 10% of each run, Pallas kernels for 4% -> 22%
where the time goes in v2:
time: 216 us; the launch traced here: 212 us
  waiting for transfers between devices  73.4 us (34%)
  Pallas kernels  55.9 us (26%)
  starting transfers between devices  46.1 us (21%)
  other arithmetic  24.7 us (11%)
  local copies, waits for them, and re-layouts  10.6 us (5%)
    ppermute x46, waiting for transfers between devices, swap(): return lax.ppermute(value, axis, [(i, i ^ bits) for i in range(size)])  73.4 us
    ppermute x46, starting transfers between devices, swap(): return lax.ppermute(value, axis, [(i, i ^ bits) for i in range(size)])  46.1 us
    pallas_call x1, Pallas kernels, forward_call(): pl.pallas_call(kernel, out_shape=(pltpu.HBM((length, width), bf16), pltpu...  13.9 us
    pallas_call x1, Pallas kernels, backward_call(): pl.pallas_call(kernel, out_shape=(blocks, blocks, jax.ShapeDtypeStruct(pa...  13.8 us
    convert_element_type x13, other arithmetic, send(): return self.summed({name: 1}).astype(bf16)  10.9 us
    pallas_call x1, Pallas kernels, turn_call(): pl.pallas_call(functools.partial(turn_kernel, slots=slots, planes=planes,...  10.5 us
    pallas_call x1, Pallas kernels, widen_call(): pl.pallas_call(functools.partial(widen_kernel, slots=slots, planes=len(bl...  7.39 us
    pallas_call x2, Pallas kernels, outer_call(): pl.pallas_call(functools.partial(kernel, steps=steps, rows_each=rows_each...  5.34 us
  transfers between devices with their start and end apart: 46, of which 19 were waited for; matrix products, arithmetic and copies ran while one was open for 10% of the time, Pallas kernels for 22%

profile of v2, /device:TPU:0, one launch (start us, length us, event | category | flops | bytes accessed | tf_op | source)
XLA Modules:
  0.0 212.5 jit_solution(4465020885917585541)
XLA Ops:
  1.8 3.1 %collective-permute-start = (bf16[64,768]{1,0:T(8,128)(2,1)S(1)}, bf16[64,768]{1,0:T(8,128)(2,1)S(1)}, u32[]{:S(2)}, u32[]{:S(2)}) collective-permute-start(bf16[64,768]{1,0:T(8,128)(2,1)S(1)} %get-tuple-element.237), channel_id=1, source_target_pairs={{0,4},{1,5},{2,6},{3,7},{4,0},{5,1},{6,2},{7,3},{8,12},{9,13},{10,... | collective-permute-start | bytes 294920 | tf_op jit(solution)/shard_map/ppermute | solution.py:740
  4.9 2.6 %collective-permute-start.1 = (bf16[64,768]{1,0:T(8,128)(2,1)S(1)}, bf16[64,768]{1,0:T(8,128)(2,1)S(1)}, u32[]{:S(2)}, u32[]{:S(2)}) collective-permute-start(bf16[64,768]{1,0:T(8,128)(2,1)S(1)} %get-tuple-element.239), channel_id=1, source_target_pairs={{0,8},{1,9},{2,10},{3,11},{4,12},{5,13},{6,14},{7,15},{8,0},{9,1},... | collective-permute-start | bytes 294920 | tf_op jit(solution)/shard_map/ppermute | solution.py:740
  9.0 2.0 constant_dynamic-slice_fusion.2
  11.5 3.8 %collective-permute-done.1 = bf16[64,768]{1,0:T(8,128)(2,1)S(1)} collective-permute-done((bf16[64,768]{1,0:T(8,128)(2,1)S(1)}, bf16[64,768]{1,0:T(8,128)(2,1)S(1)}, u32[]{:S(2)}, u32[]{:S(2)}) %collective-permute-start.1) | collective-permute-done | bytes 98336 | tf_op jit(solution)/shard_map/ppermute | solution.py:740
  16.9 7.6 %collective-permute-done.4.refs_6_ = bf16[4,64,768]{2,1,0:T(8,128)(2,1)} collective-permute-done((bf16[4,64,768]{2,1,0:T(8,128)(2,1)S(1)}, bf16[4,64,768]{2,1,0:T(8,128)(2,1)}, u32[]{:S(2)}, u32[]{:S(2)}) %collective-permute-start.4) | collective-permute-done | bytes 393248 | tf_op jit(solution)/shard_map/ppermute | solution.py:740
  24.9 2.4 %collective-permute-start.6 = (bf16[64,768]{1,0:T(8,128)(2,1)S(1)}, bf16[64,768]{1,0:T(8,128)(2,1)S(1)}, u32[]{:S(2)}, u32[]{:S(2)}) collective-permute-start(bf16[64,768]{1,0:T(8,128)(2,1)S(1)} %get-tuple-element.234), channel_id=1, source_target_pairs={{0,4},{1,5},{2,6},{3,7},{4,0},{5,1},{6,2},{7,3},{8,12},{9,13},{10,... | collective-permute-start | bytes 294920 | tf_op jit(solution)/shard_map/ppermute | solution.py:740
  29.8 13.9 %attention_forward.1 = (bf16[1024,768]{1,0:T(8,128)(2,1)}, bf16[9,1024,64]{2,1,0:T(8,128)(2,1)}, bf16[128,384]{1,0:T(8,128)(2,1)S(1)}, bf16[128,384]{1,0:T(8,128...) custom-call(s32[4]{0:T(128)S(1)} %pad_add_fusion.refs_0_.place_ref, ...), custom_call_target="tpu_custom_call" | custom-call | flops 8589934592 | bytes 8388608 | tf_op jit(solution)/shard_map/attention_forward/pallas_call | solution.py:154
  47.2 3.7 %collective-permute-done.10.refs_3_ = bf16[128,384]{1,0:T(8,128)(2,1)S(1)} collective-permute-done((bf16[128,384]{1,0:T(8,128)(2,1)}, bf16[128,384]{1,0:T(8,128)(2,1)S(1)}, u32[]{:S(2)}, u32[]{:S(2)}) %collective-permute-start.10) | collective-permute-done | bytes 98336 | tf_op jit(solution)/shard_map/ppermute | solution.py:740
  54.0 7.4 %widen.1 = (bf16[256,768]{1,0:T(8,128)(2,1)S(1)}, f32[256,768]{1,0:T(8,128)S(1)}, bf16[256,768]{1,0:T(8,128)(2,1)S(1)}, bf16[256,3072]{1,0:T(8,128)(2,1)S(1)}, b...) custom-call(s32[4]{0:T(128)S(1)} %pad_add_fusion.refs_0_.place_ref, ...), custom_call_target="tpu_custom_call" | custom-call | flops 6442450944 | bytes 6291456 | tf_op jit(solution)/shard_map/widen/pallas_call | solution.py:425
  61.4 2.5 %shrink_outer.1 = (bf16[2,2,2,2,192,384]{5,4,3,2,1,0:T(8,128)(2,1)S(1)}, bf16[2,2,2,2,192,384]{5,4,3,2,1,0:T(8,128)(2,1)S(1)}) custom-call(s32[4]{0:T(128)S(1)} %pad_add_fusion.refs_0_.place_ref, bf16[256,3072]{1,0:T(8,128)(2,1)S(1)} %get-tuple-element.137.refs_2_.hidden_ref, bf16[256,768]{1,0:T(8,128)(2,1)S(1)} %get-tuple-element.136.refs_1_.branch_ref), custom_call_target="tpu_custom_call" | custom-call | flops 2147483648 | bytes 10485760 | tf_op jit(solution)/shard_map/shrink_outer/pallas_call | solution.py:648
  64.2 10.5 %turn.1 = (bf16[256,3072]{1,0:T(8,128)(2,1)S(1)}, bf16[256,768]{1,0:T(8,128)(2,1)S(1)}, f32[256,768]{1,0:T(8,128)S(1)}, f32[1,4608]{1,0:T(1,128)S(1)}, bf16[128,...) custom-call(s32[4]{0:T(128)S(1)} %pad_add_fusion.refs_0_.place_ref, ...), custom_call_target="tpu_custom_call" | custom-call | flops 9663676416 | bytes 8388608 | tf_op jit(solution)/shard_map/turn/pallas_call | solution.py:572
  76.6 2.9 %expand_outer.1 = (bf16[2,2,2,2,48,1920]{5,4,3,2,1,0:T(8,128)(2,1)S(1)}, bf16[2,2,2,2,48,1920]{5,4,3,2,1,0:T(8,128)(2,1)S(1)}) custom-call(s32[4]{0:T(128)S(1)} %pad_add_fusion.refs_0_.place_ref, bf16[256,768]{1,0:T(8,128)(2,1)S(1)} %get-tuple-element.149.second_ref, bf16[256,3072]{1,0:T(8,128)(2,1)S(1)} %get-tuple-element.150.expanded_ref, ...), custom_call_target="tpu_custom_call" | custom-call | flops 2147483648 | bytes 10485760 | tf_op jit(solution)/shard_map/expand_outer/pallas_call | solution.py:648
  89.9 13.8 %attention_backward.1 = (bf16[17,24,576]{2,1,0:T(8,128)(2,1)S(1)}, bf16[17,24,576]{2,1,0:T(8,128)(2,1)S(1)}, bf16[2,256,768]{2,1,0:T(8,128)(2,1)S(1)}, bf16[2,256,768]{2,1,0:T(8,128)(2,1)S(1)}) custom-call(s32[4]{0:T(128)S(1)} %pad_add_fusion.refs_0_.place_ref, bf16[1024,768]{1,0:T(8,128)(2,1)} %get-tuple-element.120.refs_1_, ...), custom_call_target="tpu_custom_call" | custom-call | flops 10737418240 | bytes 10485760 | tf_op jit(solution)/shard_map/attention_backward/pallas_call | solution.py:298
  110.7 2.9 %collective-permute-done.22 = bf16[2,2,96,384]{3,2,1,0:T(8,128)(2,1)S(1)} collective-permute-done((bf16[2,2,96,384]{3,2,1,0:T(8,128)(2,1)S(1)}, bf16[2,2,96,384]{3,2,1,0:T(8,128)(2,1)S(1)}, u32[]{:S(2)}, u32[]{:S(2)}) %collective-permute-start.22) | collective-permute-done | bytes 294944 | tf_op jit(solution)/shard_map/ppermute | solution.py:740
  114.9 11.2 %collective-permute-done.24 = bf16[17,24,576]{2,1,0:T(8,128)(2,1)S(1)} collective-permute-done((bf16[17,24,576]{2,1,0:T(8,128)(2,1)S(1)}, bf16[17,24,576]{2,1,0:T(8,128)(2,1)S(1)}, u32[]{:S(2)}, u32[]{:S(2)}) %collective-permute-start.24) | collective-permute-done | bytes 470048 | tf_op jit(solution)/shard_map/ppermute | solution.py:740
  135.2 7.1 %collective-permute-done.28 = bf16[2,2,2,48,1024]{4,3,2,1,0:T(8,128)(2,1)} collective-permute-done((bf16[2,2,2,48,1024]{4,3,2,1,0:T(8,128)(2,1)}, bf16[2,2,2,48,1024]{4,3,2,1,0:T(8,128)(2,1)}, u32[]{:S(2)}, u32[]{:S(2)}) %collective-permute-start.28) | collective-permute-done | bytes 786464 | tf_op jit(solution)/shard_map/ppermute | solution.py:740
  151.6 2.8 %collective-permute-start.33 = (bf16[192,384]{1,0:T(8,128)(2,1)S(1)}, bf16[192,384]{1,0:T(8,128)(2,1)S(1)}, u32[]{:S(2)}, u32[]{:S(2)}) collective-permute-start(bf16[192,384]{1,0:T(8,128)(2,1)S(1)} %pad_maximum_fusion.9), channel_id=1, source_target_pairs={{0,8},{1,9},{2,10},{3,11},{4,12},{5,13},{6,14},{7,15},{8,0},{9,1},... | collective-permute-start | bytes 442376 | tf_op jit(solution)/shard_map/ppermute | solution.py:740
  156.6 6.2 %collective-permute-done.34 = bf16[5,24,576]{2,1,0:T(8,128)(2,1)S(1)} collective-permute-done((bf16[5,24,576]{2,1,0:T(8,128)(2,1)S(1)}, bf16[5,24,576]{2,1,0:T(8,128)(2,1)S(1)}, u32[]{:S(2)}, u32[]{:S(2)}) %collective-permute-start.34) | collective-permute-done | bytes 138272 | tf_op jit(solution)/shard_map/ppermute | solution.py:740
  172.5 2.2 %collective-permute-start.38 = (bf16[64,768]{1,0:T(8,128)(2,1)S(1)}, bf16[64,768]{1,0:T(8,128)(2,1)S(1)}, u32[]{:S(2)}, u32[]{:S(2)}) collective-permute-start(bf16[64,768]{1,0:T(8,128)(2,1)S(1)} %get-tuple-element.206), channel_id=1, source_target_pairs={{0,12},{1,13},{2,14},{3,15},{4,8},{5,9},{6,10},{7,11},{8,4},{9,5},... | collective-permute-start | bytes 294920 | tf_op jit(solution)/shard_map/ppermute | solution.py:740
  177.5 3.2 %collective-permute-done.37.refs_2_ = bf16[64,768]{1,0:T(8,128)(2,1)S(1)} collective-permute-done((bf16[64,768]{1,0:T(8,128)(2,1)S(1)}, bf16[64,768]{1,0:T(8,128)(2,1)S(1)}, u32[]{:S(2)}, u32[]{:S(2)}) %collective-permute-start.37) | collective-permute-done | bytes 98336 | tf_op jit(solution)/shard_map/ppermute | solution.py:740
  180.8 7.8 %collective-permute-done.35 = bf16[2,48,1920]{2,1,0:T(8,128)(2,1)S(1)} collective-permute-done((bf16[2,48,1920]{2,1,0:T(8,128)(2,1)S(1)}, bf16[2,48,1920]{2,1,0:T(8,128)(2,1)S(1)}, u32[]{:S(2)}, u32[]{:S(2)}) %collective-permute-start.35) | collective-permute-done | bytes 368672 | tf_op jit(solution)/shard_map/ppermute | solution.py:740
  192.6 3.0 %collective-permute-done.43 = bf16[24,2304]{1,0:T(8,128)(2,1)S(1)} collective-permute-done((bf16[24,2304]{1,0:T(8,128)(2,1)S(1)}, bf16[24,2304]{1,0:T(8,128)(2,1)S(1)}, u32[]{:S(2)}, u32[]{:S(2)}) %collective-permute-start.43) | collective-permute-done | bytes 110624 | tf_op jit(solution)/shard_map/ppermute | solution.py:740
  195.6 6.1 %collective-permute-done.44 = bf16[48,1920]{1,0:T(8,128)(2,1)S(1)} collective-permute-done((bf16[48,1920]{1,0:T(8,128)(2,1)S(1)}, bf16[48,1920]{1,0:T(8,128)(2,1)S(1)}, u32[]{:S(2)}, u32[]{:S(2)}) %collective-permute-start.44) | collective-permute-done | bytes 184352 | tf_op jit(solution)/shard_map/ppermute | solution.py:740
  205.8 4.6 %collective-permute-done.45 = bf16[48,1920]{1,0:T(8,128)(2,1)S(1)} collective-permute-done((bf16[48,1920]{1,0:T(8,128)(2,1)S(1)}, bf16[48,1920]{1,0:T(8,128)(2,1)S(1)}, u32[]{:S(2)}, u32[]{:S(2)}) %collective-permute-start.45) | collective-permute-done | bytes 184352 | tf_op jit(solution)/shard_map/ppermute | solution.py:740
  (217 shorter events, 77.6 us)
Async XLA Ops:
  16.9 12.9 %collective-permute-start.3 = (bf16[4,64,768]{2,1,0:T(8,128)(2,1)S(1)}, bf16[4,64,768]{2,1,0:T(8,128)(2,1)}, u32[]{:S(2)}, u32[]{:S(2)}) collective-permute-start(bf16[4,64,768]{2,1,0:T(8,128)(2,1)S(1)} %pad_maximum_fusion.1.refs_4_), channel_id=1, source_target_pairs={{0,1},{1,0},{2,3},{3,2},{4,5},{5,4},{6,7},{7,6},{8,9},{9,8},{10,11... | collective-permute-start | bytes 1179656 | tf_op jit(solution)/shard_map/ppermute | solution.py:740
  24.9 19.5 %collective-permute-start.6 = (bf16[64,768]{1,0:T(8,128)(2,1)S(1)}, bf16[64,768]{1,0:T(8,128)(2,1)S(1)}, u32[]{:S(2)}, u32[]{:S(2)}) collective-permute-start(bf16[64,768]{1,0:T(8,128)(2,1)S(1)} %get-tuple-element.234), channel_id=1, source_target_pairs={{0,4},{1,5},{2,6},{3,7},{4,0},{5,1},{6,2},{7,3},{8,12},{9,13},{10,... | collective-permute-start | bytes 294920 | tf_op jit(solution)/shard_map/ppermute | solution.py:740
  27.3 17.1 %collective-permute-start.7 = (bf16[64,768]{1,0:T(8,128)(2,1)S(1)}, bf16[64,768]{1,0:T(8,128)(2,1)S(1)}, u32[]{:S(2)}, u32[]{:S(2)}) collective-permute-start(bf16[64,768]{1,0:T(8,128)(2,1)S(1)} %get-tuple-element.233), channel_id=1, source_target_pairs={{0,8},{1,9},{2,10},{3,11},{4,12},{5,13},{6,14},{7,15},{8,0},{9,1},... | collective-permute-start | bytes 294920 | tf_op jit(solution)/shard_map/ppermute | solution.py:740
  28.4 16.1 %collective-permute-start.8 = (bf16[64,768]{1,0:T(8,128)(2,1)S(1)}, bf16[64,768]{1,0:T(8,128)(2,1)S(1)}, u32[]{:S(2)}, u32[]{:S(2)}) collective-permute-start(bf16[64,768]{1,0:T(8,128)(2,1)S(1)} %get-tuple-element.232), channel_id=1, source_target_pairs={{0,12},{1,13},{2,14},{3,15},{4,8},{5,9},{6,10},{7,11},{8,4},{9,5},... | collective-permute-start | bytes 294920 | tf_op jit(solution)/shard_map/ppermute | solution.py:740
  63.9 17.8 %collective-permute-start.15 = (bf16[2,2,2,2,192,384]{5,4,3,2,1,0:T(8,128)(2,1)S(1)}, bf16[2,2,2,2,192,384]{5,4,3,2,1,0:T(8,128)(2,1)S(1)}, u32[]{:S(2)}, u32[]{:S(2)}) collective-permute-start(bf16[2,2,2,2,192,384]{5,4,3,2,1,0:T(8,128)(2,1)S(1)} %get-tuple-element.154), channel_id=1, source_target_pairs={{0,1},{1,0},{2,3},{3,2},{4,5},{5,4},{6,7},{7,6},{8,9},{9,8},{10,11... | collective-permute-start | bytes 7077896 | tf_op jit(solution)/shard_map/ppermute | solution.py:740
  81.6 22.2 %collective-permute-start.18 = (bf16[2,2,2,2,48,1920]{5,4,3,2,1,0:T(8,128)(2,1)S(1)}, bf16[2,2,2,2,48,1920]{5,4,3,2,1,0:T(8,128)(2,1)S(1)}, u32[]{:S(2)}, u32[]{:S(2)}) collective-permute-start(bf16[2,2,2,2,48,1920]{5,4,3,2,1,0:T(8,128)(2,1)S(1)} %get-tuple-element.171), channel_id=1, source_target_pairs={{0,1},{1,0},{2,3},{3,2},{4,5},{5,4},{6,7},{7,6},{8,9},{9,8},{10,11... | collective-permute-start | bytes 8847368 | tf_op jit(solution)/shard_map/ppermute | solution.py:740
  83.4 20.3 %collective-permute-start.16 = (bf16[2,2,2,96,384]{4,3,2,1,0:T(8,128)(2,1)S(1)}, bf16[2,2,2,96,384]{4,3,2,1,0:T(8,128)(2,1)S(1)}, u32[]{:S(2)}, u32[]{:S(2)}) collective-permute-start(bf16[2,2,2,96,384]{4,3,2,1,0:T(8,128)(2,1)S(1)} %fusion.4), channel_id=1, source_target_pairs={{0,16},{16,0},{1,17},{17,1},{2,18},{18,2},{3,19},{19,3},{4,20},{20... | collective-permute-start | bytes 1769480 | tf_op jit(solution)/shard_map/ppermute | solution.py:740
  85.0 18.8 %collective-permute-start.17 = (bf16[2,2,2,96,384]{4,3,2,1,0:T(8,128)(2,1)S(1)}, bf16[2,2,2,96,384]{4,3,2,1,0:T(8,128)(2,1)S(1)}, u32[]{:S(2)}, u32[]{:S(2)}) collective-permute-start(bf16[2,2,2,96,384]{4,3,2,1,0:T(8,128)(2,1)S(1)} %fusion.5), channel_id=1, source_target_pairs={{0,2},{1,3},{2,0},{3,1},{4,6},{5,7},{6,4},{7,5},{8,10},{9,11},{10,... | collective-permute-start | bytes 1769480 | tf_op jit(solution)/shard_map/ppermute | solution.py:740
  86.5 17.2 %collective-permute-start.20 = (bf16[64,768]{1,0:T(8,128)(2,1)S(1)}, bf16[64,768]{1,0:T(8,128)(2,1)S(1)}, u32[]{:S(2)}, u32[]{:S(2)}) collective-permute-start(bf16[64,768]{1,0:T(8,128)(2,1)S(1)} %get-tuple-element.174), channel_id=1, source_target_pairs={{0,8},{1,9},{2,10},{3,11},{4,12},{5,13},{6,14},{7,15},{8,0},{9,1},... | collective-permute-start | bytes 294920 | tf_op jit(solution)/shard_map/ppermute | solution.py:740
  88.5 15.2 %collective-permute-start.21 = (bf16[64,768]{1,0:T(8,128)(2,1)S(1)}, bf16[64,768]{1,0:T(8,128)(2,1)S(1)}, u32[]{:S(2)}, u32[]{:S(2)}) collective-permute-start(bf16[64,768]{1,0:T(8,128)(2,1)S(1)} %get-tuple-element.175), channel_id=1, source_target_pairs={{0,12},{1,13},{2,14},{3,15},{4,8},{5,9},{6,10},{7,11},{8,4},{9,5},... | collective-permute-start | bytes 294920 | tf_op jit(solution)/shard_map/ppermute | solution.py:740
  103.8 22.3 %collective-permute-start.25 = (bf16[2,256,768]{2,1,0:T(8,128)(2,1)S(1)}, bf16[2,256,768]{2,1,0:T(8,128)(2,1)S(1)}, u32[]{:S(2)}, u32[]{:S(2)}) collective-permute-start(bf16[2,256,768]{2,1,0:T(8,128)(2,1)S(1)} %get-tuple-element.186), channel_id=1, source_target_pairs={{0,1},{1,0},{2,3},{3,2},{4,5},{5,4},{6,7},{7,6},{8,9},{9,8},{10,11... | collective-permute-start | bytes 2359304 | tf_op jit(solution)/shard_map/ppermute | solution.py:740
  106.6 19.5 %collective-permute-start.24 = (bf16[17,24,576]{2,1,0:T(8,128)(2,1)S(1)}, bf16[17,24,576]{2,1,0:T(8,128)(2,1)S(1)}, u32[]{:S(2)}, u32[]{:S(2)}) collective-permute-start(bf16[17,24,576]{2,1,0:T(8,128)(2,1)S(1)} %get-tuple-element.185), channel_id=1, source_target_pairs={{0,16},{16,0},{1,17},{17,1},{2,18},{18,2},{3,19},{19,3},{4,20},{20... | collective-permute-start | bytes 1410056 | tf_op jit(solution)/shard_map/ppermute | solution.py:740
  108.2 34.2 %collective-permute-start.28 = (bf16[2,2,2,48,1024]{4,3,2,1,0:T(8,128)(2,1)}, bf16[2,2,2,48,1024]{4,3,2,1,0:T(8,128)(2,1)}, u32[]{:S(2)}, u32[]{:S(2)}) collective-permute-start(bf16[2,2,2,48,1024]{4,3,2,1,0:T(8,128)(2,1)} %fusion), channel_id=1, source_target_pairs={{0,16},{16,0},{1,17},{17,1},{2,18},{18,2},{3,19},{19,3},{4,20},{20... | collective-permute-start | bytes 2359304 | tf_op jit(solution)/shard_map/ppermute | solution.py:740
  113.6 21.6 %collective-permute-start.29 = (bf16[2,2,2,48,896]{4,3,2,1,0:T(8,128)(2,1)}, bf16[2,2,2,48,896]{4,3,2,1,0:T(8,128)(2,1)}, u32[]{:S(2)}, u32[]{:S(2)}) collective-permute-start(bf16[2,2,2,48,896]{4,3,2,1,0:T(8,128)(2,1)} %fusion.2), channel_id=1, source_target_pairs={{0,2},{1,3},{2,0},{3,1},{4,6},{5,7},{6,4},{7,5},{8,10},{9,11},{10,... | collective-permute-start | bytes 2064392 | tf_op jit(solution)/shard_map/ppermute | solution.py:740
  127.1 15.9 %collective-permute-start.30 = (bf16[256,768]{1,0:T(8,128)(2,1)}, bf16[256,768]{1,0:T(8,128)(2,1)}, u32[]{:S(2)}, u32[]{:S(2)}) collective-permute-start(bf16[256,768]{1,0:T(8,128)(2,1)} %fusion.8), channel_id=1, source_target_pairs={{0,2},{1,3},{2,0},{3,1},{4,6},{5,7},{6,4},{7,5},{8,10},{9,11},{10,... | collective-permute-start | bytes 1179656 | tf_op jit(solution)/shard_map/ppermute | solution.py:740
  129.3 13.7 %collective-permute-start.27 = (bf16[2,192,384]{2,1,0:T(8,128)(2,1)}, bf16[2,192,384]{2,1,0:T(8,128)(2,1)}, u32[]{:S(2)}, u32[]{:S(2)}) collective-permute-start(bf16[2,192,384]{2,1,0:T(8,128)(2,1)} %pad_maximum_fusion.3), channel_id=1, source_target_pairs={{0,4},{1,5},{2,6},{3,7},{4,0},{5,1},{6,2},{7,3},{8,12},{9,13},{10,... | collective-permute-start | bytes 884744 | tf_op jit(solution)/shard_map/ppermute | solution.py:740
  130.2 12.8 %collective-permute-start.26 = (bf16[9,24,576]{2,1,0:T(8,128)(2,1)}, bf16[9,24,576]{2,1,0:T(8,128)(2,1)}, u32[]{:S(2)}, u32[]{:S(2)}) collective-permute-start(bf16[9,24,576]{2,1,0:T(8,128)(2,1)} %pad_maximum_fusion.4), channel_id=1, source_target_pairs={{0,4},{1,5},{2,6},{3,7},{4,0},{5,1},{6,2},{7,3},{8,12},{9,13},{10,... | collective-permute-start | bytes 746504 | tf_op jit(solution)/shard_map/ppermute | solution.py:740
  146.3 19.4 %collective-permute-start.31 = (bf16[2,2,48,1024]{3,2,1,0:T(8,128)(2,1)S(1)}, bf16[2,2,48,1024]{3,2,1,0:T(8,128)(2,1)S(1)}, u32[]{:S(2)}, u32[]{:S(2)}) collective-permute-start(bf16[2,2,48,1024]{3,2,1,0:T(8,128)(2,1)S(1)} %fusion.1), channel_id=1, source_target_pairs={{0,2},{1,3},{2,0},{3,1},{4,6},{5,7},{6,4},{7,5},{8,10},{9,11},{10,... | collective-permute-start | bytes 1179656 | tf_op jit(solution)/shard_map/ppermute | solution.py:740
  148.4 17.2 %collective-permute-start.32 = (bf16[2,2,48,896]{3,2,1,0:T(8,128)(2,1)S(1)}, bf16[2,2,48,896]{3,2,1,0:T(8,128)(2,1)S(1)}, u32[]{:S(2)}, u32[]{:S(2)}) collective-permute-start(bf16[2,2,48,896]{3,2,1,0:T(8,128)(2,1)S(1)} %fusion.3), channel_id=1, source_target_pairs={{0,16},{16,0},{1,17},{17,1},{2,18},{18,2},{3,19},{19,3},{4,20},{20... | collective-permute-start | bytes 1032200 | tf_op jit(solution)/shard_map/ppermute | solution.py:740
  150.0 12.7 %collective-permute-start.34 = (bf16[5,24,576]{2,1,0:T(8,128)(2,1)S(1)}, bf16[5,24,576]{2,1,0:T(8,128)(2,1)S(1)}, u32[]{:S(2)}, u32[]{:S(2)}) collective-permute-start(bf16[5,24,576]{2,1,0:T(8,128)(2,1)S(1)} %pad_maximum_fusion.7), channel_id=1, source_target_pairs={{0,8},{1,9},{2,10},{3,11},{4,12},{5,13},{6,14},{7,15},{8,0},{9,1},... | collective-permute-start | bytes 414728 | tf_op jit(solution)/shard_map/ppermute | solution.py:740
  151.6 12.8 %collective-permute-start.33 = (bf16[192,384]{1,0:T(8,128)(2,1)S(1)}, bf16[192,384]{1,0:T(8,128)(2,1)S(1)}, u32[]{:S(2)}, u32[]{:S(2)}) collective-permute-start(bf16[192,384]{1,0:T(8,128)(2,1)S(1)} %pad_maximum_fusion.9), channel_id=1, source_target_pairs={{0,8},{1,9},{2,10},{3,11},{4,12},{5,13},{6,14},{7,15},{8,0},{9,1},... | collective-permute-start | bytes 442376 | tf_op jit(solution)/shard_map/ppermute | solution.py:740
  156.0 21.5 %collective-permute-start.36 = (bf16[64,768]{1,0:T(8,128)(2,1)S(1)}, bf16[64,768]{1,0:T(8,128)(2,1)S(1)}, u32[]{:S(2)}, u32[]{:S(2)}) collective-permute-start(bf16[64,768]{1,0:T(8,128)(2,1)S(1)} %get-tuple-element.204), channel_id=1, source_target_pairs={{0,4},{1,5},{2,6},{3,7},{4,0},{5,1},{6,2},{7,3},{8,12},{9,13},{10,... | collective-permute-start | bytes 294920 | tf_op jit(solution)/shard_map/ppermute | solution.py:740
  174.7 13.8 %collective-permute-start.35 = (bf16[2,48,1920]{2,1,0:T(8,128)(2,1)S(1)}, bf16[2,48,1920]{2,1,0:T(8,128)(2,1)S(1)}, u32[]{:S(2)}, u32[]{:S(2)}) collective-permute-start(bf16[2,48,1920]{2,1,0:T(8,128)(2,1)S(1)} %pad_maximum_fusion.2), channel_id=1, source_target_pairs={{0,4},{1,5},{2,6},{3,7},{4,0},{5,1},{6,2},{7,3},{8,12},{9,13},{10,... | collective-permute-start | bytes 1105928 | tf_op jit(solution)/shard_map/ppermute | solution.py:740
  191.2 10.5 %collective-permute-start.44 = (bf16[48,1920]{1,0:T(8,128)(2,1)S(1)}, bf16[48,1920]{1,0:T(8,128)(2,1)S(1)}, u32[]{:S(2)}, u32[]{:S(2)}) collective-permute-start(bf16[48,1920]{1,0:T(8,128)(2,1)S(1)} %pad_maximum_fusion.5), channel_id=1, source_target_pairs={{0,8},{1,9},{2,10},{3,11},{4,12},{5,13},{6,14},{7,15},{8,0},{9,1},... | collective-permute-start | bytes 552968 | tf_op jit(solution)/shard_map/ppermute | solution.py:740
  (58 other events, 680.7 us)

commit v3 on v2

--- a/solution.py
+++ b/solution.py
@@ -10,6 +10,7 @@
 HEAD = 64
 TILE = 256
 WIDE = 512
+BAND = 384
 FORWARD_MIB = 24
 BACKWARD_MIB = 24
 WIDEN_MIB = 16
@@ -176,19 +177,19 @@
     return outs[:2], outs[2 : 2 + slots], outs[2 + slots :]
 
 
-def backward_kernel(*refs, planes, slots, seg, heads, rows_each, sides):
+def backward_kernel(*refs, planes, slots, seg, heads, rows_each):
     place_ref, first_from, joined_from, weight_ref, gain_ref, parts_ref = refs[:6]
     pieces = refs[6 : 6 + slots]
     length = planes * slots * seg
     tiles = length // TILE
     refs = refs[6 + slots :]
     shares_from = refs[:tiles]
-    joined_keep, joined_give, branch_keep, branch_give = refs[tiles : tiles + 4]
+    joined_out, branch_keep, branch_give = refs[tiles : tiles + 3]
     (
         grad_ref, arrived_ref, key_ref, value_ref, total_ref, outer_ref, row_ref,
         first_ref, joined_ref,
-    ) = refs[tiles + 4 : tiles + 13]
-    shares = refs[tiles + 13 : 2 * tiles + 13]
+    ) = refs[tiles + 3 : tiles + 12]
+    shares = refs[tiles + 12 : 2 * tiles + 12]
     ready = refs[-1]
     copies = [
         pltpu.make_async_copy(source, target, ready.at[at])
@@ -200,7 +201,7 @@
     for q in reversed(range(tiles)):
         copies[2 + q].start()
     copies[1].start()
-    plane, slot, side = place_ref[0], place_ref[1], place_ref[3]
+    plane, slot = place_ref[0], place_ref[1]
     width = heads * HEAD
     half = planes // 2
     for u in range(slots):
@@ -262,25 +263,22 @@
     wide = 3 * width
     row_ref[:, model : model + parts_ref.shape[1]] = parts_ref[...]
     gains = model + parts_ref.shape[1]
-    rows = rows_each // sides
-    outs = [joined_keep, joined_give][:sides] if sides > 1 else [joined_keep]
-    for other, out in enumerate(outs):
-        at = 0
-        for _, code in codes(range(bits_of(planes))):
-            for u in range(slots):
-                offset = ((plane ^ code) * slots + (slot ^ u)) * rows_each + (side ^ other) * rows
-                if sides == 1:
-                    offset = ((plane ^ code) * slots + (slot ^ u)) * rows_each
-                out[at] = outer_ref[pl.ds(pl.multiple_of(offset, rows), rows), :].astype(bf16)
-                at += 1
-        out[at] = jnp.zeros((rows, wide), bf16)
-        for r in range(-(-gains // wide)):
-            end = min((r + 1) * wide, gains)
-            out[at, r : r + 1, : end - r * wide] = row_ref[:, r * wide : end].astype(bf16)
+    at = 0
+    for _, code in codes(range(bits_of(planes))):
+        for u in range(slots):
+            offset = ((plane ^ code) * slots + (slot ^ u)) * rows_each
+            joined_out[at] = outer_ref[
+                pl.ds(pl.multiple_of(offset, rows_each), rows_each), :
+            ].astype(bf16)
+            at += 1
+    joined_out[at] = jnp.zeros((rows_each, wide), bf16)
+    for r in range(-(-gains // wide)):
+        end = min((r + 1) * wide, gains)
+        joined_out[at, r : r + 1, : end - r * wide] = row_ref[:, r * wide : end].astype(bf16)
 
 
 def backward_call(
-    place, first, joined, weight, gain, parts, pieces, shares, planes, sides
+    place, first, joined, weight, gain, parts, pieces, shares, planes
 ):
     slots = len(pieces)
     tokens = pieces[0].shape[0] * 2
@@ -289,17 +287,15 @@
     rows_each = width // (planes * slots)
     kernel = functools.partial(
         backward_kernel, planes=planes, slots=slots, seg=tokens // planes, heads=heads,
-        rows_each=rows_each, sides=sides,
+        rows_each=rows_each,
     )
     pairs = (2,) * (bits_of(slots) - 1)
     wide = 3 * heads * HEAD
     row = -(-(width + parts.shape[1]) // 128) * 128
-    blocks = jax.ShapeDtypeStruct((planes * slots + 1, rows_each // sides, wide), bf16)
     return pl.pallas_call(
         kernel,
         out_shape=(
-            blocks,
-            blocks,
+            jax.ShapeDtypeStruct((planes * slots + 1, rows_each, wide), bf16),
             jax.ShapeDtypeStruct(pairs + (tokens, width), bf16),
             jax.ShapeDtypeStruct(pairs + (tokens, width), bf16),
         ),
@@ -307,7 +303,7 @@
         + [hbm_spec()] * 2
         + [vmem_spec()] * (3 + slots)
         + [hbm_spec()] * len(shares),
-        out_specs=(vmem_spec(),) * 4,
+        out_specs=(vmem_spec(),) * 3,
         scratch_shapes=[
             pltpu.VMEM((length, wide), bf16),
             pltpu.VMEM((length, heads * HEAD), bf16),
@@ -327,7 +323,7 @@
     )(place, first, joined, weight, gain, parts, *pieces, *shares)
 
 
-def widen_kernel(*refs, slots, planes, groups, width, spread):
+def widen_kernel(*refs, slots, planes, groups, width, spread, block):
     place_ref = refs[0]
     pieces = refs[1 : 1 + slots]
     blocks = refs[1 + slots : 1 + slots + planes]
@@ -336,10 +332,10 @@
         valid_ref, input_ref, mixed_gain_ref, second_gain_ref, hidden_gain_ref, merge_ref, expand_from,
     ) = refs[:7]
     (
-        mixed_ref, middle_ref, second_ref, hidden_ref, normal_ref, slope_ref, held_ref,
-        mixed_rate_ref, hidden_rate_ref, branch_ref,
-    ) = refs[7:17]
-    expand_ref, gelu_ref, ready = refs[17:]
+        mixed_ref, middle_ref, second_ref, hidden_ref, hidden_give_ref, normal_ref, slope_ref,
+        held_ref, mixed_rate_ref, hidden_rate_ref, branch_ref,
+    ) = refs[7:18]
+    expand_ref, gelu_ref, ready = refs[18:]
     steps = spread // WIDE
 
     def copy(step):
@@ -400,11 +396,23 @@
         total = total + jnp.sum(centred * centred, axis=-1, keepdims=True)
     rate = lax.rsqrt(total * (1.0 / spread) + norm_epsilon)
     hidden_rate_ref[...] = rate
-    for step in range(steps):
-        at = slice(step * WIDE, (step + 1) * WIDE)
-        normal = (gelu_ref[:, at] - mean) * rate
-        normal_ref[:, at] = normal.astype(bf16)
-        hidden_ref[:, at] = (normal * hidden_gain_ref[:, at]).astype(bf16)
+    core = slot % 2
+    for at in range(0, spread, 2 * BAND):
+        ours, theirs = [], []
+        for start in range(at, at + 2 * BAND, 2 * block):
+            low = slice(start, start + block)
+            high = slice(start + block, start + 2 * block)
+            parts = []
+            for part in (low, high):
+                normal = (gelu_ref[:, part] - mean) * rate
+                normal_ref[:, part] = normal.astype(bf16)
+                parts.append((normal * hidden_gain_ref[:, part]).astype(bf16))
+            ours.append(parts[0])
+            theirs.append(parts[1])
+        even, odd = jnp.concatenate(ours, axis=1), jnp.concatenate(theirs, axis=1)
+        half_at = slice(at // 2, at // 2 + BAND)
+        hidden_ref[:, half_at] = jnp.where(core == 0, even, odd)
+        hidden_give_ref[:, half_at] = jnp.where(core == 0, odd, even)
 
 
 def widen_call(
@@ -425,13 +433,14 @@
     return pl.pallas_call(
         functools.partial(
             widen_kernel, slots=slots, planes=len(blocks), groups=groups, width=width,
-            spread=spread,
+            spread=spread, block=spread // (slots * len(blocks)),
         ),
         out_shape=(
             low(tokens, width),
             full(tokens, width),
             low(tokens, width),
-            low(tokens, spread),
+            low(tokens, spread // 2),
+            low(tokens, spread // 2),
             low(tokens, spread),
             low(tokens, spread),
             full(slots, tokens, piece),
@@ -442,7 +451,7 @@
         in_specs=[pl.BlockSpec(memory_space=pltpu.SMEM)]
         + [vmem_spec()] * (6 + slots + len(blocks))
         + [hbm_spec()],
-        out_specs=(vmem_spec(),) * 10,
+        out_specs=(vmem_spec(),) * 11,
         scratch_shapes=[
             pltpu.VMEM((width, spread), bf16),
             pltpu.VMEM((tokens, spread), f32),
@@ -459,14 +468,14 @@
 
 def turn_kernel(*refs, slots, planes, groups, width, spread):
     (
-        place_ref, branch_ref, hidden_ref, normal_ref, slope_ref, middle_ref, held_ref,
+        place_ref, branch_ref, normal_ref, slope_ref, middle_ref, held_ref,
         mixed_rate_ref, hidden_rate_ref,
         mixed_gain_ref, second_gain_ref, hidden_gain_ref, merge_ref, shrink_from, expand_from,
-    ) = refs[:15]
-    expanded_ref, mix_ref, grad_ref, parts_ref = refs[15:19]
-    away = refs[19 : 19 + slots]
-    results = refs[19 + slots : 19 + slots + planes]
-    shrink_ref, expand_ref, weighted_ref, sent_ref, ready = refs[19 + slots + planes :]
+    ) = refs[:14]
+    expanded_ref, mix_ref, grad_ref, parts_ref = refs[14:18]
+    away = refs[18 : 18 + slots]
+    results = refs[18 + slots : 18 + slots + planes]
+    shrink_ref, expand_ref, weighted_ref, sent_ref, ready = refs[18 + slots + planes :]
     steps = spread // WIDE
 
     def copy_shrink(step):
@@ -494,9 +503,10 @@
     for step in range(steps):
         copy_shrink(step).wait()
         at = slice(step * WIDE, (step + 1) * WIDE)
-        result = result + dot(hidden_ref[:, at], shrink_ref[at, :])
+        normal = normal_ref[:, at].astype(f32)
+        hidden = (normal * hidden_gain_ref[:, at]).astype(bf16)
+        result = result + dot(hidden, shrink_ref[at, :])
         grad_hidden = dot_nt(branch, shrink_ref[at, :])
-        normal = normal_ref[:, at].astype(f32)
         start = 2 * width + step * WIDE
         parts_ref[:, start : start + WIDE] = jnp.sum(grad_hidden * normal, axis=0, keepdims=True)
         weighted = grad_hidden * hidden_gain_ref[:, at]
@@ -556,7 +566,7 @@
 
 
 def turn_call(
-    place, branch, hidden, normal, slope, middle, held, mixed_rate, hidden_rate,
+    place, branch, normal, slope, middle, held, mixed_rate, hidden_rate,
     mixed_gain, second_gain, hidden_gain, merge, shrink, expand, planes,
 ):
     slots, tokens, piece = held.shape
@@ -581,7 +591,7 @@
         )
         + (low(tokens // 2, 2 * piece),) * slots
         + (low(tokens // planes, width),) * planes,
-        in_specs=[pl.BlockSpec(memory_space=pltpu.SMEM)] + [vmem_spec()] * 12 + [hbm_spec()] * 2,
+        in_specs=[pl.BlockSpec(memory_space=pltpu.SMEM)] + [vmem_spec()] * 11 + [hbm_spec()] * 2,
         out_specs=(vmem_spec(),) * (4 + slots + planes),
         scratch_shapes=[
             pltpu.VMEM((spread, width), bf16),
@@ -594,63 +604,100 @@
         cost_estimate=cost(9 << 30, 8 << 20),
         name="turn",
     )(
-        place, branch, hidden, normal, slope, middle, held, mixed_rate, hidden_rate,
+        place, branch, normal, slope, middle, held, mixed_rate, hidden_rate,
         mixed_gain.reshape(groups, 1, piece), second_gain.reshape(1, width),
         hidden_gain.reshape(1, spread), merge, shrink, expand,
     )
     return outs[:4], outs[4 : 4 + slots], outs[4 + slots :]
 
 
-def cut_out(keep_ref, give_ref, total_ref, place_ref, bands, steps, rows_each):
-    rank, side = place_ref[2], place_ref[3]
+def cut_out(outs, total_ref, place_ref, bands, steps, rows_each, axis, cut):
+    whole_ref, firsts = outs[0], outs[1:]
+    far_rank, side = place_ref[2] // 2, place_ref[3]
     for at, code in codes(steps):
         other, far = code & 1, code >> 1
-        for out, core in ((keep_ref, 0), (give_ref, 1)):
-            offset = pl.multiple_of((rank ^ (far << 1 | core)) * rows_each, rows_each)
-            start = 0
-            for first, wide in bands:
-                column = pl.multiple_of(first + (side ^ other) * wide, 128)
-                out[at + (slice(None), slice(start, start + wide))] = total_ref[
-                    pl.ds(offset, rows_each), pl.ds(column, wide)
-                ].astype(bf16)
-                start += wide
+        offset = pl.multiple_of((far_rank ^ far) * rows_each, rows_each)
+        parts = []
+        for first, wide in bands:
+            column = pl.multiple_of(first + (side ^ other) * wide, 128)
+            parts.append(
+                total_ref[pl.ds(offset, rows_each), pl.ds(column, wide)].astype(bf16)
+            )
+        value = parts[0] if len(parts) == 1 else jnp.concatenate(parts, axis=1)
+        whole_ref[at] = value
+        for chain, first_ref in enumerate(firsts):
+            if at[chain] == 1:
+                band = slice(0, cut) if chain == 0 else slice(cut, None)
+                first_ref[at[:chain] + at[chain + 1 :]] = (
+                    value[band] if axis == 0 else value[:, band]
+                )
 
 
 def shrink_kernel(
-    place_ref, hidden_ref, branch_ref, keep_ref, give_ref, total_ref, *, steps, rows_each
+    place_ref, hidden_ref, branch_ref, hidden_got_ref, branch_got_ref, *refs, cutting
 ):
-    spread, width = total_ref.shape
+    total_ref = refs[-1]
+    spread, _ = total_ref.shape
+    branch = jnp.concatenate([branch_ref[...], branch_got_ref[...]], axis=0)
     for at in range(0, spread, WIDE):
-        total_ref[at : at + WIDE, :] = dot_tn(hidden_ref[:, at : at + WIDE], branch_ref[...])
-    cut_out(
-        keep_ref, give_ref, total_ref, place_ref, ((0, width // 2),), steps, rows_each
-    )
+        hidden = jnp.concatenate(
+            [hidden_ref[:, at : at + WIDE], hidden_got_ref[:, at : at + WIDE]], axis=0
+        )
+        total_ref[at : at + WIDE, :] = dot_tn(hidden, branch)
+    cut_out(refs[:-1], total_ref, place_ref, **cutting)
 
 
 def expand_kernel(
-    place_ref, second_ref, expanded_ref, mixed_ref, mix_ref, keep_ref, give_ref, total_ref,
-    *, steps, rows_each,
+    place_ref, second_ref, mixed_ref, second_got_ref, mixed_got_ref,
+    expanded_ref, mix_ref, expanded_got_ref, mix_got_ref, *refs, cutting,
 ):
-    width, spread = second_ref.shape[1], expanded_ref.shape[1]
-    turned = second_ref[...].T
+    turned_ref, total_ref = refs[-2:]
+    tokens, spread = expanded_ref.shape
+    width = second_ref.shape[1]
+    core = place_ref[2] % 2
+    rows_each = cutting["rows_each"]
+
+    def left(own_ref, got_ref):
+        turned_ref[:, :tokens] = own_ref[...].astype(f32).T
+        turned_ref[:, tokens:] = got_ref[...].astype(f32).T
+        rows = [
+            turned_ref[pl.ds(pl.multiple_of((2 * i + core) * rows_each, rows_each), rows_each), :]
+            for i in range(width // (2 * rows_each))
+        ]
+        return jnp.concatenate(rows, axis=0).astype(bf16)
+
+    second = left(second_ref, second_got_ref)
     for at in range(0, spread, WIDE):
-        total_ref[:, at : at + WIDE] = dot(turned, expanded_ref[:, at : at + WIDE])
-    total_ref[:, spread:] = dot(mixed_ref[...].T, mix_ref[...])
-    cut_out(
-        keep_ref, give_ref, total_ref, place_ref,
-        ((0, spread // 2), (spread, width // 2)), steps, rows_each,
-    )
-
-
-def outer_call(kernel, place, operands, rows, columns, steps, size, name):
+        band = slice(at, at + WIDE)
+        total_ref[:, band] = dot(
+            second, jnp.concatenate([expanded_ref[:, band], expanded_got_ref[:, band]], axis=0)
+        )
+    mixed = left(mixed_ref, mixed_got_ref)
+    total_ref[:, spread:] = dot(
+        mixed, jnp.concatenate([mix_ref[...], mix_got_ref[...]], axis=0)
+    )
+    cut_out(refs[:-2], total_ref, place_ref, **cutting)
+
+
+def outer_call(kernel, place, operands, rows, columns, bands, steps, size, axis, cut, scratch, name):
     rows_each = rows // size
-    out = jax.ShapeDtypeStruct((2,) * len(steps) + (rows_each, columns // 2), bf16)
+    shape = (rows_each, columns // 2)
+    low = (cut, shape[1]) if axis == 0 else (shape[0], cut)
+    high = (shape[0] - cut, shape[1]) if axis == 0 else (shape[0], shape[1] - cut)
+    pairs = (2,) * (len(steps) - 1)
     return pl.pallas_call(
-        functools.partial(kernel, steps=steps, rows_each=rows_each),
-        out_shape=(out, out),
+        functools.partial(
+            kernel,
+            cutting=dict(bands=bands, steps=steps, rows_each=rows_each, axis=axis, cut=cut),
+        ),
+        out_shape=(
+            jax.ShapeDtypeStruct((2,) + pairs + shape, bf16),
+            jax.ShapeDtypeStruct(pairs + low, bf16),
+            jax.ShapeDtypeStruct(pairs + high, bf16),
+        ),
         in_specs=[pl.BlockSpec(memory_space=pltpu.SMEM)] + [vmem_spec()] * len(operands),
-        out_specs=(vmem_spec(),) * 2,
-        scratch_shapes=[pltpu.VMEM((rows, columns), f32)],
+        out_specs=(vmem_spec(),) * 3,
+        scratch_shapes=scratch + [pltpu.VMEM((rows // 2, columns), f32)],
         compiler_params=params(OUTER_MIB),
         cost_estimate=cost(2 << 30, 10 << 20),
         name=name,
@@ -687,7 +734,7 @@
             start = (part * groups + g) * piece
             joined_out[:, start : start + piece] = held_ref[
                 g, :, part * piece : (part + 1) * piece
-            ].astype(joined_out.dtype)
+            ]
     while len(sums) > 1:
         sums = [sums[i] + sums[i + 1] for i in range(0, len(sums), 2)]
     wide = 3 * piece
@@ -696,12 +743,12 @@
         gains_out[:, r * wide : end] = sums[0][r : r + 1, : end - r * wide]
 
 
-def heads_call(place, blocks, width, gains, dtype):
+def heads_call(place, blocks, width, gains):
     _, rows, wide = blocks[0].shape
     return pl.pallas_call(
         functools.partial(heads_kernel, groups=3 * width // wide, gains=gains),
         out_shape=(
-            jax.ShapeDtypeStruct((rows, 3 * width), dtype),
+            jax.ShapeDtypeStruct((rows, 3 * width), f32),
             jax.ShapeDtypeStruct((1, gains), f32),
         ),
         in_specs=[pl.BlockSpec(memory_space=pltpu.SMEM)] + [vmem_spec()] * len(blocks),
@@ -855,7 +902,8 @@
     sent, cotangent_blocks = lax.optimization_barrier((sent, cotangent_blocks))
     input_rows = arrived.reshape(tokens, width)
     (
-        mixed, middle, second, hidden, normal, slope, held, mixed_rate, hidden_rate, branch,
+        mixed, middle, second, hidden, hidden_give, normal, slope, held, mixed_rate, hidden_rate,
+        branch,
     ) = widen_call(
         place, over_slots(sent), cotangent_blocks, valid, input_rows, mixed_gain, second_gain,
         hidden_gain, merge_weight, expand_weight,
@@ -865,34 +913,25 @@
     plane_bits = list(range(bits_of(slots), bits_of(size)))
     names = ["side"] + row_bits + plane_bits + ["rows", "columns"]
     steps = [0] + row_bits + plane_bits
+    orders = (["side"] + row_bits, row_bits + ["side"])
+    stages = len(orders[0])
 
     def cross(name, value):
         return swap(value, "batch", 1) if name == "side" else swap(value, "blk", 1 << name)
 
-    def chains(axis, cut, keep, arrived):
+    def chains(axis, cut, whole):
         both = []
         for band in (slice(0, cut), slice(cut, None)):
             chain = Halves({axis: band})
-            chain.hold(keep, names)
-            chain.hold(arrived, names)
+            chain.hold(whole, names)
             both.append(chain)
         return both
 
-    shrink_keep, shrink_give = outer_call(
-        shrink_kernel, place, [hidden, branch], spread, width, steps, size, "shrink_outer"
-    )
-    shrink_got = swap(shrink_give, "blk", 1)
-    (expanded, mix, grad_middle, parts), away, results = turn_call(
-        place, branch, hidden, normal, slope, middle, held, mixed_rate, hidden_rate,
-        mixed_gain, second_gain, hidden_gain, merge_weight, shrink_weight, expand_weight, planes,
-    )
-    orders = (["side"] + row_bits, row_bits + ["side"])
-    stages = len(orders[0])
-
-    def depart(pair, at):
-        return [
-            cross(order[at], chain.send(order[at])) for chain, order in zip(pair, orders)
-        ]
+    def sends(pair, at):
+        return [chain.send(order[at]) for chain, order in zip(pair, orders)]
+
+    def crossed(at, values):
+        return [cross(order[at], value) for order, value in zip(orders, values)]
 
     def arrive(pair, at, values):
         for chain, order, value in zip(pair, orders, values):
@@ -921,54 +960,63 @@
         other = swap(value, "batch", 1)
         return jnp.where(side == 0, value, other), jnp.where(side == 0, other, value)
 
+    cut = spread // size // 2
+    shrink_whole, *shrink_firsts = outer_call(
+        shrink_kernel, place,
+        [hidden, branch, swap(hidden_give, "blk", 1), swap(branch, "blk", 1)],
+        spread, width, ((0, width // 2),), steps, size, 0, cut, [], "shrink_outer",
+    )
+    shrink_sent = crossed(0, shrink_firsts)
+    second_got, mixed_got = swap(second, "blk", 1), swap(mixed, "blk", 1)
+    (expanded, mix, grad_middle, parts), away, results = turn_call(
+        place, branch, normal, slope, middle, held, mixed_rate, hidden_rate,
+        mixed_gain, second_gain, hidden_gain, merge_weight, shrink_weight, expand_weight, planes,
+    )
+    shrink_sent, second_got, mixed_got, expanded, mix = lax.optimization_barrier(
+        (shrink_sent, second_got, mixed_got, expanded, mix)
+    )
+    shrink_chains = chains("rows", cut, shrink_whole)
+    arrive(shrink_chains, 0, shrink_sent)
+
     returned = over_slots(away)
-    expand_keep, expand_give = outer_call(
-        expand_kernel, place, [second, expanded, mixed, mix], width, spread + width, steps, size,
-        "expand_outer",
-    )
-    returned, expand_give, shrink_got, results = lax.optimization_barrier(
-        (returned, expand_give, shrink_got, results)
-    )
-    shrink_chains = chains("rows", spread // size // 2, shrink_keep, shrink_got)
-    expand_got = swap(expand_give, "blk", 1)
-    shrink_sent = depart(shrink_chains, 0)
+    expanded_got, mix_got = swap(expanded, "blk", 1), swap(mix, "blk", 1)
+    returned, expanded_got, mix_got = lax.optimization_barrier((returned, expanded_got, mix_got))
+    cut = ((spread + width) // 4 + 127) // 128 * 128
+    expand_whole, *expand_firsts = outer_call(
+        expand_kernel, place,
+        [second, mixed, second_got, mixed_got, expanded, mix, expanded_got, mix_got],
+        width, spread + width, ((0, spread // 2), (spread, width // 2)), steps, size, 1, cut,
+        [pltpu.VMEM((width, 2 * tokens), f32)], "expand_outer",
+    )
+    for at in range(1, stages):
+        shrink_sent = crossed(at, sends(shrink_chains, at))
+        if at < stages - 1:
+            arrive(shrink_chains, at, shrink_sent)
+    expand_firsts, results = lax.optimization_barrier((expand_firsts, results))
     result_blocks = [results[0]] + [
         swap(results[k], "blk", k * slots) for k in range(1, planes)
     ]
-    rows_each = width // size
-    joined_sides = 2 if batches > 1 and rows_each % 16 == 0 else 1
-    joined_keep, joined_give, branch_keep, branch_give = backward_call(
+    returned, expand_firsts, shrink_sent = lax.optimization_barrier(
+        (returned, expand_firsts, shrink_sent)
+    )
+    arrive(shrink_chains, stages - 1, shrink_sent)
+    expand_sent = crossed(0, expand_firsts)
+    shrink_both = plane_depart(shrink_chains, plane_bits[0], -2)
+    joined_part, branch_keep, branch_give = backward_call(
         place, *in_hbm(first, joined), own_weight, first_gain.reshape(width, 1), parts,
-        returned, in_hbm(*shares), planes, joined_sides,
+        returned, in_hbm(*shares), planes,
     )
     (
-        joined_give, branch_give, shrink_sent, expand_got, result_blocks,
+        joined_part, branch_give, shrink_both, expand_sent, result_blocks,
     ) = lax.optimization_barrier(
-        (joined_give, branch_give, shrink_sent, expand_got, result_blocks)
-    )
-    expand_chains = chains(
-        "columns", ((spread + width) // 4 + 127) // 128 * 128, expand_keep, expand_got
-    )
-    arrive(shrink_chains, 0, shrink_sent)
-
-    joined_held, batch_bits = [joined_keep], list(range(bits_of(batches)))
-    branch_got = swap(branch_give, "blk", 1)
-    for at in range(1, stages):
-        shrink_sent = depart(shrink_chains, at)
-        if at < stages - 1:
-            arrive(shrink_chains, at, shrink_sent)
-    expand_sent = depart(expand_chains, 0)
-    if joined_sides > 1:
-        joined_held.append(swap(joined_give, "batch", 1))
-        batch_bits = batch_bits[1:]
-    shrink_sent, joined_held, branch_got = lax.optimization_barrier(
-        (shrink_sent, joined_held, branch_got)
-    )
-    arrive(shrink_chains, stages - 1, shrink_sent)
+        (joined_part, branch_give, shrink_both, expand_sent, result_blocks)
+    )
+    plane_arrive(shrink_chains, plane_bits[0], -2, shrink_both)
+    expand_chains = chains("columns", cut, expand_whole)
+    arrive(expand_chains, 0, expand_sent)
 
     blocks = planes * slots
-    gains = sum(v[blocks].astype(f32) for v in joined_held)
-    joined_sum = [v[:blocks] for v in joined_held]
+    gains, joined_sum = joined_part[blocks].astype(f32), [joined_part[:blocks]]
 
     def joined_depart(bit):
         half = joined_sum[0].shape[0] // 2
@@ -983,68 +1031,71 @@
         )
 
     joined_got = joined_depart(plane_bits[0])
-    shrink_both = plane_depart(shrink_chains, plane_bits[0], -2)
+    branch_got = swap(branch_give, "blk", 1)
+    for at in range(1, stages):
+        expand_sent = crossed(at, sends(expand_chains, at))
+        if at < stages - 1:
+            arrive(expand_chains, at, expand_sent)
+    for bit in plane_bits[1:]:
+        shrink_both = plane_depart(shrink_chains, bit, -2)
+        if bit != plane_bits[-1]:
+            plane_arrive(shrink_chains, bit, -2, shrink_both)
+    joined_got, branch_got, expand_sent, shrink_both = lax.optimization_barrier(
+        (joined_got, branch_got, expand_sent, shrink_both)
+    )
+    joined_sum, gains = joined_arrive(joined_got)
+    arrive(expand_chains, stages - 1, expand_sent)
+    plane_arrive(shrink_chains, plane_bits[-1], -2, shrink_both)
+
     branch_held, prefixes = [branch_keep, branch_got], [(), ()]
     for bit in row_bits:
         give = sum(v[p + (1,)].astype(f32) for v, p in zip(branch_held, prefixes)).astype(bf16)
         prefixes = [p + (0,) for p in prefixes] + [()]
         branch_held.append(swap(give, "blk", 1 << bit))
-    joined_got, shrink_both, expand_sent, branch_held = lax.optimization_barrier(
-        (joined_got, shrink_both, expand_sent, branch_held)
+    expand_both = plane_depart(expand_chains, plane_bits[0], -1)
+    for bit in plane_bits[1:]:
+        joined_got = joined_depart(bit)
+        if bit != plane_bits[-1]:
+            joined_sum, gains = joined_arrive(joined_got)
+    joined_got, expand_both, branch_held = lax.optimization_barrier(
+        (joined_got, expand_both, branch_held)
     )
     joined_sum, gains = joined_arrive(joined_got)
-    plane_arrive(shrink_chains, plane_bits[0], -2, shrink_both)
-    arrive(expand_chains, 0, expand_sent)
-
-    for at in range(1, stages):
-        expand_sent = depart(expand_chains, at)
-        if at < stages - 1:
-            arrive(expand_chains, at, expand_sent)
+    plane_arrive(expand_chains, plane_bits[0], -1, expand_both)
+
     input_blocks = input_call(
         input_rows, grad_middle, first_gain, branch_held, prefixes, planes
     )
-    for bit in plane_bits[1:]:
-        joined_sum, gains = joined_arrive(joined_depart(bit))
-        plane_arrive(shrink_chains, bit, -2, plane_depart(shrink_chains, bit, -2))
-    shrink_last, joined_last = closed(shrink_chains, -2), jnp.concatenate(
-        [sum(v.astype(f32) for v in joined_sum), gains[None]]
-    ).astype(bf16)
-    expand_sent, shrink_last, joined_last = lax.optimization_barrier(
-        (expand_sent, shrink_last, joined_last)
-    )
-    arrive(expand_chains, stages - 1, expand_sent)
-
-    expand_both = plane_depart(expand_chains, plane_bits[0], -1)
     input_blocks = [input_blocks[0]] + [
         swap(input_blocks[k], "blk", k * slots) for k in range(1, planes)
     ]
-    for bit in batch_bits:
+    joined_last = jnp.concatenate(
+        [sum(v.astype(f32) for v in joined_sum), gains[None]]
+    ).astype(bf16)
+    for bit in range(bits_of(batches)):
         joined_last = total([joined_last, swap(joined_last, "batch", 1 << bit)]).astype(bf16)
-    shrink_lower, shrink_upper = both_sides(shrink_last)
-    shrink_grad = jnp.concatenate([shrink_lower, shrink_upper], axis=1).astype(f32)
-    joined_half, gain_row = heads_call(
+    for bit in plane_bits[1:]:
+        expand_both = plane_depart(expand_chains, bit, -1)
+        if bit != plane_bits[-1]:
+            plane_arrive(expand_chains, bit, -1, expand_both)
+    joined_last, expand_both = lax.optimization_barrier((joined_last, expand_both))
+    plane_arrive(expand_chains, plane_bits[-1], -1, expand_both)
+
+    joined_grad, gain_row = heads_call(
         place,
         [jnp.stack([joined_last[0], joined_last[slots]])]
         + [
             swap(jnp.stack([joined_last[u], joined_last[slots]]), "blk", u)
             for u in range(1, slots)
         ],
-        width, 3 * width + spread, f32 if joined_sides == 1 else bf16,
-    )
-    expand_both, input_blocks, joined_half, shrink_grad = lax.optimization_barrier(
-        (expand_both, input_blocks, joined_half, shrink_grad)
-    )
-    plane_arrive(expand_chains, plane_bits[0], -1, expand_both)
-    for bit in plane_bits[1:]:
-        plane_arrive(expand_chains, bit, -1, plane_depart(expand_chains, bit, -1))
+        width, 3 * width + spread,
+    )
+    shrink_lower, shrink_upper = both_sides(closed(shrink_chains, -2))
+    shrink_grad = jnp.concatenate([shrink_lower, shrink_upper], axis=1).astype(f32)
     expand_lower, expand_upper = both_sides(closed(expand_chains, -1))
     cut = spread // 2
     expand_grad = jnp.concatenate([expand_lower[:, :cut], expand_upper[:, :cut]], axis=1)
     merge_grad = jnp.concatenate([expand_lower[:, cut:], expand_upper[:, cut:]], axis=1)
-    if joined_sides == 1:
-        joined_grad = joined_half
-    else:
-        joined_grad = jnp.concatenate(both_sides(joined_half), axis=0).astype(f32)
     layer_result = settle_call(place, result_blocks).reshape(layer_input.shape)
     input_grad = settle_call(place, input_blocks).reshape(layer_input.shape)
     gain_row = gain_row[0]

time: 216 us -> 198 us (0.917)
  waiting for transfers between devices: 73.4 us -> 62.4 us
  other arithmetic: 24.7 us -> 15.4 us
  starting transfers between devices: 46.1 us -> 49.1 us
    ppermute x46 -> x49, waiting for transfers between devices: 73.4 us -> 62.4 us  [swap(): return lax.ppermute(value, axis, [(i, i ^ bits) for i in range(size)])]
    convert_element_type x13 -> x9, other arithmetic: 10.9 us -> 2.75 us  [send(): return self.summed({name: 1}).astype(bf16)]
    ppermute x46 -> x49, starting transfers between devices: 46.1 us -> 49.1 us  [swap(): return lax.ppermute(value, axis, [(i, i ^ bits) for i in range(size)])]
    unnamed x72 -> x62, local copies, waits for them, and re-layouts: 4.98 us -> 4.95 us
  transfers between devices with their start and end apart: 46 -> 49, of which waited for: 19 -> 19; matrix products, arithmetic and copies ran while one was open for 10% -> 8% of each run, Pallas kernels for 22% -> 25%
where the time goes in v3:
time: 198 us; the launch traced here: 195 us
  waiting for transfers between devices  62.4 us (32%)
  Pallas kernels  55.7 us (28%)
  starting transfers between devices  49.1 us (25%)
  other arithmetic  15.4 us (8%)
  local copies, waits for them, and re-layouts  10.7 us (5%)
    ppermute x49, waiting for transfers between devices, swap(): return lax.ppermute(value, axis, [(i, i ^ bits) for i in range(size)])  62.4 us
    ppermute x49, starting transfers between devices, swap(): return lax.ppermute(value, axis, [(i, i ^ bits) for i in range(size)])  49.1 us
    pallas_call x1, Pallas kernels, forward_call(): pl.pallas_call(kernel, out_shape=(pltpu.HBM((length, width), bf16), pltpu...  13.9 us
    pallas_call x1, Pallas kernels, backward_call(): pl.pallas_call(kernel, out_shape=(jax.ShapeDtypeStruct((planes * slots +...  13.9 us
    pallas_call x1, Pallas kernels, turn_call(): pl.pallas_call(functools.partial(turn_kernel, slots=slots, planes=planes,...  10.5 us
    pallas_call x1, Pallas kernels, widen_call(): pl.pallas_call(functools.partial(widen_kernel, slots=slots, planes=len(bl...  7.14 us
    pallas_call x2, Pallas kernels, outer_call(): pl.pallas_call(functools.partial(kernel, cutting=dict(bands=bands, steps=...  5.48 us
    unnamed x62, local copies, waits for them, and re-layouts  4.95 us
  transfers between devices with their start and end apart: 49, of which 19 were waited for; matrix products, arithmetic and copies ran while one was open for 8% of the time, Pallas kernels for 25%

profile of v3, /device:TPU:0, one launch (start us, length us, event | category | flops | bytes accessed | tf_op | source)
XLA Modules:
  0.0 194.9 jit_solution(8036341719987978698)
XLA Ops:
  1.8 3.1 %collective-permute-start = (bf16[64,768]{1,0:T(8,128)(2,1)S(1)}, bf16[64,768]{1,0:T(8,128)(2,1)S(1)}, u32[]{:S(2)}, u32[]{:S(2)}) collective-permute-start(bf16[64,768]{1,0:T(8,128)(2,1)S(1)} %get-tuple-element.251), channel_id=1, source_target_pairs={{0,4},{1,5},{2,6},{3,7},{4,0},{5,1},{6,2},{7,3},{8,12},{9,13},{10,... | collective-permute-start | bytes 294920 | tf_op jit(solution)/shard_map/ppermute | solution.py:787
  4.9 2.6 %collective-permute-start.1 = (bf16[64,768]{1,0:T(8,128)(2,1)S(1)}, bf16[64,768]{1,0:T(8,128)(2,1)S(1)}, u32[]{:S(2)}, u32[]{:S(2)}) collective-permute-start(bf16[64,768]{1,0:T(8,128)(2,1)S(1)} %get-tuple-element.253), channel_id=1, source_target_pairs={{0,8},{1,9},{2,10},{3,11},{4,12},{5,13},{6,14},{7,15},{8,0},{9,1},... | collective-permute-start | bytes 294920 | tf_op jit(solution)/shard_map/ppermute | solution.py:787
  9.0 2.0 %constant_dynamic-slice_fusion.2 = (bf16[768,192]{1,0:T(8,128)(2,1)S(1)}, bf16[768,192]{1,0:T(8,128)(2,1)S(1)}, bf16[768,192]{1,0:T(8,128)(2,1)S(1)}) fusion(bf16[768,2304]{1,0:T(8,128)(2,1)} %param.14, s32[]{:T(128)S(6)} %select_n.79, s32[]{:T(128)S(6)} %select_n.81, s32[]{:T(128)S(6)} %select_n.80), kind=kLoop, calls=%fused_computation.98 | loop fusion | bytes 1769484 | tf_op jit(solution)/shard_map/dynamic_slice | solution.py:882
  11.5 3.8 %collective-permute-done.1 = bf16[64,768]{1,0:T(8,128)(2,1)S(1)} collective-permute-done((bf16[64,768]{1,0:T(8,128)(2,1)S(1)}, bf16[64,768]{1,0:T(8,128)(2,1)S(1)}, u32[]{:S(2)}, u32[]{:S(2)}) %collective-permute-start.1) | collective-permute-done | bytes 98336 | tf_op jit(solution)/shard_map/ppermute | solution.py:787
  16.9 7.6 %collective-permute-done.4.refs_6_ = bf16[4,64,768]{2,1,0:T(8,128)(2,1)} collective-permute-done((bf16[4,64,768]{2,1,0:T(8,128)(2,1)S(1)}, bf16[4,64,768]{2,1,0:T(8,128)(2,1)}, u32[]{:S(2)}, u32[]{:S(2)}) %collective-permute-start.4) | collective-permute-done | bytes 393248 | tf_op jit(solution)/shard_map/ppermute | solution.py:787
  24.9 2.4 %collective-permute-start.6 = (bf16[64,768]{1,0:T(8,128)(2,1)S(1)}, bf16[64,768]{1,0:T(8,128)(2,1)S(1)}, u32[]{:S(2)}, u32[]{:S(2)}) collective-permute-start(bf16[64,768]{1,0:T(8,128)(2,1)S(1)} %get-tuple-element.248), channel_id=1, source_target_pairs={{0,4},{1,5},{2,6},{3,7},{4,0},{5,1},{6,2},{7,3},{8,12},{9,13},{10,... | collective-permute-start | bytes 294920 | tf_op jit(solution)/shard_map/ppermute | solution.py:787
  29.8 13.9 %attention_forward.1 = (bf16[1024,768]{1,0:T(8,128)(2,1)}, bf16[9,1024,64]{2,1,0:T(8,128)(2,1)}, bf16[128,384]{1,0:T(8,128)(2,1)S(1)}, bf16[128,384]{1,0:T(8,128...) custom-call(s32[4]{0:T(128)S(1)} %pad_add_fusion.refs_0_.place_ref, ...), custom_call_target="tpu_custom_call" | custom-call | flops 8589934592 | bytes 8388608 | tf_op jit(solution)/shard_map/attention_forward/pallas_call | solution.py:155
  46.6 3.8 %collective-permute-done.10.refs_3_ = bf16[128,384]{1,0:T(8,128)(2,1)S(1)} collective-permute-done((bf16[128,384]{1,0:T(8,128)(2,1)}, bf16[128,384]{1,0:T(8,128)(2,1)S(1)}, u32[]{:S(2)}, u32[]{:S(2)}) %collective-permute-start.10) | collective-permute-done | bytes 98336 | tf_op jit(solution)/shard_map/ppermute | solution.py:787
  52.5 7.1 %widen.1 = (bf16[256,768]{1,0:T(8,128)(2,1)S(1)}, f32[256,768]{1,0:T(8,128)S(1)}, bf16[256,768]{1,0:T(8,128)(2,1)S(1)}, bf16[256,1536]{1,0:T(8,128)(2,1)S(1)}, b...) custom-call(s32[4]{0:T(128)S(1)} %pad_add_fusion.refs_0_.place_ref, ...), custom_call_target="tpu_custom_call" | custom-call | flops 6442450944 | bytes 6291456 | tf_op jit(solution)/shard_map/widen/pallas_call | solution.py:433
  62.5 2.5 %shrink_outer.1 = (bf16[2,2,2,2,192,384]{5,4,3,2,1,0:T(8,128)(2,1)S(1)}, bf16[2,2,2,96,384]{4,3,2,1,0:T(8,128)(2,1)S(1)}, bf16[2,2,2,96,384]{4,3,2,1,0:T(8,128)(2,1)S(1)}) custom-call(s32[4]{0:T(128)S(1)} %pad_add_fusion.refs_0_.place_ref, bf16[256,1536]{1,0:T(8,128)(2,1)S(1)} %get-tuple-element.155.hidden_ref, ...), custom_call_target="tpu_custom_call" | custom-call | flops 2147483648 | bytes 10485760 | tf_op jit(solution)/shard_map/shrink_outer/pallas_call | solution.py:688
  68.1 10.5 %turn.1 = (bf16[256,3072]{1,0:T(8,128)(2,1)S(1)}, bf16[256,768]{1,0:T(8,128)(2,1)S(1)}, f32[256,768]{1,0:T(8,128)S(1)}, f32[1,4608]{1,0:T(1,128)S(1)}, bf16[128,...) custom-call(s32[4]{0:T(128)S(1)} %pad_add_fusion.refs_0_.place_ref, ...), custom_call_target="tpu_custom_call" | custom-call | flops 9663676416 | bytes 8388608 | tf_op jit(solution)/shard_map/turn/pallas_call | solution.py:582
  78.7 1.9 collective-permute-done.17
  89.3 3.0 %expand_outer.1 = (bf16[2,2,2,2,48,1920]{5,4,3,2,1,0:T(8,128)(2,1)S(1)}, bf16[2,2,2,48,1024]{4,3,2,1,0:T(8,128)(2,1)S(1)}, bf16[2,2,2,48,896]{4,3,2,1,0:T(8,128)(2,1)S(1)}) custom-call(s32[4]{0:T(128)S(1)} %pad_add_fusion.refs_0_.place_ref, bf16[256,768]{1,0:T(8,128)(2,1)S(1)} %get-tuple-element.159.second_ref, ...), custom_call_target="tpu_custom_call" | custom-call | flops 2147483648 | bytes 10485760 | tf_op jit(solution)/shard_map/expand_outer/pallas_call | solution.py:688
  92.3 3.7 %collective-permute-done.23 = bf16[2,2,96,384]{3,2,1,0:T(8,128)(2,1)S(1)} collective-permute-done((bf16[2,2,96,384]{3,2,1,0:T(8,128)(2,1)S(1)}, bf16[2,2,96,384]{3,2,1,0:T(8,128)(2,1)S(1)}, u32[]{:S(2)}, u32[]{:S(2)}) %collective-permute-start.23) | collective-permute-done | bytes 294944 | tf_op jit(solution)/shard_map/ppermute | solution.py:787
  100.5 2.0 %collective-permute-start.29 = (bf16[64,768]{1,0:T(8,128)(2,1)S(1)}, bf16[64,768]{1,0:T(8,128)(2,1)S(1)}, u32[]{:S(2)}, u32[]{:S(2)}) collective-permute-start(bf16[64,768]{1,0:T(8,128)(2,1)S(1)} %get-tuple-element.200), channel_id=1, source_target_pairs={{0,8},{1,9},{2,10},{3,11},{4,12},{5,13},{6,14},{7,15},{8,0},{9,1},... | collective-permute-start | bytes 294920 | tf_op jit(solution)/shard_map/ppermute | solution.py:787
  103.1 1.9 collective-permute-start.30
  105.0 13.9 %attention_backward.1 = (bf16[17,48,576]{2,1,0:T(8,128)(2,1)S(1)}, bf16[2,256,768]{2,1,0:T(8,128)(2,1)S(1)}, bf16[2,256,768]{2,1,0:T(8,128)(2,1)S(1)}) custom-call(s32[4]{0:T(128)S(1)} %pad_add_fusion.refs_0_.place_ref, bf16[1024,768]{1,0:T(8,128)(2,1)} %get-tuple-element.127.refs_1_, bf16[9,1024,64]{2,1,0:T(8,128)(2,1)} %get-tuple-element.128.refs_2_, ...), custom_call_target="tpu_custom_call" | custom-call | flops 10737418240 | bytes 10485760 | tf_op jit(solution)/shard_map/attention_backward/pallas_call | solution.py:295
  119.4 2.5 %collective-permute-start.33 = (bf16[2,2,48,1024]{3,2,1,0:T(8,128)(2,1)S(1)}, bf16[2,2,48,1024]{3,2,1,0:T(8,128)(2,1)S(1)}, u32[]{:S(2)}, u32[]{:S(2)}) collective-permute-start(bf16[2,2,48,1024]{3,2,1,0:T(8,128)(2,1)S(1)} %fusion), channel_id=1, source_target_pairs={{0,2},{1,3},{2,0},{3,1},{4,6},{5,7},{6,4},{7,5},{8,10},{9,11},{10,... | collective-permute-start | bytes 1179656 | tf_op jit(solution)/shard_map/ppermute | solution.py:787
  122.2 2.0 %collective-permute-start.35 = (bf16[192,384]{1,0:T(8,128)(2,1)S(1)}, bf16[192,384]{1,0:T(8,128)(2,1)S(1)}, u32[]{:S(2)}, u32[]{:S(2)}) collective-permute-start(bf16[192,384]{1,0:T(8,128)(2,1)S(1)} %pad_maximum_fusion.11), channel_id=1, source_target_pairs={{0,8},{1,9},{2,10},{3,11},{4,12},{5,13},{6,14},{7,15},{8,0},{9,1},... | collective-permute-start | bytes 442376 | tf_op jit(solution)/shard_map/ppermute | solution.py:787
  124.2 7.6 %collective-permute-done.35 = bf16[192,384]{1,0:T(8,128)(2,1)S(1)} collective-permute-done((bf16[192,384]{1,0:T(8,128)(2,1)S(1)}, bf16[192,384]{1,0:T(8,128)(2,1)S(1)}, u32[]{:S(2)}, u32[]{:S(2)}) %collective-permute-start.35) | collective-permute-done | bytes 147488 | tf_op jit(solution)/shard_map/ppermute | solution.py:787
  147.7 7.4 %collective-permute-done.36 = bf16[5,48,576]{2,1,0:T(8,128)(2,1)} collective-permute-done((bf16[5,48,576]{2,1,0:T(8,128)(2,1)}, bf16[5,48,576]{2,1,0:T(8,128)(2,1)}, u32[]{:S(2)}, u32[]{:S(2)}) %collective-permute-start.36) | collective-permute-done | bytes 276512 | tf_op jit(solution)/shard_map/ppermute | solution.py:787
  161.7 2.0 %collective-permute-start.40 = (bf16[64,768]{1,0:T(8,128)(2,1)S(1)}, bf16[64,768]{1,0:T(8,128)(2,1)S(1)}, u32[]{:S(2)}, u32[]{:S(2)}) collective-permute-start(bf16[64,768]{1,0:T(8,128)(2,1)S(1)} %get-tuple-element.223), channel_id=1, source_target_pairs={{0,8},{1,9},{2,10},{3,11},{4,12},{5,13},{6,14},{7,15},{8,0},{9,1},... | collective-permute-start | bytes 294920 | tf_op jit(solution)/shard_map/ppermute | solution.py:787
  163.7 2.4 %collective-permute-start.41 = (bf16[64,768]{1,0:T(8,128)(2,1)S(1)}, bf16[64,768]{1,0:T(8,128)(2,1)S(1)}, u32[]{:S(2)}, u32[]{:S(2)}) collective-permute-start(bf16[64,768]{1,0:T(8,128)(2,1)S(1)} %get-tuple-element.224), channel_id=1, source_target_pairs={{0,12},{1,13},{2,14},{3,15},{4,8},{5,9},{6,10},{7,11},{8,4},{9,5},... | collective-permute-start | bytes 294920 | tf_op jit(solution)/shard_map/ppermute | solution.py:787
  166.3 13.6 %collective-permute-done.43 = bf16[48,1920]{1,0:T(8,128)(2,1)S(1)} collective-permute-done((bf16[48,1920]{1,0:T(8,128)(2,1)S(1)}, bf16[48,1920]{1,0:T(8,128)(2,1)S(1)}, u32[]{:S(2)}, u32[]{:S(2)}) %collective-permute-start.43) | collective-permute-done | bytes 184352 | tf_op jit(solution)/shard_map/ppermute | solution.py:787
  (206 shorter events, 70.0 us)
Async XLA Ops:
  4.9 10.4 %collective-permute-start.1 = (bf16[64,768]{1,0:T(8,128)(2,1)S(1)}, bf16[64,768]{1,0:T(8,128)(2,1)S(1)}, u32[]{:S(2)}, u32[]{:S(2)}) collective-permute-start(bf16[64,768]{1,0:T(8,128)(2,1)S(1)} %get-tuple-element.253), channel_id=1, source_target_pairs={{0,8},{1,9},{2,10},{3,11},{4,12},{5,13},{6,14},{7,15},{8,0},{9,1},... | collective-permute-start | bytes 294920 | tf_op jit(solution)/shard_map/ppermute | solution.py:787
  16.9 12.9 %collective-permute-start.3 = (bf16[4,64,768]{2,1,0:T(8,128)(2,1)S(1)}, bf16[4,64,768]{2,1,0:T(8,128)(2,1)}, u32[]{:S(2)}, u32[]{:S(2)}) collective-permute-start(bf16[4,64,768]{2,1,0:T(8,128)(2,1)S(1)} %pad_maximum_fusion.1.refs_4_), channel_id=1, source_target_pairs={{0,1},{1,0},{2,3},{3,2},{4,5},{5,4},{6,7},{7,6},{8,9},{9,8},{10,11... | collective-permute-start | bytes 1179656 | tf_op jit(solution)/shard_map/ppermute | solution.py:787
  24.9 19.5 %collective-permute-start.6 = (bf16[64,768]{1,0:T(8,128)(2,1)S(1)}, bf16[64,768]{1,0:T(8,128)(2,1)S(1)}, u32[]{:S(2)}, u32[]{:S(2)}) collective-permute-start(bf16[64,768]{1,0:T(8,128)(2,1)S(1)} %get-tuple-element.248), channel_id=1, source_target_pairs={{0,4},{1,5},{2,6},{3,7},{4,0},{5,1},{6,2},{7,3},{8,12},{9,13},{10,... | collective-permute-start | bytes 294920 | tf_op jit(solution)/shard_map/ppermute | solution.py:787
  27.3 17.1 %collective-permute-start.7 = (bf16[64,768]{1,0:T(8,128)(2,1)S(1)}, bf16[64,768]{1,0:T(8,128)(2,1)S(1)}, u32[]{:S(2)}, u32[]{:S(2)}) collective-permute-start(bf16[64,768]{1,0:T(8,128)(2,1)S(1)} %get-tuple-element.247), channel_id=1, source_target_pairs={{0,8},{1,9},{2,10},{3,11},{4,12},{5,13},{6,14},{7,15},{8,0},{9,1},... | collective-permute-start | bytes 294920 | tf_op jit(solution)/shard_map/ppermute | solution.py:787
  28.4 16.0 %collective-permute-start.8 = (bf16[64,768]{1,0:T(8,128)(2,1)S(1)}, bf16[64,768]{1,0:T(8,128)(2,1)S(1)}, u32[]{:S(2)}, u32[]{:S(2)}) collective-permute-start(bf16[64,768]{1,0:T(8,128)(2,1)S(1)} %get-tuple-element.246), channel_id=1, source_target_pairs={{0,12},{1,13},{2,14},{3,15},{4,8},{5,9},{6,10},{7,11},{8,4},{9,5},... | collective-permute-start | bytes 294920 | tf_op jit(solution)/shard_map/ppermute | solution.py:787
  60.2 18.5 %collective-permute-start.19 = (bf16[256,768]{1,0:T(8,128)(2,1)S(1)}, bf16[256,768]{1,0:T(8,128)(2,1)S(1)}, u32[]{:S(2)}, u32[]{:S(2)}) collective-permute-start(bf16[256,768]{1,0:T(8,128)(2,1)S(1)} %get-tuple-element.159.second_ref), channel_id=1, source_target_pairs={{0,1},{1,0},{2,3},{3,2},{4,5},{5,4},{6,7},{7,6},{8,9},{9,8},{10,11... | collective-permute-start | bytes 1179656 | tf_op jit(solution)/shard_map/ppermute | solution.py:787
  60.4 18.2 %collective-permute-start.20 = (bf16[256,768]{1,0:T(8,128)(2,1)S(1)}, bf16[256,768]{1,0:T(8,128)(2,1)S(1)}, u32[]{:S(2)}, u32[]{:S(2)}) collective-permute-start(bf16[256,768]{1,0:T(8,128)(2,1)S(1)} %get-tuple-element.160.mixed_ref), channel_id=1, source_target_pairs={{0,1},{1,0},{2,3},{3,2},{4,5},{5,4},{6,7},{7,6},{8,9},{9,8},{10,11... | collective-permute-start | bytes 1179656 | tf_op jit(solution)/shard_map/ppermute | solution.py:787
  65.0 15.6 %collective-permute-start.17 = (bf16[2,2,2,96,384]{4,3,2,1,0:T(8,128)(2,1)S(1)}, bf16[2,2,2,96,384]{4,3,2,1,0:T(8,128)(2,1)S(1)}, u32[]{:S(2)}, u32[]{:S(2)}) collective-permute-start(bf16[2,2,2,96,384]{4,3,2,1,0:T(8,128)(2,1)S(1)} %get-tuple-element.157), channel_id=1, source_target_pairs={{0,16},{16,0},{1,17},{17,1},{2,18},{18,2},{3,19},{19,3},{4,20},{20... | collective-permute-start | bytes 1769480 | tf_op jit(solution)/shard_map/ppermute | solution.py:787
  66.6 15.2 %collective-permute-start.18 = (bf16[2,2,2,96,384]{4,3,2,1,0:T(8,128)(2,1)S(1)}, bf16[2,2,2,96,384]{4,3,2,1,0:T(8,128)(2,1)S(1)}, u32[]{:S(2)}, u32[]{:S(2)}) collective-permute-start(bf16[2,2,2,96,384]{4,3,2,1,0:T(8,128)(2,1)S(1)} %get-tuple-element.158), channel_id=1, source_target_pairs={{0,2},{1,3},{2,0},{3,1},{4,6},{5,7},{6,4},{7,5},{8,10},{9,11},{10,... | collective-permute-start | bytes 1769480 | tf_op jit(solution)/shard_map/ppermute | solution.py:787
  97.4 21.5 %collective-permute-start.25 = (bf16[2,192,384]{2,1,0:T(8,128)(2,1)S(1)}, bf16[2,192,384]{2,1,0:T(8,128)(2,1)S(1)}, u32[]{:S(2)}, u32[]{:S(2)}) collective-permute-start(bf16[2,192,384]{2,1,0:T(8,128)(2,1)S(1)} %pad_maximum_fusion.5), channel_id=1, source_target_pairs={{0,4},{1,5},{2,6},{3,7},{4,0},{5,1},{6,2},{7,3},{8,12},{9,13},{10,... | collective-permute-start | bytes 884744 | tf_op jit(solution)/shard_map/ppermute | solution.py:787
  98.5 20.5 %collective-permute-start.26 = (bf16[2,2,2,48,1024]{4,3,2,1,0:T(8,128)(2,1)S(1)}, bf16[2,2,2,48,1024]{4,3,2,1,0:T(8,128)(2,1)S(1)}, u32[]{:S(2)}, u32[]{:S(2)}) collective-permute-start(bf16[2,2,2,48,1024]{4,3,2,1,0:T(8,128)(2,1)S(1)} %get-tuple-element.196), channel_id=1, source_target_pairs={{0,16},{16,0},{1,17},{17,1},{2,18},{18,2},{3,19},{19,3},{4,20},{20... | collective-permute-start | bytes 2359304 | tf_op jit(solution)/shard_map/ppermute | solution.py:787
  99.0 19.9 %collective-permute-start.27 = (bf16[2,2,2,48,896]{4,3,2,1,0:T(8,128)(2,1)S(1)}, bf16[2,2,2,48,896]{4,3,2,1,0:T(8,128)(2,1)S(1)}, u32[]{:S(2)}, u32[]{:S(2)}) collective-permute-start(bf16[2,2,2,48,896]{4,3,2,1,0:T(8,128)(2,1)S(1)} %get-tuple-element.197), channel_id=1, source_target_pairs={{0,2},{1,3},{2,0},{3,1},{4,6},{5,7},{6,4},{7,5},{8,10},{9,11},{10,... | collective-permute-start | bytes 2064392 | tf_op jit(solution)/shard_map/ppermute | solution.py:787
  100.5 18.4 %collective-permute-start.29 = (bf16[64,768]{1,0:T(8,128)(2,1)S(1)}, bf16[64,768]{1,0:T(8,128)(2,1)S(1)}, u32[]{:S(2)}, u32[]{:S(2)}) collective-permute-start(bf16[64,768]{1,0:T(8,128)(2,1)S(1)} %get-tuple-element.200), channel_id=1, source_target_pairs={{0,8},{1,9},{2,10},{3,11},{4,12},{5,13},{6,14},{7,15},{8,0},{9,1},... | collective-permute-start | bytes 294920 | tf_op jit(solution)/shard_map/ppermute | solution.py:787
  103.1 15.8 %collective-permute-start.30 = (bf16[64,768]{1,0:T(8,128)(2,1)S(1)}, bf16[64,768]{1,0:T(8,128)(2,1)S(1)}, u32[]{:S(2)}, u32[]{:S(2)}) collective-permute-start(bf16[64,768]{1,0:T(8,128)(2,1)S(1)} %get-tuple-element.201), channel_id=1, source_target_pairs={{0,12},{1,13},{2,14},{3,15},{4,8},{5,9},{6,10},{7,11},{8,4},{9,5},... | collective-permute-start | bytes 294920 | tf_op jit(solution)/shard_map/ppermute | solution.py:787
  119.0 15.0 %collective-permute-start.31 = (bf16[9,48,576]{2,1,0:T(8,128)(2,1)S(1)}, bf16[9,48,576]{2,1,0:T(8,128)(2,1)S(1)}, u32[]{:S(2)}, u32[]{:S(2)}) collective-permute-start(bf16[9,48,576]{2,1,0:T(8,128)(2,1)S(1)} %concatenate.44), channel_id=1, source_target_pairs={{0,4},{1,5},{2,6},{3,7},{4,0},{5,1},{6,2},{7,3},{8,12},{9,13},{10,... | collective-permute-start | bytes 1493000 | tf_op jit(solution)/shard_map/ppermute | solution.py:787
  119.3 14.7 %collective-permute-start.32 = (bf16[2,256,768]{2,1,0:T(8,128)(2,1)S(1)}, bf16[2,256,768]{2,1,0:T(8,128)(2,1)S(1)}, u32[]{:S(2)}, u32[]{:S(2)}) collective-permute-start(bf16[2,256,768]{2,1,0:T(8,128)(2,1)S(1)} %get-tuple-element.208), channel_id=1, source_target_pairs={{0,1},{1,0},{2,3},{3,2},{4,5},{5,4},{6,7},{7,6},{8,9},{9,8},{10,11... | collective-permute-start | bytes 2359304 | tf_op jit(solution)/shard_map/ppermute | solution.py:787
  119.4 12.8 %collective-permute-start.33 = (bf16[2,2,48,1024]{3,2,1,0:T(8,128)(2,1)S(1)}, bf16[2,2,48,1024]{3,2,1,0:T(8,128)(2,1)S(1)}, u32[]{:S(2)}, u32[]{:S(2)}) collective-permute-start(bf16[2,2,48,1024]{3,2,1,0:T(8,128)(2,1)S(1)} %fusion), channel_id=1, source_target_pairs={{0,2},{1,3},{2,0},{3,1},{4,6},{5,7},{6,4},{7,5},{8,10},{9,11},{10,... | collective-permute-start | bytes 1179656 | tf_op jit(solution)/shard_map/ppermute | solution.py:787
  135.1 20.0 %collective-permute-start.37 = (bf16[2,48,1920]{2,1,0:T(8,128)(2,1)}, bf16[2,48,1920]{2,1,0:T(8,128)(2,1)}, u32[]{:S(2)}, u32[]{:S(2)}) collective-permute-start(bf16[2,48,1920]{2,1,0:T(8,128)(2,1)} %pad_maximum_fusion.2), channel_id=1, source_target_pairs={{0,4},{1,5},{2,6},{3,7},{4,0},{5,1},{6,2},{7,3},{8,12},{9,13},{10,... | collective-permute-start | bytes 1105928 | tf_op jit(solution)/shard_map/ppermute | solution.py:787
  137.3 17.7 %collective-permute-start.38 = (bf16[256,768]{1,0:T(8,128)(2,1)}, bf16[256,768]{1,0:T(8,128)(2,1)S(1)}, u32[]{:S(2)}, u32[]{:S(2)}) collective-permute-start(bf16[256,768]{1,0:T(8,128)(2,1)} %fusion.4), channel_id=1, source_target_pairs={{0,2},{1,3},{2,0},{3,1},{4,6},{5,7},{6,4},{7,5},{8,10},{9,11},{10,... | collective-permute-start | bytes 1179656 | tf_op jit(solution)/shard_map/ppermute | solution.py:787
  141.0 14.1 %collective-permute-start.36 = (bf16[5,48,576]{2,1,0:T(8,128)(2,1)}, bf16[5,48,576]{2,1,0:T(8,128)(2,1)}, u32[]{:S(2)}, u32[]{:S(2)}) collective-permute-start(bf16[5,48,576]{2,1,0:T(8,128)(2,1)} %pad_maximum_fusion.3), channel_id=1, source_target_pairs={{0,8},{1,9},{2,10},{3,11},{4,12},{5,13},{6,14},{7,15},{8,0},{9,1},... | collective-permute-start | bytes 829448 | tf_op jit(solution)/shard_map/ppermute | solution.py:787
  161.6 21.0 %collective-permute-start.39 = (bf16[64,768]{1,0:T(8,128)(2,1)S(1)}, bf16[64,768]{1,0:T(8,128)(2,1)S(1)}, u32[]{:S(2)}, u32[]{:S(2)}) collective-permute-start(bf16[64,768]{1,0:T(8,128)(2,1)S(1)} %get-tuple-element.222), channel_id=1, source_target_pairs={{0,4},{1,5},{2,6},{3,7},{4,0},{5,1},{6,2},{7,3},{8,12},{9,13},{10,... | collective-permute-start | bytes 294920 | tf_op jit(solution)/shard_map/ppermute | solution.py:787
  161.7 22.4 %collective-permute-start.40 = (bf16[64,768]{1,0:T(8,128)(2,1)S(1)}, bf16[64,768]{1,0:T(8,128)(2,1)S(1)}, u32[]{:S(2)}, u32[]{:S(2)}) collective-permute-start(bf16[64,768]{1,0:T(8,128)(2,1)S(1)} %get-tuple-element.223), channel_id=1, source_target_pairs={{0,8},{1,9},{2,10},{3,11},{4,12},{5,13},{6,14},{7,15},{8,0},{9,1},... | collective-permute-start | bytes 294920 | tf_op jit(solution)/shard_map/ppermute | solution.py:787
  163.7 21.7 %collective-permute-start.41 = (bf16[64,768]{1,0:T(8,128)(2,1)S(1)}, bf16[64,768]{1,0:T(8,128)(2,1)S(1)}, u32[]{:S(2)}, u32[]{:S(2)}) collective-permute-start(bf16[64,768]{1,0:T(8,128)(2,1)S(1)} %get-tuple-element.224), channel_id=1, source_target_pairs={{0,12},{1,13},{2,14},{3,15},{4,8},{5,9},{6,10},{7,11},{8,4},{9,5},... | collective-permute-start | bytes 294920 | tf_op jit(solution)/shard_map/ppermute | solution.py:787
  166.1 13.8 %collective-permute-start.43 = (bf16[48,1920]{1,0:T(8,128)(2,1)S(1)}, bf16[48,1920]{1,0:T(8,128)(2,1)S(1)}, u32[]{:S(2)}, u32[]{:S(2)}) collective-permute-start(bf16[48,1920]{1,0:T(8,128)(2,1)S(1)} %pad_maximum_fusion.6), channel_id=1, source_target_pairs={{0,8},{1,9},{2,10},{3,11},{4,12},{5,13},{6,14},{7,15},{8,0},{9,1},... | collective-permute-start | bytes 552968 | tf_op jit(solution)/shard_map/ppermute | solution.py:787
  (56 other events, 538.4 us)

commit v4 on v3

--- a/solution.py
+++ b/solution.py
@@ -11,8 +11,8 @@
 TILE = 256
 WIDE = 512
 BAND = 384
-FORWARD_MIB = 24
-BACKWARD_MIB = 24
+FORWARD_MIB = 14
+BACKWARD_MIB = 14
 WIDEN_MIB = 16
 TURN_MIB = 20
 OUTER_MIB = 16
@@ -65,6 +65,14 @@
     return pl.CostEstimate(flops=flops, bytes_accessed=moved, transcendentals=0)
 
 
+def document_ends(lengths_ref, plane):
+    ends, end = [], jnp.int32(0)
+    for d in range(lengths_ref.shape[1]):
+        end = end + lengths_ref[plane, d]
+        ends.append(end)
+    return ends
+
+
 def codes(steps):
     listed = [((), 0)]
     for bit in steps:
@@ -73,28 +81,20 @@
 
 
 def forward_kernel(*refs, planes, slots, seg, heads):
-    place_ref, start_ref, gain_ref, weight_ref = refs[:4]
-    pieces = refs[4 : 4 + slots]
-    refs = refs[4 + slots :]
+    place_ref, lengths_ref, gain_ref, weight_ref = refs[:4]
+    pieces = refs[4 : 4 + slots * planes]
+    refs = refs[4 + slots * planes :]
     length = planes * slots * seg
     tiles = length // TILE
-    first_to, joined_to = refs[:2]
+    first_ref, joined_ref = refs[:2]
     sent = refs[2 : 2 + slots]
-    shares_to = refs[2 + slots : 2 + slots + tiles]
-    rows_ref, first_ref, joined_ref, attention_ref = refs[2 + slots + tiles : 6 + slots + tiles]
-    shares = refs[6 + slots + tiles : 6 + slots + 2 * tiles]
-    ready = refs[-1]
-    copies = [
-        pltpu.make_async_copy(source, target, ready.at[at])
-        for at, (source, target) in enumerate(
-            zip((first_ref, joined_ref) + shares, (first_to, joined_to) + shares_to)
-        )
-    ]
+    shares = refs[2 + slots : 2 + slots + tiles]
+    rows_ref, attention_ref = refs[2 + slots + tiles :]
     plane, slot = place_ref[0], place_ref[1]
     for u in range(slots):
         for k in range(planes):
             offset = ((plane ^ k) * slots + (slot ^ u)) * seg
-            rows_ref[pl.ds(pl.multiple_of(offset, seg), seg), :] = pieces[u][k]
+            rows_ref[pl.ds(pl.multiple_of(offset, seg), seg), :] = pieces[k * slots + u][...]
     width = heads * HEAD
 
     def project(tile, carry):
@@ -113,14 +113,17 @@
         return carry
 
     lax.fori_loop(0, tiles, project, 0)
-    copies[0].start()
-    copies[1].start()
+    ends = document_ends(lengths_ref, plane)
     for q in reversed(range(tiles)):
         rows = slice(q * TILE, (q + 1) * TILE)
         reach = (q + 1) * TILE
+        places = q * TILE + lax.broadcasted_iota(jnp.int32, (TILE, 1), 0)
+        start = jnp.zeros((TILE, 1), jnp.int32)
+        for end in ends:
+            start = jnp.maximum(start, jnp.where(places >= end, end, 0))
         query_pos = q * TILE + lax.broadcasted_iota(jnp.int32, (TILE, reach), 0)
         key_pos = lax.broadcasted_iota(jnp.int32, (TILE, reach), 1)
-        allowed = (key_pos <= query_pos) & (key_pos >= start_ref[rows, :])
+        allowed = (key_pos <= query_pos) & (key_pos >= start)
         for h in range(heads):
             scores = dot_nt(joined_ref[h, rows, :], joined_ref[heads + h, :reach, :])
             scores = jnp.where(allowed, scores, big_negative)
@@ -130,7 +133,6 @@
             share = (raised * (1.0 / total)).astype(bf16)
             shares[q][h] = share
             attention_ref[h, rows, :] = dot(share, joined_ref[2 * heads + h, :reach, :])
-        copies[2 + q].start()
     half = planes // 2
     for u in range(slots):
         for k in range(planes):
@@ -140,13 +142,11 @@
                 part = attention_ref[h, pl.ds(pl.multiple_of(offset, seg), seg), :]
                 column = k // half * width + h * HEAD
                 sent[u][rows, column : column + HEAD] = part.astype(bf16)
-    for copy in copies:
-        copy.wait()
-
-
-def forward_call(place, start, gain, weight, pieces):
-    slots = len(pieces)
-    planes, seg, width = pieces[0].shape
+
+
+def forward_call(place, lengths, gain, weight, pieces):
+    planes, slots = len(pieces), len(pieces[0])
+    seg, width = pieces[0][0].shape
     length = planes * slots * seg
     heads = weight.shape[1] // (3 * HEAD)
     kernel = functools.partial(forward_kernel, planes=planes, slots=slots, seg=seg, heads=heads)
@@ -155,52 +155,34 @@
     outs = pl.pallas_call(
         kernel,
         out_shape=(
-            pltpu.HBM((length, width), bf16),
-            pltpu.HBM((3 * heads, length, HEAD), bf16),
+            pltpu.VMEM((length, width), bf16),
+            pltpu.VMEM((3 * heads, length, HEAD), bf16),
         )
         + (packed,) * slots
-        + tuple(pltpu.HBM(shape, bf16) for shape in tiled),
-        in_specs=[pl.BlockSpec(memory_space=pltpu.SMEM)] + [vmem_spec()] * (3 + slots),
-        out_specs=(hbm_spec(),) * 2 + (vmem_spec(),) * slots + (hbm_spec(),) * len(tiled),
+        + tuple(pltpu.VMEM(shape, bf16) for shape in tiled),
+        in_specs=[pl.BlockSpec(memory_space=pltpu.SMEM)] * 2
+        + [vmem_spec()] * (2 + slots * planes),
+        out_specs=(vmem_spec(),) * (2 + slots + len(tiled)),
         scratch_shapes=[
             pltpu.VMEM((length, width), bf16),
-            pltpu.VMEM((length, width), bf16),
-            pltpu.VMEM((3 * heads, length, HEAD), bf16),
             pltpu.VMEM((heads, length, HEAD), f32),
-        ]
-        + [pltpu.VMEM(shape, bf16) for shape in tiled]
-        + [pltpu.SemaphoreType.DMA((2 + len(tiled),))],
+        ],
         compiler_params=params(FORWARD_MIB * length // 1024),
         cost_estimate=cost(8 << 30, 8 << 20),
         name="attention_forward",
-    )(place, start, gain, weight, *pieces)
+    )(place, lengths, gain, weight, *[block for blocks in pieces for block in blocks])
     return outs[:2], outs[2 : 2 + slots], outs[2 + slots :]
 
 
 def backward_kernel(*refs, planes, slots, seg, heads, rows_each):
-    place_ref, first_from, joined_from, weight_ref, gain_ref, parts_ref = refs[:6]
+    place_ref, first_ref, joined_ref, weight_ref, gain_ref, parts_ref = refs[:6]
     pieces = refs[6 : 6 + slots]
     length = planes * slots * seg
     tiles = length // TILE
     refs = refs[6 + slots :]
-    shares_from = refs[:tiles]
+    shares = refs[:tiles]
     joined_out, branch_keep, branch_give = refs[tiles : tiles + 3]
-    (
-        grad_ref, arrived_ref, key_ref, value_ref, total_ref, outer_ref, row_ref,
-        first_ref, joined_ref,
-    ) = refs[tiles + 3 : tiles + 12]
-    shares = refs[tiles + 12 : 2 * tiles + 12]
-    ready = refs[-1]
-    copies = [
-        pltpu.make_async_copy(source, target, ready.at[at])
-        for at, (source, target) in enumerate(
-            zip((joined_from, first_from) + shares_from, (joined_ref, first_ref) + shares)
-        )
-    ]
-    copies[0].start()
-    for q in reversed(range(tiles)):
-        copies[2 + q].start()
-    copies[1].start()
+    grad_ref, arrived_ref, key_ref, value_ref, total_ref, outer_ref, row_ref = refs[tiles + 3 :]
     plane, slot = place_ref[0], place_ref[1]
     width = heads * HEAD
     half = planes // 2
@@ -211,14 +193,11 @@
             arrived_ref[pl.ds(pl.multiple_of(offset, seg), seg), :] = pieces[u][
                 k % half * seg : (k % half + 1) * seg, column : column + width
             ]
-    copies[0].wait()
     for h in range(heads):
         for q in reversed(range(tiles)):
             rows = slice(q * TILE, (q + 1) * TILE)
             reach = (q + 1) * TILE
             grad = arrived_ref[rows, h * HEAD : (h + 1) * HEAD]
-            if h == 0:
-                copies[2 + q].wait()
             share = shares[q][h]
             product = share.astype(f32) * dot_nt(grad, joined_ref[2 * heads + h, :reach, :])
             inner = jnp.sum(product, axis=-1, keepdims=True)
@@ -253,13 +232,12 @@
                     pl.ds(pl.multiple_of(offset, seg), seg), :
                 ].astype(bf16)
     model = first_ref.shape[1]
-    copies[1].wait()
     for d in range(0, model, TILE):
         outer = dot_tn(first_ref[:, d : d + TILE], grad_ref[...])
         outer_ref[d : d + TILE, :] = outer
         scaled = jnp.sum(outer * weight_ref[d : d + TILE, :].astype(f32), axis=-1, keepdims=True)
-        scaled = jnp.broadcast_to(scaled / gain_ref[d : d + TILE, :], (TILE, 128)).T
-        row_ref[:, d : d + TILE] = scaled[:1]
+        scaled = jnp.broadcast_to(scaled, (TILE, 128)).T
+        row_ref[:, d : d + TILE] = scaled[:1] / gain_ref[:, d : d + TILE]
     wide = 3 * width
     row_ref[:, model : model + parts_ref.shape[1]] = parts_ref[...]
     gains = model + parts_ref.shape[1]
@@ -300,9 +278,7 @@
             jax.ShapeDtypeStruct(pairs + (tokens, width), bf16),
         ),
         in_specs=[pl.BlockSpec(memory_space=pltpu.SMEM)]
-        + [hbm_spec()] * 2
-        + [vmem_spec()] * (3 + slots)
-        + [hbm_spec()] * len(shares),
+        + [vmem_spec()] * (5 + slots + len(shares)),
         out_specs=(vmem_spec(),) * 3,
         scratch_shapes=[
             pltpu.VMEM((length, wide), bf16),
@@ -312,11 +288,7 @@
             pltpu.VMEM((length, width), f32),
             pltpu.VMEM((width, wide), f32),
             pltpu.VMEM((1, row), f32),
-            pltpu.VMEM(first.shape, bf16),
-            pltpu.VMEM(joined.shape, bf16),
-        ]
-        + [pltpu.VMEM(share.shape, bf16) for share in shares]
-        + [pltpu.SemaphoreType.DMA((2 + len(shares),))],
+        ],
         compiler_params=params(BACKWARD_MIB * length // 1024),
         cost_estimate=cost(10 << 30, 10 << 20),
         name="attention_backward",
@@ -326,16 +298,14 @@
 def widen_kernel(*refs, slots, planes, groups, width, spread, block):
     place_ref = refs[0]
     pieces = refs[1 : 1 + slots]
-    blocks = refs[1 + slots : 1 + slots + planes]
+    inputs = refs[1 + slots : 1 + slots + planes]
     refs = refs[1 + slots + planes :]
-    (
-        valid_ref, input_ref, mixed_gain_ref, second_gain_ref, hidden_gain_ref, merge_ref, expand_from,
-    ) = refs[:7]
+    mixed_gain_ref, second_gain_ref, hidden_gain_ref, merge_ref, expand_from = refs[:5]
     (
         mixed_ref, middle_ref, second_ref, hidden_ref, hidden_give_ref, normal_ref, slope_ref,
-        held_ref, mixed_rate_ref, hidden_rate_ref, branch_ref,
-    ) = refs[7:18]
-    expand_ref, gelu_ref, ready = refs[18:]
+        held_ref, mixed_rate_ref, hidden_rate_ref,
+    ) = refs[5:15]
+    expand_ref, gelu_ref, ready = refs[15:]
     steps = spread // WIDE
 
     def copy(step):
@@ -348,7 +318,7 @@
         copy(step).start()
     slot = place_ref[1]
     piece = width // groups
-    tokens = input_ref.shape[0]
+    tokens = planes * inputs[0].shape[0]
     half = tokens // 2
     for u in range(slots):
         for side in range(2):
@@ -363,7 +333,7 @@
         square = square + jnp.sum(centred * centred, axis=-1, keepdims=True)
     mixed_rate = lax.rsqrt(square * (1.0 / width) + norm_epsilon)
     mixed_rate_ref[...] = mixed_rate
-    middle = input_ref[...].astype(f32)
+    middle = jnp.concatenate([block[...] for block in inputs], axis=0).astype(f32)
     for g in range(groups):
         normal = held_ref[g] * mixed_rate
         held_ref[g] = normal
@@ -371,10 +341,6 @@
         mixed_ref[:, g * piece : (g + 1) * piece] = mixed
         middle = middle + dot(mixed, merge_ref[g * piece : (g + 1) * piece, :])
     middle_ref[...] = middle
-    seg = tokens // planes
-    for k in range(planes):
-        at = slice(k * seg, (k + 1) * seg)
-        branch_ref[at, :] = (blocks[k][...].astype(f32) * valid_ref[at, :]).astype(bf16)
     second_normal, _ = normalized(middle)
     second = (second_normal * second_gain_ref[...]).astype(bf16)
     second_ref[...] = second
@@ -416,10 +382,10 @@
 
 
 def widen_call(
-    place, pieces, blocks, valid, inputs, mixed_gain, second_gain, hidden_gain, merge, expand
+    place, pieces, inputs, mixed_gain, second_gain, hidden_gain, merge, expand
 ):
     slots = len(pieces)
-    tokens = inputs.shape[0]
+    tokens = len(inputs) * inputs[0].shape[0]
     piece = pieces[0].shape[1] // 2
     width, spread = expand.shape
     groups = width // piece
@@ -432,8 +398,8 @@
 
     return pl.pallas_call(
         functools.partial(
-            widen_kernel, slots=slots, planes=len(blocks), groups=groups, width=width,
-            spread=spread, block=spread // (slots * len(blocks)),
+            widen_kernel, slots=slots, planes=len(inputs), groups=groups, width=width,
+            spread=spread, block=spread // (slots * len(inputs)),
         ),
         out_shape=(
             low(tokens, width),
@@ -446,12 +412,11 @@
             full(slots, tokens, piece),
             full(tokens, 1),
             full(tokens, 1),
-            low(tokens, width),
         ),
         in_specs=[pl.BlockSpec(memory_space=pltpu.SMEM)]
-        + [vmem_spec()] * (6 + slots + len(blocks))
+        + [vmem_spec()] * (4 + slots + len(inputs))
         + [hbm_spec()],
-        out_specs=(vmem_spec(),) * 11,
+        out_specs=(vmem_spec(),) * 10,
         scratch_shapes=[
             pltpu.VMEM((width, spread), bf16),
             pltpu.VMEM((tokens, spread), f32),
@@ -461,9 +426,32 @@
         cost_estimate=cost(6 << 30, 6 << 20),
         name="widen",
     )(
-        place, *pieces, *blocks, valid, inputs, mixed_gain.reshape(groups, 1, piece),
-        second_gain.reshape(1, width), hidden_gain.reshape(1, spread), merge, expand,
-    )
+        place, *pieces, *inputs, mixed_gain, second_gain, hidden_gain, merge, expand,
+    )
+
+
+def branch_kernel(place_ref, lengths_ref, *refs, slots):
+    blocks, branch_ref = refs[:-1], refs[-1]
+    seg = blocks[0].shape[0]
+    limit = document_ends(lengths_ref, place_ref[0])[-1]
+    for k, block in enumerate(blocks):
+        offset = ((place_ref[0] ^ k) * slots + place_ref[1]) * seg
+        valid = offset + lax.broadcasted_iota(jnp.int32, (seg, 1), 0) < limit
+        branch_ref[k * seg : (k + 1) * seg, :] = jnp.where(
+            valid, block[...], jnp.zeros((), bf16)
+        )
+
+
+def branch_call(place, lengths, blocks, slots):
+    seg, width = blocks[0].shape
+    return pl.pallas_call(
+        functools.partial(branch_kernel, slots=slots),
+        out_shape=jax.ShapeDtypeStruct((len(blocks) * seg, width), bf16),
+        in_specs=[pl.BlockSpec(memory_space=pltpu.SMEM)] * 2 + [vmem_spec()] * len(blocks),
+        out_specs=vmem_spec(),
+        compiler_params=params(4),
+        name="branch",
+    )(place, lengths, *blocks)
 
 
 def turn_kernel(*refs, slots, planes, groups, width, spread):
@@ -605,8 +593,7 @@
         name="turn",
     )(
         place, branch, normal, slope, middle, held, mixed_rate, hidden_rate,
-        mixed_gain.reshape(groups, 1, piece), second_gain.reshape(1, width),
-        hidden_gain.reshape(1, spread), merge, shrink, expand,
+        mixed_gain, second_gain, hidden_gain, merge, shrink, expand,
     )
     return outs[:4], outs[4 : 4 + slots], outs[4 + slots :]
 
@@ -760,26 +747,31 @@
 
 
 def input_kernel(*refs, planes, parts):
-    input_ref, grad_ref, gain_ref = refs[:3]
-    grad = sum(ref[at].astype(f32) for ref, at in zip(refs[3 : 3 + len(parts)], parts))
-    outs = refs[3 + len(parts) :]
-    normal, rate = normalized(input_ref[...].astype(f32))
+    inputs = refs[:planes]
+    refs = refs[planes:]
+    grad_ref, gain_ref = refs[:2]
+    grad = sum(ref[at].astype(f32) for ref, at in zip(refs[2 : 2 + len(parts)], parts))
+    outs = refs[2 + len(parts) :]
+    normal, rate = normalized(
+        jnp.concatenate([block[...] for block in inputs], axis=0).astype(f32)
+    )
     value = grad_ref[...] + norm_back(normal, rate, grad * gain_ref[...])
     seg = value.shape[0] // planes
     for k in range(planes):
         outs[k][...] = value[k * seg : (k + 1) * seg, :].astype(bf16)
 
 
-def input_call(inputs, grad_middle, gain, held, parts, planes):
-    tokens, width = inputs.shape
+def input_call(inputs, grad_middle, gain, held, parts):
+    planes = len(inputs)
+    tokens, width = grad_middle.shape
     return pl.pallas_call(
         functools.partial(input_kernel, planes=planes, parts=parts),
         out_shape=(jax.ShapeDtypeStruct((tokens // planes, width), bf16),) * planes,
-        in_specs=[vmem_spec()] * (3 + len(held)),
+        in_specs=[vmem_spec()] * (2 + planes + len(held)),
         out_specs=(vmem_spec(),) * planes,
         compiler_params=params(16),
         name="input_back",
-    )(inputs, grad_middle, gain.reshape(1, width), *held)
+    )(*inputs, grad_middle, gain, *held)
 
 
 def swap(value, axis, bits):
@@ -801,6 +793,34 @@
 
 def total(values):
     return sum(v.astype(f32) for v in values)
+
+
+def sums_kernel(*refs, listed):
+    outs = refs[-len(listed) :]
+    for out, terms in zip(outs, listed):
+        out[...] = sum(refs[i][at].astype(f32) for i, at in terms).astype(bf16)
+
+
+def sums_call(sums, name):
+    arrays, listed, shapes = [], [], []
+    for terms in sums:
+        entry = []
+        for array, at in terms:
+            where = [i for i, held in enumerate(arrays) if held is array]
+            if not where:
+                arrays.append(array)
+                where = [len(arrays) - 1]
+            entry.append((where[0], at))
+        listed.append(entry)
+        shapes.append(jax.eval_shape(lambda v, at=terms[0][1]: v[at], terms[0][0]).shape)
+    return pl.pallas_call(
+        functools.partial(sums_kernel, listed=listed),
+        out_shape=tuple(jax.ShapeDtypeStruct(shape, bf16) for shape in shapes),
+        in_specs=[vmem_spec()] * len(arrays),
+        out_specs=(vmem_spec(),) * len(shapes),
+        compiler_params=params(4),
+        name=name,
+    )(*arrays)
 
 
 class Halves:
@@ -812,10 +832,10 @@
     def hold(self, array, names):
         self.entries.append((array, names))
 
-    def summed(self, choice=()):
+    def terms(self, choice=()):
         chosen = dict(self.chosen)
         chosen.update(choice)
-        values = []
+        listed = []
         for array, names in self.entries:
             at = tuple(
                 chosen[n] if n in chosen
@@ -823,8 +843,11 @@
                 else slice(None)
                 for n in names
             )
-            values.append(array[at].astype(f32))
-        return sum(values)
+            listed.append((array, at))
+        return listed
+
+    def summed(self, choice=()):
+        return sum(array[at].astype(f32) for array, at in self.terms(choice))
 
     def send(self, name):
         return self.summed({name: 1}).astype(bf16)
@@ -872,10 +895,6 @@
     spread = expand_weight.shape[1]
     expand_weight, shrink_weight = in_hbm(expand_weight, shrink_weight)
     first_arrived = to_planes(layer_input[0])
-    ends = jnp.cumsum(pick(doc_lengths[0], plane), axis=-1)
-    positions = jnp.arange(length, dtype=jnp.int32)
-    reached = ends[None, :] <= positions[:, None]
-    start = jnp.max(jnp.where(reached, ends[None, :], 0), axis=-1, keepdims=True)
     own_start = jnp.minimum(slot, groups - 1) * piece
     own_weight = jnp.concatenate(
         [
@@ -884,30 +903,33 @@
         ],
         axis=1,
     )
-    own_pos = (
-        (plane ^ jnp.arange(planes, dtype=jnp.int32))[:, None] * (slots * seg)
-        + slot * seg
-        + jnp.arange(seg, dtype=jnp.int32)[None, :]
-    ).reshape(tokens, 1)
-    valid = (own_pos < ends[-1]).astype(f32)
-    first_arrived, start, own_weight, valid, cotangent = lax.optimization_barrier(
-        (first_arrived, start, own_weight, valid, cotangent)
-    )
-    arrived = jnp.stack(first_arrived)
+    lengths = doc_lengths[0]
+    gain_row = first_gain.reshape(1, width)
+    mixed_gain = mixed_gain.reshape(groups, 1, piece)
+    second_gain = second_gain.reshape(1, width)
+    hidden_gain = hidden_gain.reshape(1, spread)
+    (
+        first_arrived[-1], place, lengths, gain_row, mixed_gain, second_gain, hidden_gain, own_weight,
+    ) = lax.optimization_barrier(
+        (
+            first_arrived[-1], place, lengths, gain_row, mixed_gain, second_gain, hidden_gain,
+            own_weight,
+        )
+    )
+    pieces = [all_slots(block) for block in first_arrived]
+    (first, joined), sent, shares = forward_call(
+        place, lengths, gain_row, own_weight, pieces
+    )
+    sent, cotangent = lax.optimization_barrier((sent, cotangent))
     cotangent_blocks = to_planes(cotangent[0])
-    pieces = all_slots(arrived)
-    (first, joined), sent, shares = forward_call(
-        place, start, first_gain.reshape(1, width), own_weight, pieces
-    )
-    sent, cotangent_blocks = lax.optimization_barrier((sent, cotangent_blocks))
-    input_rows = arrived.reshape(tokens, width)
     (
         mixed, middle, second, hidden, hidden_give, normal, slope, held, mixed_rate, hidden_rate,
-        branch,
     ) = widen_call(
-        place, over_slots(sent), cotangent_blocks, valid, input_rows, mixed_gain, second_gain,
-        hidden_gain, merge_weight, expand_weight,
-    )
+        place, over_slots(sent), first_arrived, mixed_gain, second_gain, hidden_gain, merge_weight,
+        expand_weight,
+    )
+    hidden_give, cotangent_blocks = lax.optimization_barrier((hidden_give, cotangent_blocks))
+    branch = branch_call(place, lengths, cotangent_blocks, slots)
 
     row_bits = list(range(1, bits_of(slots)))
     plane_bits = list(range(bits_of(slots), bits_of(size)))
@@ -929,6 +951,11 @@
 
     def sends(pair, at):
         return [chain.send(order[at]) for chain, order in zip(pair, orders)]
+
+    def sends_in_kernel(pair, at):
+        return sums_call(
+            [chain.terms({order[at]: 1}) for chain, order in zip(pair, orders)], "next_halves"
+        )
 
     def crossed(at, values):
         return [cross(order[at], value) for order, value in zip(orders, values)]
@@ -989,7 +1016,7 @@
         [pltpu.VMEM((width, 2 * tokens), f32)], "expand_outer",
     )
     for at in range(1, stages):
-        shrink_sent = crossed(at, sends(shrink_chains, at))
+        shrink_sent = crossed(at, sends_in_kernel(shrink_chains, at))
         if at < stages - 1:
             arrive(shrink_chains, at, shrink_sent)
     expand_firsts, results = lax.optimization_barrier((expand_firsts, results))
@@ -1001,17 +1028,23 @@
     )
     arrive(shrink_chains, stages - 1, shrink_sent)
     expand_sent = crossed(0, expand_firsts)
-    shrink_both = plane_depart(shrink_chains, plane_bits[0], -2)
+    shrink_both = [
+        cross(plane_bits[0], value)
+        for value in sums_call(
+            [chain.terms({plane_bits[0]: 1}) for chain in shrink_chains], "plane_halves"
+        )
+    ]
     joined_part, branch_keep, branch_give = backward_call(
-        place, *in_hbm(first, joined), own_weight, first_gain.reshape(width, 1), parts,
-        returned, in_hbm(*shares), planes,
+        place, first, joined, own_weight, gain_row, parts,
+        returned, shares, planes,
     )
     (
         joined_part, branch_give, shrink_both, expand_sent, result_blocks,
     ) = lax.optimization_barrier(
         (joined_part, branch_give, shrink_both, expand_sent, result_blocks)
     )
-    plane_arrive(shrink_chains, plane_bits[0], -2, shrink_both)
+    for chain, value in zip(shrink_chains, shrink_both):
+        chain.receive(plane_bits[0], value)
     expand_chains = chains("columns", cut, expand_whole)
     arrive(expand_chains, 0, expand_sent)
 
@@ -1057,14 +1090,11 @@
         joined_got = joined_depart(bit)
         if bit != plane_bits[-1]:
             joined_sum, gains = joined_arrive(joined_got)
-    joined_got, expand_both, branch_held = lax.optimization_barrier(
-        (joined_got, expand_both, branch_held)
-    )
     joined_sum, gains = joined_arrive(joined_got)
     plane_arrive(expand_chains, plane_bits[0], -1, expand_both)
 
     input_blocks = input_call(
-        input_rows, grad_middle, first_gain, branch_held, prefixes, planes
+        first_arrived, grad_middle, gain_row, branch_held, prefixes
     )
     input_blocks = [input_blocks[0]] + [
         swap(input_blocks[k], "blk", k * slots) for k in range(1, planes)
@@ -1078,10 +1108,9 @@
         expand_both = plane_depart(expand_chains, bit, -1)
         if bit != plane_bits[-1]:
             plane_arrive(expand_chains, bit, -1, expand_both)
-    joined_last, expand_both = lax.optimization_barrier((joined_last, expand_both))
     plane_arrive(expand_chains, plane_bits[-1], -1, expand_both)
 
-    joined_grad, gain_row = heads_call(
+    joined_grad, gain_grads = heads_call(
         place,
         [jnp.stack([joined_last[0], joined_last[slots]])]
         + [
@@ -1098,11 +1127,11 @@
     merge_grad = jnp.concatenate([expand_lower[:, cut:], expand_upper[:, cut:]], axis=1)
     layer_result = settle_call(place, result_blocks).reshape(layer_input.shape)
     input_grad = settle_call(place, input_blocks).reshape(layer_input.shape)
-    gain_row = gain_row[0]
+    gain_grads = gain_grads[0]
     return (
         layer_result, input_grad, joined_grad, merge_grad.astype(f32), expand_grad.astype(f32),
-        shrink_grad, gain_row[:width], gain_row[width : 2 * width],
-        gain_row[2 * width : 3 * width], gain_row[3 * width :],
+        shrink_grad, gain_grads[:width], gain_grads[width : 2 * width],
+        gain_grads[2 * width : 3 * width], gain_grads[3 * width :],
     )
 
 

time: 198 us -> 183 us (0.924)
  waiting for transfers between devices: 62.4 us -> 47.8 us
  Pallas kernels: 55.7 us -> 51.6 us
  local copies, waits for them, and re-layouts: 10.7 us -> 14.4 us
  starting transfers between devices: 49.1 us -> 46.8 us
    ppermute x49 -> x59, waiting for transfers between devices: 62.4 us -> 47.8 us  [swap(): return lax.ppermute(value, axis, [(i, i ^ bits) for i in range(size)])]
    convert_element_type x9 -> x7, other arithmetic: 2.75 us -> 5.89 us  [send(): return self.summed({name: 1}).astype(bf16)]
    pallas_call x2 -> x5, Pallas kernels: 21 us -> 18.2 us  [the longest x1 9.59 us: forward_call(): pl.pallas_call(kernel, out_shape=(pltpu.VMEM((length, width), bf16), pltp...]
    ppermute x49 -> x59, starting transfers between devices: 49.1 us -> 46.8 us  [swap(): return lax.ppermute(value, axis, [(i, i ^ bits) for i in range(size)])]
    unnamed x62 -> x72, local copies, waits for them, and re-layouts: 4.95 us -> 7.07 us
    pallas_call x1, Pallas kernels: 13.9 us -> 11.9 us  [backward_call(): pl.pallas_call(kernel, out_shape=(jax.ShapeDtypeStruct((planes * slots +...]
    another operation x7 -> x5, other arithmetic: 4.49 us -> 4.28 us
  transfers between devices with their start and end apart: 49 -> 59, of which waited for: 19 -> 23; matrix products, arithmetic and copies ran while one was open for 8% -> 10% of each run, Pallas kernels for 25% -> 23%
where the time goes in v4:
time: 183 us; the launch traced here: 180 us
  Pallas kernels  51.6 us (28%)
  waiting for transfers between devices  47.8 us (26%)
  starting transfers between devices  46.8 us (26%)
  other arithmetic  17.3 us (9%)
  local copies, waits for them, and re-layouts  14.4 us (8%)
  between operations  1.83 us (1%)
    ppermute x59, waiting for transfers between devices, swap(): return lax.ppermute(value, axis, [(i, i ^ bits) for i in range(size)])  47.8 us
    ppermute x59, starting transfers between devices, swap(): return lax.ppermute(value, axis, [(i, i ^ bits) for i in range(size)])  46.8 us
    pallas_call x1, Pallas kernels, backward_call(): pl.pallas_call(kernel, out_shape=(jax.ShapeDtypeStruct((planes * slots +...  11.9 us
    pallas_call x1, Pallas kernels, turn_call(): pl.pallas_call(functools.partial(turn_kernel, slots=slots, planes=planes,...  10.3 us
    pallas_call x1, Pallas kernels, forward_call(): pl.pallas_call(kernel, out_shape=(pltpu.VMEM((length, width), bf16), pltp...  9.59 us
    pallas_call x1, Pallas kernels, widen_call(): pl.pallas_call(functools.partial(widen_kernel, slots=slots, planes=len(in...  7.67 us
    unnamed x72, local copies, waits for them, and re-layouts  7.07 us
    convert_element_type x7, other arithmetic, send(): return self.summed({name: 1}).astype(bf16)  5.89 us
  transfers between devices with their start and end apart: 59, of which 23 were waited for; matrix products, arithmetic and copies ran while one was open for 10% of the time, Pallas kernels for 23%

profile of v4, /device:TPU:0, one launch (start us, length us, event | category | flops | bytes accessed | tf_op | source)
XLA Modules:
  0.0 179.7 jit_solution(14650617011888896005)
XLA Ops:
  2.3 2.6 %collective-permute-start.2 = (bf16[64,768]{1,0:T(8,128)(2,1)S(1)}, bf16[64,768]{1,0:T(8,128)(2,1)S(1)}, u32[]{:S(2)}, u32[]{:S(2)}) collective-permute-start(bf16[64,768]{1,0:T(8,128)(2,1)S(1)} %get-tuple-element.245.refs_4_.refs_5_.refs_0_), channel_id=1, source_target_pairs={{0,2},{1,3},{2,0},{3,1},{4,6},{5,7},{6,4},{7,5},{8,10},{9,11},{10,... | collective-permute-start | bytes 294920 | tf_op jit(solution)/shard_map/ppermute | solution.py:779
  4.9 3.6 %collective-permute-start = (bf16[64,768]{1,0:T(8,128)(2,1)S(1)}, bf16[64,768]{1,0:T(8,128)(2,1)S(1)}, u32[]{:S(2)}, u32[]{:S(2)}) collective-permute-start(bf16[64,768]{1,0:T(8,128)(2,1)S(1)} %get-tuple-element.246), channel_id=1, source_target_pairs={{0,12},{1,13},{2,14},{3,15},{4,8},{5,9},{6,10},{7,11},{8,4},{9,5},... | collective-permute-start | bytes 294920 | tf_op jit(solution)/shard_map/ppermute | solution.py:779
  11.4 2.0 %constant_dynamic-slice_fusion.2 = (bf16[768,192]{1,0:T(8,128)(2,1)S(1)}, bf16[768,192]{1,0:T(8,128)(2,1)S(1)}, bf16[768,192]{1,0:T(8,128)(2,1)S(1)}) fusion(bf16[768,2304]{1,0:T(8,128)(2,1)} %param.14, s32[]{:T(128)S(6)} %select_n.69, s32[]{:T(128)S(6)} %select_n.71, s32[]{:T(128)S(6)} %select_n.70), kind=kLoop, calls=%fused_computation.88 | loop fusion | bytes 1769484 | tf_op jit(solution)/shard_map/dynamic_slice | solution.py:901
  15.3 1.8 collective-permute-done.8.refs_12_.refs_7_.refs_2_
  20.4 2.4 %collective-permute-done.10.refs_14_ = bf16[64,768]{1,0:T(8,128)(2,1)S(1)} collective-permute-done((bf16[64,768]{1,0:T(8,128)(2,1)S(1)}, bf16[64,768]{1,0:T(8,128)(2,1)S(1)}, u32[]{:S(2)}, u32[]{:S(2)}) %collective-permute-start.10) | collective-permute-done | bytes 98336 | tf_op jit(solution)/shard_map/ppermute | solution.py:779
  25.5 9.6 %attention_forward.1 = (bf16[1024,768]{1,0:T(8,128)(2,1)S(1)}, bf16[9,1024,64]{2,1,0:T(8,128)(2,1)S(1)}, bf16[128,384]{1,0:T(8,128)(2,1)S(1)}, bf16[128,384]{1,0...) custom-call(s32[4]{0:T(128)S(1)} %pad_add_fusion.refs_0_.place_ref, ...), custom_call_target="tpu_custom_call" | custom-call | flops 8589934592 | bytes 8388608 | tf_op jit(solution)/shard_map/attention_forward/pallas_call | solution.py:155
  38.6 1.9 %collective-permute-start.19 = (bf16[64,768]{1,0:T(8,128)(2,1)S(1)}, bf16[64,768]{1,0:T(8,128)(2,1)S(1)}, u32[]{:S(2)}, u32[]{:S(2)}) collective-permute-start(bf16[64,768]{1,0:T(8,128)(2,1)S(1)} %get-tuple-element.241), channel_id=1, source_target_pairs={{0,8},{1,9},{2,10},{3,11},{4,12},{5,13},{6,14},{7,15},{8,0},{9,1},... | collective-permute-start | bytes 294920 | tf_op jit(solution)/shard_map/ppermute | solution.py:779
  42.0 7.7 %widen.1 = (bf16[256,768]{1,0:T(8,128)(2,1)S(1)}, f32[256,768]{1,0:T(8,128)S(1)}, bf16[256,768]{1,0:T(8,128)(2,1)S(1)}, bf16[256,1536]{1,0:T(8,128)(2,1)S(1)}, b...) custom-call(s32[4]{0:T(128)S(1)} %pad_add_fusion.refs_0_.place_ref, ...), custom_call_target="tpu_custom_call" | custom-call | flops 6442450944 | bytes 6291456 | tf_op jit(solution)/shard_map/widen/pallas_call | solution.py:399
  52.7 2.5 %shrink_outer.1 = (bf16[2,2,2,2,192,384]{5,4,3,2,1,0:T(8,128)(2,1)S(1)}, bf16[2,2,2,96,384]{4,3,2,1,0:T(8,128)(2,1)S(1)}, bf16[2,2,2,96,384]{4,3,2,1,0:T(8,128)(2,1)S(1)}) custom-call(s32[4]{0:T(128)S(1)} %pad_add_fusion.refs_0_.place_ref, bf16[256,1536]{1,0:T(8,128)(2,1)S(1)} %get-tuple-element.155.hidden_ref, ...), custom_call_target="tpu_custom_call" | custom-call | flops 2147483648 | bytes 10485760 | tf_op jit(solution)/shard_map/shrink_outer/pallas_call | solution.py:675
  57.3 10.3 %turn.1 = (bf16[256,3072]{1,0:T(8,128)(2,1)S(1)}, bf16[256,768]{1,0:T(8,128)(2,1)S(1)}, f32[256,768]{1,0:T(8,128)S(1)}, f32[1,4608]{1,0:T(1,128)S(1)}, bf16[128,...) custom-call(s32[4]{0:T(128)S(1)} %pad_add_fusion.refs_0_.place_ref, ...), custom_call_target="tpu_custom_call" | custom-call | flops 9663676416 | bytes 8388608 | tf_op jit(solution)/shard_map/turn/pallas_call | solution.py:570
  67.7 3.3 %collective-permute-done.26.refs_1_ = bf16[2,2,2,96,384]{4,3,2,1,0:T(8,128)(2,1)S(1)} collective-permute-done((bf16[2,2,2,96,384]{4,3,2,1,0:T(8,128)(2,1)S(1)}, bf16[2,2,2,96,384]{4,3,2,1,0:T(8,128)(2,1)S(1)}, u32[]{:S(2)}, u32[]{:S(2)}) %collective-permute-start.26) | collective-permute-done | bytes 589856 | tf_op jit(solution)/shard_map/ppermute | solution.py:779
  79.6 2.9 %expand_outer.1 = (bf16[2,2,2,2,48,1920]{5,4,3,2,1,0:T(8,128)(2,1)S(1)}, bf16[2,2,2,48,1024]{4,3,2,1,0:T(8,128)(2,1)S(1)}, bf16[2,2,2,48,896]{4,3,2,1,0:T(8,128)(2,1)S(1)}) custom-call(s32[4]{0:T(128)S(1)} %pad_add_fusion.refs_0_.place_ref, bf16[256,768]{1,0:T(8,128)(2,1)S(1)} %get-tuple-element.159.second_ref, ...), custom_call_target="tpu_custom_call" | custom-call | flops 2147483648 | bytes 10485760 | tf_op jit(solution)/shard_map/expand_outer/pallas_call | solution.py:675
  82.6 1.7 collective-permute-start.38
  84.3 1.9 %collective-permute-start.39 = (bf16[64,768]{1,0:T(8,128)(2,1)S(1)}, bf16[64,768]{1,0:T(8,128)(2,1)S(1)}, u32[]{:S(2)}, u32[]{:S(2)}) collective-permute-start(bf16[64,768]{1,0:T(8,128)(2,1)S(1)} %get-tuple-element.204), channel_id=1, source_target_pairs={{0,8},{1,9},{2,10},{3,11},{4,12},{5,13},{6,14},{7,15},{8,0},{9,1},... | collective-permute-start | bytes 294920 | tf_op jit(solution)/shard_map/ppermute | solution.py:779
  90.5 2.0 %collective-permute-done.39.refs_2_ = bf16[64,768]{1,0:T(8,128)(2,1)S(1)} collective-permute-done((bf16[64,768]{1,0:T(8,128)(2,1)S(1)}, bf16[64,768]{1,0:T(8,128)(2,1)S(1)}, u32[]{:S(2)}, u32[]{:S(2)}) %collective-permute-start.39) | collective-permute-done | bytes 98336 | tf_op jit(solution)/shard_map/ppermute | solution.py:779
  94.8 11.9 %attention_backward.1 = (bf16[17,48,576]{2,1,0:T(8,128)(2,1)S(1)}, bf16[2,256,768]{2,1,0:T(8,128)(2,1)S(1)}, bf16[2,256,768]{2,1,0:T(8,128)(2,1)}) custom-call(s32[4]{0:T(128)S(1)} %pad_add_fusion.refs_0_.place_ref, bf16[1024,768]{1,0:T(8,128)(2,1)S(1)} %get-tuple-element.125.refs_1_, bf16[9,1024,64]{2,1,0:T(8,128)(2,1)S(1)} %get-tuple-element.126.refs_2_, ...), custom_call_target="tpu_custom_call" | custom-call | flops 10737418240 | bytes 10485760 | tf_op jit(solution)/shard_map/attention_backward/pallas_call | solution.py:273
  120.6 4.2 %collective-permute-done.45 = bf16[192,384]{1,0:T(8,128)(2,1)} collective-permute-done((bf16[192,384]{1,0:T(8,128)(2,1)}, bf16[192,384]{1,0:T(8,128)(2,1)}, u32[]{:S(2)}, u32[]{:S(2)}) %collective-permute-start.45) | collective-permute-done | bytes 147488 | tf_op jit(solution)/shard_map/ppermute | solution.py:779
  124.8 2.2 %collective-permute-done.41 = bf16[9,48,576]{2,1,0:T(8,128)(2,1)} collective-permute-done((bf16[9,48,576]{2,1,0:T(8,128)(2,1)}, bf16[9,48,576]{2,1,0:T(8,128)(2,1)}, u32[]{:S(2)}, u32[]{:S(2)}) %collective-permute-start.41) | collective-permute-done | bytes 497696 | tf_op jit(solution)/shard_map/ppermute | solution.py:779
  137.2 4.0 %collective-permute-done.58 = bf16[192,384]{1,0:T(8,128)(2,1)S(1)} collective-permute-done((bf16[192,384]{1,0:T(8,128)(2,1)S(1)}, bf16[192,384]{1,0:T(8,128)(2,1)S(1)}, u32[]{:S(2)}, u32[]{:S(2)}) %collective-permute-start.58) | collective-permute-done | bytes 147488 | tf_op jit(solution)/shard_map/ppermute | solution.py:779
  141.3 4.0 %collective-permute-done.50 = bf16[5,48,576]{2,1,0:T(8,128)(2,1)S(1)} collective-permute-done((bf16[5,48,576]{2,1,0:T(8,128)(2,1)S(1)}, bf16[5,48,576]{2,1,0:T(8,128)(2,1)S(1)}, u32[]{:S(2)}, u32[]{:S(2)}) %collective-permute-start.50) | collective-permute-done | bytes 276512 | tf_op jit(solution)/shard_map/ppermute | solution.py:779
  147.1 3.5 %collective-permute-done.55 = bf16[2,48,1920]{2,1,0:T(8,128)(2,1)S(1)} collective-permute-done((bf16[2,48,1920]{2,1,0:T(8,128)(2,1)S(1)}, bf16[2,48,1920]{2,1,0:T(8,128)(2,1)S(1)}, u32[]{:S(2)}, u32[]{:S(2)}) %collective-permute-start.55) | collective-permute-done | bytes 368672 | tf_op jit(solution)/shard_map/ppermute | solution.py:779
  152.8 1.7 input_back.1
  155.6 2.0 %collective-permute-start.48 = (bf16[64,768]{1,0:T(8,128)(2,1)S(1)}, bf16[64,768]{1,0:T(8,128)(2,1)S(1)}, u32[]{:S(2)}, u32[]{:S(2)}) collective-permute-start(bf16[64,768]{1,0:T(8,128)(2,1)S(1)} %get-tuple-element.222), channel_id=1, source_target_pairs={{0,8},{1,9},{2,10},{3,11},{4,12},{5,13},{6,14},{7,15},{8,0},{9,1},... | collective-permute-start | bytes 294920 | tf_op jit(solution)/shard_map/ppermute | solution.py:779
  159.3 7.3 %collective-permute-done.56 = bf16[48,1920]{1,0:T(8,128)(2,1)S(1)} collective-permute-done((bf16[48,1920]{1,0:T(8,128)(2,1)S(1)}, bf16[48,1920]{1,0:T(8,128)(2,1)S(1)}, u32[]{:S(2)}, u32[]{:S(2)}) %collective-permute-start.56) | collective-permute-done | bytes 184352 | tf_op jit(solution)/shard_map/ppermute | solution.py:779
  (225 shorter events, 80.9 us)
Async XLA Ops:
  1.8 15.8 %collective-permute-start.1 = (bf16[64,768]{1,0:T(8,128)(2,1)S(1)}, bf16[64,768]{1,0:T(8,128)(2,1)S(1)}, u32[]{:S(2)}, u32[]{:S(2)}) collective-permute-start(bf16[64,768]{1,0:T(8,128)(2,1)S(1)} %get-tuple-element.245.refs_4_.refs_5_.refs_0_), channel_id=1, source_target_pairs={{0,1},{1,0},{2,3},{3,2},{4,5},{5,4},{6,7},{7,6},{8,9},{9,8},{10,11... | collective-permute-start | bytes 294920 | tf_op jit(solution)/shard_map/ppermute | solution.py:779
  37.1 12.6 %collective-permute-start.18 = (bf16[64,768]{1,0:T(8,128)(2,1)S(1)}, bf16[64,768]{1,0:T(8,128)(2,1)S(1)}, u32[]{:S(2)}, u32[]{:S(2)}) collective-permute-start(bf16[64,768]{1,0:T(8,128)(2,1)S(1)} %get-tuple-element.242), channel_id=1, source_target_pairs={{0,4},{1,5},{2,6},{3,7},{4,0},{5,1},{6,2},{7,3},{8,12},{9,13},{10,... | collective-permute-start | bytes 294920 | tf_op jit(solution)/shard_map/ppermute | solution.py:779
  51.0 16.7 %collective-permute-start.28 = (bf16[256,768]{1,0:T(8,128)(2,1)S(1)}, bf16[256,768]{1,0:T(8,128)(2,1)S(1)}, u32[]{:S(2)}, u32[]{:S(2)}) collective-permute-start(bf16[256,768]{1,0:T(8,128)(2,1)S(1)} %get-tuple-element.159.second_ref), channel_id=1, source_target_pairs={{0,1},{1,0},{2,3},{3,2},{4,5},{5,4},{6,7},{7,6},{8,9},{9,8},{10,11... | collective-permute-start | bytes 1179656 | tf_op jit(solution)/shard_map/ppermute | solution.py:779
  51.4 16.2 %collective-permute-start.29 = (bf16[256,768]{1,0:T(8,128)(2,1)S(1)}, bf16[256,768]{1,0:T(8,128)(2,1)S(1)}, u32[]{:S(2)}, u32[]{:S(2)}) collective-permute-start(bf16[256,768]{1,0:T(8,128)(2,1)S(1)} %get-tuple-element.160.mixed_ref), channel_id=1, source_target_pairs={{0,1},{1,0},{2,3},{3,2},{4,5},{5,4},{6,7},{7,6},{8,9},{9,8},{10,11... | collective-permute-start | bytes 1179656 | tf_op jit(solution)/shard_map/ppermute | solution.py:779
  55.2 15.7 %collective-permute-start.26 = (bf16[2,2,2,96,384]{4,3,2,1,0:T(8,128)(2,1)S(1)}, bf16[2,2,2,96,384]{4,3,2,1,0:T(8,128)(2,1)S(1)}, u32[]{:S(2)}, u32[]{:S(2)}) collective-permute-start(bf16[2,2,2,96,384]{4,3,2,1,0:T(8,128)(2,1)S(1)} %get-tuple-element.157), channel_id=1, source_target_pairs={{0,16},{16,0},{1,17},{17,1},{2,18},{18,2},{3,19},{19,3},{4,20},{20... | collective-permute-start | bytes 1769480 | tf_op jit(solution)/shard_map/ppermute | solution.py:779
  56.8 15.3 %collective-permute-start.27 = (bf16[2,2,2,96,384]{4,3,2,1,0:T(8,128)(2,1)S(1)}, bf16[2,2,2,96,384]{4,3,2,1,0:T(8,128)(2,1)S(1)}, u32[]{:S(2)}, u32[]{:S(2)}) collective-permute-start(bf16[2,2,2,96,384]{4,3,2,1,0:T(8,128)(2,1)S(1)} %get-tuple-element.158), channel_id=1, source_target_pairs={{0,2},{1,3},{2,0},{3,1},{4,6},{5,7},{6,4},{7,5},{8,10},{9,11},{10,... | collective-permute-start | bytes 1769480 | tf_op jit(solution)/shard_map/ppermute | solution.py:779
  86.6 21.0 %collective-permute-start.34 = (bf16[2,96,384]{2,1,0:T(8,128)(2,1)S(1)}, bf16[2,96,384]{2,1,0:T(8,128)(2,1)S(1)}, u32[]{:S(2)}, u32[]{:S(2)}) collective-permute-start(bf16[2,96,384]{2,1,0:T(8,128)(2,1)S(1)} %get-tuple-element.198), channel_id=1, source_target_pairs={{0,4},{1,5},{2,6},{3,7},{4,0},{5,1},{6,2},{7,3},{8,12},{9,13},{10,... | collective-permute-start | bytes 442376 | tf_op jit(solution)/shard_map/ppermute | solution.py:779
  88.4 19.2 %collective-permute-start.35 = (bf16[2,96,384]{2,1,0:T(8,128)(2,1)S(1)}, bf16[2,96,384]{2,1,0:T(8,128)(2,1)S(1)}, u32[]{:S(2)}, u32[]{:S(2)}) collective-permute-start(bf16[2,96,384]{2,1,0:T(8,128)(2,1)S(1)} %get-tuple-element.199), channel_id=1, source_target_pairs={{0,4},{1,5},{2,6},{3,7},{4,0},{5,1},{6,2},{7,3},{8,12},{9,13},{10,... | collective-permute-start | bytes 442376 | tf_op jit(solution)/shard_map/ppermute | solution.py:779
  88.7 18.9 %collective-permute-start.36 = (bf16[2,2,2,48,1024]{4,3,2,1,0:T(8,128)(2,1)S(1)}, bf16[2,2,2,48,1024]{4,3,2,1,0:T(8,128)(2,1)S(1)}, u32[]{:S(2)}, u32[]{:S(2)}) collective-permute-start(bf16[2,2,2,48,1024]{4,3,2,1,0:T(8,128)(2,1)S(1)} %get-tuple-element.200), channel_id=1, source_target_pairs={{0,16},{16,0},{1,17},{17,1},{2,18},{18,2},{3,19},{19,3},{4,20},{20... | collective-permute-start | bytes 2359304 | tf_op jit(solution)/shard_map/ppermute | solution.py:779
  89.9 17.8 %collective-permute-start.37 = (bf16[2,2,2,48,896]{4,3,2,1,0:T(8,128)(2,1)S(1)}, bf16[2,2,2,48,896]{4,3,2,1,0:T(8,128)(2,1)S(1)}, u32[]{:S(2)}, u32[]{:S(2)}) collective-permute-start(bf16[2,2,2,48,896]{4,3,2,1,0:T(8,128)(2,1)S(1)} %get-tuple-element.201), channel_id=1, source_target_pairs={{0,2},{1,3},{2,0},{3,1},{4,6},{5,7},{6,4},{7,5},{8,10},{9,11},{10,... | collective-permute-start | bytes 2064392 | tf_op jit(solution)/shard_map/ppermute | solution.py:779
  93.1 14.5 %collective-permute-start.40 = (bf16[64,768]{1,0:T(8,128)(2,1)S(1)}, bf16[64,768]{1,0:T(8,128)(2,1)S(1)}, u32[]{:S(2)}, u32[]{:S(2)}) collective-permute-start(bf16[64,768]{1,0:T(8,128)(2,1)S(1)} %get-tuple-element.205), channel_id=1, source_target_pairs={{0,12},{1,13},{2,14},{3,15},{4,8},{5,9},{6,10},{7,11},{8,4},{9,5},... | collective-permute-start | bytes 294920 | tf_op jit(solution)/shard_map/ppermute | solution.py:779
  109.7 17.3 %collective-permute-start.41 = (bf16[9,48,576]{2,1,0:T(8,128)(2,1)}, bf16[9,48,576]{2,1,0:T(8,128)(2,1)}, u32[]{:S(2)}, u32[]{:S(2)}) collective-permute-start(bf16[9,48,576]{2,1,0:T(8,128)(2,1)} %concatenate.40), channel_id=1, source_target_pairs={{0,4},{1,5},{2,6},{3,7},{4,0},{5,1},{6,2},{7,3},{8,12},{9,13},{10,... | collective-permute-start | bytes 1493000 | tf_op jit(solution)/shard_map/ppermute | solution.py:779
  109.8 17.3 %collective-permute-start.42 = (bf16[2,256,768]{2,1,0:T(8,128)(2,1)}, bf16[2,256,768]{2,1,0:T(8,128)(2,1)}, u32[]{:S(2)}, u32[]{:S(2)}) collective-permute-start(bf16[2,256,768]{2,1,0:T(8,128)(2,1)} %get-tuple-element.213), channel_id=1, source_target_pairs={{0,1},{1,0},{2,3},{3,2},{4,5},{5,4},{6,7},{7,6},{8,9},{9,8},{10,11... | collective-permute-start | bytes 2359304 | tf_op jit(solution)/shard_map/ppermute | solution.py:779
  110.6 14.2 %collective-permute-start.43 = (bf16[2,2,48,1024]{3,2,1,0:T(8,128)(2,1)}, bf16[2,2,48,1024]{3,2,1,0:T(8,128)(2,1)}, u32[]{:S(2)}, u32[]{:S(2)}) collective-permute-start(bf16[2,2,48,1024]{3,2,1,0:T(8,128)(2,1)} %fusion), channel_id=1, source_target_pairs={{0,2},{1,3},{2,0},{3,1},{4,6},{5,7},{6,4},{7,5},{8,10},{9,11},{10,... | collective-permute-start | bytes 1179656 | tf_op jit(solution)/shard_map/ppermute | solution.py:779
  112.8 12.0 %collective-permute-start.44 = (bf16[2,2,48,896]{3,2,1,0:T(8,128)(2,1)}, bf16[2,2,48,896]{3,2,1,0:T(8,128)(2,1)}, u32[]{:S(2)}, u32[]{:S(2)}) collective-permute-start(bf16[2,2,48,896]{3,2,1,0:T(8,128)(2,1)} %fusion.1), channel_id=1, source_target_pairs={{0,16},{16,0},{1,17},{17,1},{2,18},{18,2},{3,19},{19,3},{4,20},{20... | collective-permute-start | bytes 1032200 | tf_op jit(solution)/shard_map/ppermute | solution.py:779
  130.2 22.5 %collective-permute-start.46 = (bf16[256,768]{1,0:T(8,128)(2,1)S(1)}, bf16[256,768]{1,0:T(8,128)(2,1)S(1)}, u32[]{:S(2)}, u32[]{:S(2)}) collective-permute-start(bf16[256,768]{1,0:T(8,128)(2,1)S(1)} %fusion.2), channel_id=1, source_target_pairs={{0,2},{1,3},{2,0},{3,1},{4,6},{5,7},{6,4},{7,5},{8,10},{9,11},{10,... | collective-permute-start | bytes 1179656 | tf_op jit(solution)/shard_map/ppermute | solution.py:779
  131.3 14.0 %collective-permute-start.50 = (bf16[5,48,576]{2,1,0:T(8,128)(2,1)S(1)}, bf16[5,48,576]{2,1,0:T(8,128)(2,1)S(1)}, u32[]{:S(2)}, u32[]{:S(2)}) collective-permute-start(bf16[5,48,576]{2,1,0:T(8,128)(2,1)S(1)} %pad_maximum_fusion.2), channel_id=1, source_target_pairs={{0,8},{1,9},{2,10},{3,11},{4,12},{5,13},{6,14},{7,15},{8,0},{9,1},... | collective-permute-start | bytes 829448 | tf_op jit(solution)/shard_map/ppermute | solution.py:779
  136.5 14.1 %collective-permute-start.55 = (bf16[2,48,1920]{2,1,0:T(8,128)(2,1)S(1)}, bf16[2,48,1920]{2,1,0:T(8,128)(2,1)S(1)}, u32[]{:S(2)}, u32[]{:S(2)}) collective-permute-start(bf16[2,48,1920]{2,1,0:T(8,128)(2,1)S(1)} %pad_maximum_fusion.1), channel_id=1, source_target_pairs={{0,4},{1,5},{2,6},{3,7},{4,0},{5,1},{6,2},{7,3},{8,12},{9,13},{10,... | collective-permute-start | bytes 1105928 | tf_op jit(solution)/shard_map/ppermute | solution.py:779
  146.5 12.4 %collective-permute-start.51 = (bf16[5,48,576]{2,1,0:T(8,128)(2,1)S(1)}, bf16[5,48,576]{2,1,0:T(8,128)(2,1)S(1)}, u32[]{:S(2)}, u32[]{:S(2)}) collective-permute-start(bf16[5,48,576]{2,1,0:T(8,128)(2,1)S(1)} %pad_maximum_fusion.3), channel_id=1, source_target_pairs={{0,16},{16,0},{1,17},{17,1},{2,18},{18,2},{3,19},{19,3},{4,20},{20... | collective-permute-start | bytes 829448 | tf_op jit(solution)/shard_map/ppermute | solution.py:779
  152.6 14.0 %collective-permute-start.56 = (bf16[48,1920]{1,0:T(8,128)(2,1)S(1)}, bf16[48,1920]{1,0:T(8,128)(2,1)S(1)}, u32[]{:S(2)}, u32[]{:S(2)}) collective-permute-start(bf16[48,1920]{1,0:T(8,128)(2,1)S(1)} %pad_maximum_fusion.4), channel_id=1, source_target_pairs={{0,8},{1,9},{2,10},{3,11},{4,12},{5,13},{6,14},{7,15},{8,0},{9,1},... | collective-permute-start | bytes 552968 | tf_op jit(solution)/shard_map/ppermute | solution.py:779
  154.5 15.7 %collective-permute-start.47 = (bf16[64,768]{1,0:T(8,128)(2,1)S(1)}, bf16[64,768]{1,0:T(8,128)(2,1)S(1)}, u32[]{:S(2)}, u32[]{:S(2)}) collective-permute-start(bf16[64,768]{1,0:T(8,128)(2,1)S(1)} %get-tuple-element.221), channel_id=1, source_target_pairs={{0,4},{1,5},{2,6},{3,7},{4,0},{5,1},{6,2},{7,3},{8,12},{9,13},{10,... | collective-permute-start | bytes 294920 | tf_op jit(solution)/shard_map/ppermute | solution.py:779
  155.6 14.7 %collective-permute-start.48 = (bf16[64,768]{1,0:T(8,128)(2,1)S(1)}, bf16[64,768]{1,0:T(8,128)(2,1)S(1)}, u32[]{:S(2)}, u32[]{:S(2)}) collective-permute-start(bf16[64,768]{1,0:T(8,128)(2,1)S(1)} %get-tuple-element.222), channel_id=1, source_target_pairs={{0,8},{1,9},{2,10},{3,11},{4,12},{5,13},{6,14},{7,15},{8,0},{9,1},... | collective-permute-start | bytes 294920 | tf_op jit(solution)/shard_map/ppermute | solution.py:779
  157.6 14.4 %collective-permute-start.49 = (bf16[64,768]{1,0:T(8,128)(2,1)S(1)}, bf16[64,768]{1,0:T(8,128)(2,1)S(1)}, u32[]{:S(2)}, u32[]{:S(2)}) collective-permute-start(bf16[64,768]{1,0:T(8,128)(2,1)S(1)} %get-tuple-element.223), channel_id=1, source_target_pairs={{0,12},{1,13},{2,14},{3,15},{4,8},{5,9},{6,10},{7,11},{8,4},{9,5},... | collective-permute-start | bytes 294920 | tf_op jit(solution)/shard_map/ppermute | solution.py:779
  159.2 14.1 %collective-permute-start.52 = (bf16[2,48,576]{2,1,0:T(8,128)(2,1)S(1)}, bf16[2,48,576]{2,1,0:T(8,128)(2,1)S(1)}, u32[]{:S(2)}, u32[]{:S(2)}) collective-permute-start(bf16[2,48,576]{2,1,0:T(8,128)(2,1)S(1)} %get-tuple-element.257), channel_id=1, source_target_pairs={{0,1},{1,0},{2,3},{3,2},{4,5},{5,4},{6,7},{7,6},{8,9},{9,8},{10,11... | collective-permute-start | bytes 331784 | tf_op jit(solution)/shard_map/ppermute | solution.py:779
  (71 other events, 756.7 us)
